TPU v7x, 128 devices: a whole 4x4x4 slice. The times are simulated.
128 devices in a mesh: dp: 4 (over y), ctx: 8 (over z, x_hi), tensor: 4 (over x_lo, core).
Axes of the slice: x: 4 (x_hi: 2, x_lo: 2; x = x_hi * 2 + x_lo), y: 4, z: 4, core: 2. Of those that a mesh axis runs over, the one named last changes fastest.
Arguments:
- tokens: bfloat16 [4096, 4096], P(('dp', 'ctx')), may hold values from -6 to 6
- out_grad: bfloat16 [4096, 4096], P(('dp', 'ctx')), may hold values from -6 to 6
- expert_ids: int32 [4096, 8], P(('dp', 'ctx')), may hold values from 0 to 31, as said below
- gate_probs: float32 [4096, 8], P(('dp', 'ctx')), may hold values from 0.1 to 0.5
- w_gate: bfloat16 [32, 768, 4096], P(('ctx', 'tensor')), may hold values from -0.09375 to 0.09375
- w_up: bfloat16 [32, 768, 4096], P(('ctx', 'tensor')), may hold values from -0.09375 to 0.09375
- w_down: bfloat16 [32, 768, 4096], P(('ctx', 'tensor')), may hold values from -0.21875 to 0.21875
Outputs:
- in_grad: bfloat16 [4096, 4096], P(('dp', 'ctx', 'tensor'))
- grad_gate: bfloat16 [32, 768, 4096], P(('ctx', 'tensor'), 'dp')
- grad_up: bfloat16 [32, 768, 4096], P(('ctx', 'tensor'), 'dp')
- grad_down: bfloat16 [32, 768, 4096], P(('ctx', 'tensor'), 'dp')
Inputs may be any that keep to these rules, and one draw needn't show every extreme that they name: `expert_ids`: each token names 8 different experts. Cut a token's slots into 4 runs of 2 consecutive slots; over the 128 tokens of one index pair of dp and ctx, one run names one expert at most 16 times, and in some run of every such block some expert exactly 16 times.
All inputs are finite; a program needn't handle non-finite values.
Results may differ from a plain program's by a relative error of at most 0.023.
Values may be sent and summed in bfloat16 or wider, within the bound.
No kernel may reach another device: no remote copies, remote signals or barrier semaphores. Data moves between devices by JAX's collectives and lax.ppermute only.
A program may use at most 192 MiB of HBM per device.

v0:
```python
import jax
import jax.numpy as jnp
from jax import lax
from jax.experimental import pallas as pl
from jax.experimental.pallas import tpu as pltpu
from jax.sharding import Mesh
from jax.sharding import PartitionSpec as P

BF16 = jnp.bfloat16
F32 = jnp.float32
VMEM_LIMIT = 56 * 1024 * 1024
PLANE = ("z", "xh", "xl", "core")
LANES = 128


def hidden_kernel(expert_ref, gathered_ref, gate_ref, up_ref, down_ref, out_ref, held, prob_ref, sems):
    unit, tile = pl.program_id(0), pl.program_id(1)
    rows = out_ref.shape[2]
    width = gate_ref.shape[1]

    def copy(index):
        span = pl.ds(pl.multiple_of(index * rows, rows), rows)
        return pltpu.make_async_copy(gathered_ref.at[span], held.at[span], sems.at[index])

    @pl.when((unit == 0) & (tile == 0))
    def _():
        for index in range(held.shape[0] // rows):
            copy(index).start()

    span = pl.ds(pl.multiple_of(tile * rows, rows), rows)

    @pl.when(unit == 0)
    def _():
        copy(tile).wait()
        lane = lax.broadcasted_iota(jnp.int32, (8, LANES), 1)
        expert = expert_ref[0]
        chosen = ((lane == expert) | (lane == expert + LANES // 2)).astype(F32).astype(BF16)
        prob_ref[:, span] = lax.dot_general(
            chosen, held[span, 2 * width :], (((1,), (1,)), ((), ())), preferred_element_type=F32
        )

    tokens = held[span, :width]
    grads = held[span, width : 2 * width]
    by_features = (((1,), (1,)), ((), ()))
    gate_pre = lax.dot_general(gate_ref[...], tokens, by_features, preferred_element_type=F32)
    up_pre = lax.dot_general(up_ref[...], tokens, by_features, preferred_element_type=F32)
    down_pre = lax.dot_general(down_ref[...], grads, by_features, preferred_element_type=F32)
    prob = prob_ref[0:1, span]
    sigmoid = jax.nn.sigmoid(gate_pre)
    active = gate_pre * sigmoid
    slope = sigmoid * (1.0 + gate_pre * (1.0 - sigmoid))
    hidden_grad = prob * down_pre
    out_ref[0] = (hidden_grad * up_pre * slope).astype(BF16)
    out_ref[1] = (hidden_grad * active).astype(BF16)
    out_ref[2] = (prob * active * up_pre).astype(BF16)


def hidden_rows(gathered, expert, w_gate, w_up, w_down):
    token_count = gathered.shape[0]
    units, width = w_gate.shape
    step, rows = 256, 256
    weight = pl.BlockSpec((step, width), lambda u, t, e: (u, 0))
    return pl.pallas_call(
        hidden_kernel,
        grid_spec=pltpu.PrefetchScalarGridSpec(
            num_scalar_prefetch=1,
            grid=(units // step, token_count // rows),
            in_specs=[pl.BlockSpec(memory_space=pl.ANY), weight, weight, weight],
            out_specs=pl.BlockSpec((3, step, rows), lambda u, t, e: (0, u, t)),
            scratch_shapes=[
                pltpu.VMEM(gathered.shape, BF16),
                pltpu.VMEM((8, token_count), F32),
                pltpu.SemaphoreType.DMA((token_count // rows,)),
            ],
        ),
        out_shape=jax.ShapeDtypeStruct((3, units, token_count), BF16),
        compiler_params=pltpu.CompilerParams(vmem_limit_bytes=VMEM_LIMIT),
        cost_estimate=pl.CostEstimate(
            flops=6 * token_count * units * width,
            bytes_accessed=2 * gathered.size + 6 * w_gate.size + 6 * token_count * units,
            transcendentals=token_count * units,
        ),
        name="hidden_rows",
    )(expert, gathered, w_gate, w_up, w_down)


def input_kernel(hidden_ref, gate_ref, up_ref, out_ref, turned):
    @pl.when(pl.program_id(0) == 0)
    def _():
        turned[0] = hidden_ref[0].T
        turned[1] = hidden_ref[1].T

    total = jnp.dot(turned[0], gate_ref[...], preferred_element_type=F32)
    total += jnp.dot(turned[1], up_ref[...], preferred_element_type=F32)
    total = total.astype(BF16).reshape(out_ref.shape[1], 2, out_ref.shape[2], out_ref.shape[3])
    out_ref[0] = total[:, 0]
    out_ref[1] = total[:, 1]


def input_rows(hidden, w_gate, w_up, share):
    _, units, token_count = hidden.shape
    width = w_gate.shape[1]
    step = 512
    groups = token_count // (2 * share)
    weight = pl.BlockSpec((units, step), lambda i: (0, i))
    return pl.pallas_call(
        input_kernel,
        grid=(width // step,),
        in_specs=[
            pl.BlockSpec((2, units, token_count), lambda i: (0, 0, 0)),
            weight,
            weight,
        ],
        out_specs=pl.BlockSpec((2, groups, share, step), lambda i: (0, 0, 0, i)),
        out_shape=jax.ShapeDtypeStruct((2, groups, share, width), BF16),
        scratch_shapes=[pltpu.VMEM((2, token_count, units), BF16)],
        compiler_params=pltpu.CompilerParams(vmem_limit_bytes=VMEM_LIMIT),
        cost_estimate=pl.CostEstimate(
            flops=4 * token_count * units * width,
            bytes_accessed=4 * w_gate.size + 2 * token_count * width,
            transcendentals=0,
        ),
        name="input_rows",
    )(hidden, w_gate, w_up)


def weight_kernel(hidden_ref, gathered_ref, out_ref):
    out_ref[0, 0] = jnp.dot(hidden_ref[0], gathered_ref[...], preferred_element_type=F32).astype(BF16)


def weight_grads(hidden, gathered, width, owners):
    _, units, token_count = hidden.shape
    share = units // owners
    return pl.pallas_call(
        weight_kernel,
        grid=(2, owners * 3),
        in_specs=[
            pl.BlockSpec((1, share, token_count), lambda h, i: (i % 3, i // 3, 0)),
            pl.BlockSpec((token_count, width // 2), lambda h, i: (0, h + 2 * ((i % 3) // 2))),
        ],
        out_specs=pl.BlockSpec((1, 1, share, width // 2), lambda h, i: (i // 3, i % 3, 0, h)),
        out_shape=jax.ShapeDtypeStruct((owners, 3, share, width), BF16),
        compiler_params=pltpu.CompilerParams(vmem_limit_bytes=VMEM_LIMIT),
        cost_estimate=pl.CostEstimate(
            flops=6 * token_count * units * width,
            bytes_accessed=4 * token_count * width + 6 * units * width,
            transcendentals=0,
        ),
        name="weight_grads",
    )(hidden, gathered)


def per_device(tokens, out_grad, expert_ids, gate_probs, w_gate, w_up, w_down):
    token_count, width = tokens.shape
    owners = lax.axis_size("dp")
    ranks = lax.axis_size(("xl", "core"))
    experts = lax.axis_size(PLANE)
    share = token_count // ranks
    rank = lax.axis_index(("xl", "core"))
    core = lax.axis_index("core")
    expert = lax.axis_index(PLANE)

    def own_share(array):
        return lax.dynamic_slice_in_dim(array, rank * share, share, 0)

    hits = own_share(expert_ids)[:, :, None] == jnp.arange(experts, dtype=jnp.int32)
    table = jnp.sum(jnp.where(hits, own_share(gate_probs)[:, :, None], 0.0), axis=1)
    coarse = table.astype(BF16)
    fine = (table - coarse.astype(F32)).astype(BF16)
    pad = jnp.zeros((share, LANES // 2 - experts), BF16)
    payload = jnp.concatenate(
        [own_share(tokens), own_share(out_grad), coarse, pad, fine, pad], axis=1
    )
    gathered = lax.all_gather(payload, PLANE, axis=0, tiled=True)
    hidden = hidden_rows(gathered, expert[None], w_gate[0], w_up[0], w_down[0])
    grads = weight_grads(hidden, gathered, width, owners)
    summed = lax.psum_scatter(
        grads.reshape(owners * 3, -1, width), "dp", scatter_dimension=0, tiled=True
    )
    hidden, grads = lax.optimization_barrier((hidden, grads))
    rows = input_rows(hidden, w_gate[0], w_up[0], share)
    kept = lax.dynamic_index_in_dim(rows, core, 0, keepdims=False)
    given = lax.dynamic_index_in_dim(rows, 1 - core, 0, keepdims=False)
    taken = lax.ppermute(given, "core", [(0, 1), (1, 0)])
    paired = (kept.astype(F32) + taken.astype(F32)).astype(BF16)
    returned = lax.all_to_all(paired, PLANE[:3], split_axis=0, concat_axis=0, tiled=True)
    in_grad = jnp.sum(returned.astype(F32), axis=0).astype(BF16)
    return (in_grad, summed[0:1], summed[1:2], summed[2:3])


def solution(mesh):
    dp, ctx, tensor = (mesh.shape[name] for name in ("dp", "ctx", "tensor"))
    fine = Mesh(
        mesh.devices.reshape(dp, ctx // 2, 2, tensor // 2, 2), ("dp", "z", "xh", "xl", "core")
    )
    token_spec = P(("dp", "z", "xh"), None)
    weight_spec = P(PLANE, None, None)
    grad_spec = P(PLANE, "dp", None)
    return jax.shard_map(
        per_device,
        mesh=fine,
        in_specs=(token_spec,) * 4 + (weight_spec,) * 3,
        out_specs=(P(("dp",) + PLANE, None), grad_spec, grad_spec, grad_spec),
        check_vma=False,
    )
```

profile of v0, /device:TPU:2, one launch (start us, length us, event | category | flops | bytes accessed | tf_op | source)
XLA Modules:
  0.0 504.8 jit_solution(10855987188940313639)
XLA Ops:
  7.2 0.0 copy-start
  7.2 0.0 all-gather.2.cloned.1.call-start
  7.2 0.6 copy-done
  7.9 0.1 constant_dynamic-slice_fusion.1
  7.9 0.1 copy.15
  8.0 0.8 constant_dynamic-slice_fusion
  8.8 0.1 copy.16
  8.8 0.1 select_reduce_fusion
  9.0 1.1 constant_dynamic-slice_fusion.2
  10.1 0.9 concatenate.3
  11.0 0.0 all-gather.2.cloned.1.call-update
  11.1 0.0 all-reduce.3.cloned.1.call-start
  11.1 75.7 %all-gather.2.cloned.1.call-done.gathered_ref = bf16[1024,8320]{1,0:T(8,128)(2,1)} async-done(((bf16[32,8320]{1,0:T(8,128)(2,1)}), bf16[1024,8320]{1,0:T(8,128)(2,1)}) %all-gather.2.cloned.1.call-update) | async-done | bytes 17039376 | tf_op jit(solution)/shard_map/all_gather | solution.py:174
  86.8 31.6 %hidden_rows.1.hidden_ref = bf16[3,768,1024]{2,1,0:T(8,128)(2,1)} custom-call(s32[1]{0:T(128)} %bitcast.expert_ref, bf16[1024,8320]{1,0:T(8,128)(2,1)} %all-gather.2.cloned.1.call-done.gathered_ref, bf16[768,4096]{1,0:T(8,128)(2,1)} %bitcast.13, bf16[768,4096]{1,0:T(8,128)(2,1)} %bitcast.15, bf16[768,4096]{1,0:T(8,128)(2,1)} %bitcast.12), custom_call_target="tpu_custom_call" | custom-call | flops 19327352832 | bytes 40632320 | tf_op jit(solution)/shard_map/hidden_rows/pallas_call | solution.py:63
  118.5 46.2 %weight_grads.1 = bf16[4,3,192,4096]{3,2,1,0:T(8,128)(2,1)} custom-call(bf16[3,768,1024]{2,1,0:T(8,128)(2,1)} %hidden_rows.1.hidden_ref, bf16[1024,8320]{1,0:T(8,128)(2,1)} %all-gather.2.cloned.1.call-done.gathered_ref), custom_call_target="tpu_custom_call" | custom-call | flops 19327352832 | bytes 35651584 | tf_op jit(solution)/shard_map/weight_grads/pallas_call | solution.py:134
  164.6 0.0 all-reduce.3.cloned.1.call-update
  164.6 19.1 %input_rows.1 = bf16[2,16,32,4096]{3,2,1,0:T(8,128)(2,1)} custom-call(bf16[3,768,1024]{2,1,0:T(8,128)(2,1)} %hidden_rows.1.hidden_ref, bf16[768,4096]{1,0:T(8,128)(2,1)} %bitcast.14, bf16[768,4096]{1,0:T(8,128)(2,1)} %bitcast.16), custom_call_target="tpu_custom_call" | custom-call | flops 12884901888 | bytes 20971520 | tf_op jit(solution)/shard_map/input_rows/pallas_call | solution.py:106
  183.7 4.8 dynamic-slice_bitcast_fusion
  188.5 0.3 collective-permute-start
  188.8 7.2 %collective-permute-done = bf16[16,32,4096]{2,1,0:T(8,128)(2,1)} collective-permute-done((bf16[16,32,4096]{2,1,0:T(8,128)(2,1)}, bf16[16,32,4096]{2,1,0:T(8,128)(2,1)}, u32[]{:S(2)}, u32[]{:S(2)}) %collective-permute-start) | collective-permute-done | bytes 4194336 | tf_op jit(solution)/shard_map/ppermute | solution.py:184
  196.0 7.4 %fusion = bf16[16,32,4096]{2,1,0:T(8,128)(2,1)} fusion(bf16[16,32,4096]{2,1,0:T(8,128)(2,1)} %collective-permute-done, bf16[2,16,32,4096]{3,2,1,0:T(8,128)(2,1)} %input_rows.1, s32[]{:T(128)S(6)} %select_n.19), kind=kLoop, calls=%fused_computation.1 | loop fusion | flops 8388608 | bytes 12582916 | tf_op jit(solution)/shard_map/convert_element_type | solution.py:185
  203.4 0.0 copy-start.2
  203.4 5.6 %all-to-all-start = ((bf16[16,32,4096]{2,1,0:T(8,128)(2,1)}), bf16[16,32,4096]{2,1,0:T(8,128)(2,1)}, u32[]{:S(2)}, u32[]{:S(2)}) async-start(bf16[16,32,4096]{2,1,0:T(8,128)(2,1)} %fusion), calls=%async_computation | async-start | bytes 8388608 | tf_op jit(solution)/shard_map/all_to_all | solution.py:186
  208.9 0.0 copy-done.2
  208.9 0.6 dynamic-slice
  210.2 58.6 %all-to-all-done = bf16[16,32,4096]{2,1,0:T(8,128)(2,1)} async-done(((bf16[16,32,4096]{2,1,0:T(8,128)(2,1)}), bf16[16,32,4096]{2,1,0:T(8,128)(2,1)}, u32[]{:S(2)}, u32[]{:S(2)}) %all-to-all-start) | async-done | bytes 4194336 | tf_op jit(solution)/shard_map/all_to_all | solution.py:186
  268.8 0.0 copy-start.1
  268.8 4.1 reduce_sum.22
  272.9 220.4 %all-reduce.3.cloned.1.call-done = bf16[12,192,4096]{2,1,0:T(8,128)(2,1)} async-done(((bf16[12,192,4096]{2,1,0:T(8,128)(2,1)}), bf16[12,192,4096]{2,1,0:T(8,128)(2,1)}) %all-reduce.3.cloned.1.call-update) | async-done | bytes 18874384
  493.3 4.7 constant_dynamic-slice_fusion.6
  498.0 0.0 copy-done.1
  (2 shorter events, 0.0 us)
Async XLA Ops:
  7.2 0.7 copy-start
  7.2 79.6 %all-gather.2.cloned.1.call-start = ((), (), s32[]{:S(2)}) async-start(), calls=%async_computation.1 | async-start | bytes 17571840 | tf_op jit(solution)/shard_map/all_gather | solution.py:174
  11.1 482.2 %all-reduce.3.cloned.1.call-start = ((), (), s32[]{:S(2)}) async-start(), calls=%async_computation.2 | async-start | bytes 37748736
  188.5 7.5 %collective-permute-start = (bf16[16,32,4096]{2,1,0:T(8,128)(2,1)}, bf16[16,32,4096]{2,1,0:T(8,128)(2,1)}, u32[]{:S(2)}, u32[]{:S(2)}) collective-permute-start(bf16[16,32,4096]{2,1,0:T(8,128)(2,1)} %dynamic-slice_bitcast_fusion), channel_id=1, source_target_pairs={{0,1},{1,0},{2,3},{3,2},{4,5},{5,4},{6,7},{7,6},{8,9},{9,8},{10,11... | collective-permute-start | bytes 12582920 | tf_op jit(solution)/shard_map/ppermute | solution.py:184
  203.4 5.6 %copy-start.2 = (u32[128]{0:T(128)S(1)}, u32[128]{0:T(128)}, u32[]{:S(2)}) copy-start(u32[128]{0:T(128)} %constant.46) | copy-start | bytes 1540
  203.4 65.5 %all-to-all-start = ((bf16[16,32,4096]{2,1,0:T(8,128)(2,1)}), bf16[16,32,4096]{2,1,0:T(8,128)(2,1)}, u32[]{:S(2)}, u32[]{:S(2)}) async-start(bf16[16,32,4096]{2,1,0:T(8,128)(2,1)} %fusion), calls=%async_computation | async-start | bytes 8388608 | tf_op jit(solution)/shard_map/all_to_all | solution.py:186
  268.8 229.2 %copy-start.1 = (s32[128,8]{0,1:T(8,128)S(1)}, s32[128,8]{0,1:T(8,128)}, u32[]{:S(2)}) copy-start(s32[128,8]{0,1:T(8,128)} %param.9) | copy-start | bytes 12292
Sparse Core Ops, SparseCore 0:
  11.2 75.5 all-gather.1
  164.8 328.4 all-reduce.2
where the time goes:
time: 506 us; the launch traced here: 505 us
  waiting for transfers between devices  362 us (72%)
  Pallas kernels  96.9 us (19%)
  between operations  14.8 us (3%)
  local copies, waits for them, and re-layouts  13.7 us (3%)
  other arithmetic  11.6 us (2%)
  starting transfers between devices  5.96 us (1%)
    unnamed x3, waiting for transfers between devices  220 us
    all_gather x1, waiting for transfers between devices, per_device(): gathered = lax.all_gather(payload, PLANE, axis=0, tiled=True)  75.7 us
    all_to_all x1, waiting for transfers between devices, per_device(): lax.all_to_all(paired, PLANE[:3], split_axis=0, concat_axis=0, tiled=True)  58.6 us
    pallas_call x1, Pallas kernels, weight_grads(): pl.pallas_call(weight_kernel, grid=(2, owners * 3), in_specs=[pl.BlockSpe...  46.2 us
    pallas_call x1, Pallas kernels, hidden_rows(): pl.pallas_call(hidden_kernel, grid_spec=pltpu.PrefetchScalarGridSpec(num_...  31.6 us
    pallas_call x1, Pallas kernels, input_rows(): pl.pallas_call(input_kernel, grid=(width // step,), in_specs=[pl.BlockSpe...  19.1 us
  transfers between devices with their start and end apart: 4, of which 4 were waited for; matrix products, arithmetic and copies ran while one was open for 3% of the time, Pallas kernels for 4%

commit v1 on v0

v1 whole, which is shorter than its diff:
```python
import jax
import jax.numpy as jnp
from jax import lax
from jax.experimental import pallas as pl
from jax.experimental.pallas import tpu as pltpu
from jax.sharding import Mesh
from jax.sharding import PartitionSpec as P

BF16 = jnp.bfloat16
F32 = jnp.float32
VMEM_LIMIT = 56 * 1024 * 1024
PLANE = ("z", "xh", "xl", "core")
LANES = 128


def hidden_kernel(
    route_ref, gathered_ref, gate_ref, up_ref, down_ref, out_ref, near_ref, far_ref,
    held, gate, up, down, token_sems, weight_sems,
):
    tile = pl.program_id(0)
    rows = out_ref.shape[3]
    share, width = gate_ref.shape[1], gate_ref.shape[2]
    weights = ((gate_ref, gate), (up_ref, up), (down_ref, down))

    def token_copy(index):
        span = pl.ds(pl.multiple_of(index * rows, rows), rows)
        return pltpu.make_async_copy(gathered_ref.at[span], held.at[index % 2], token_sems.at[index % 2])

    def weight_copy(which, place):
        source, target = weights[which]
        return pltpu.make_async_copy(
            source.at[route_ref[place]],
            target.at[pl.ds(place * share, share)],
            weight_sems.at[which, place],
        )

    @pl.when(tile == 0)
    def _():
        token_copy(0).start()
        for half in range(2):
            for which in range(3):
                for place in (2 * half, 2 * half + 1):
                    weight_copy(which, place).start()

    token_copy(tile).wait()

    @pl.when(tile + 1 < pl.num_programs(0))
    def _():
        token_copy(tile + 1).start()

    slot = tile % 2
    tokens = held[slot, :, :width]
    grads = held[slot, :, width : 2 * width]
    lane = lax.broadcasted_iota(jnp.int32, (8, LANES), 1)
    expert = route_ref[4]
    chosen = ((lane == expert) | (lane == expert + LANES // 2)).astype(F32).astype(BF16)
    by_features = (((1,), (1,)), ((), ()))
    prob = lax.dot_general(
        chosen, held[slot, :, 2 * width :], by_features, preferred_element_type=F32
    )[0:1]
    for half in range(2):
        span = pl.ds(2 * half * share, 2 * share)

        def product(which, array, right):
            @pl.when(tile == 0)
            def _():
                weight_copy(which, 2 * half).wait()
                weight_copy(which, 2 * half + 1).wait()

            return lax.dot_general(array[span], right, by_features, preferred_element_type=F32)

        gate_pre = product(0, gate, tokens)
        up_pre = product(1, up, tokens)
        hidden_grad = prob * product(2, down, grads)
        sigmoid = jax.nn.sigmoid(gate_pre)
        active = gate_pre * sigmoid
        slope = sigmoid * (1.0 + gate_pre * (1.0 - sigmoid))
        results = (hidden_grad * up_pre * slope, hidden_grad * active, prob * active * up_pre)
        for which, result in enumerate(results):
            result = result.astype(BF16).reshape(2, share, rows)
            out_ref[which, route_ref[2 * half]] = result[0]
            out_ref[which, route_ref[2 * half + 1]] = result[1]
            if half == 0:
                near_ref[which] = result
                far_ref[which, 0] = result[1]
            else:
                far_ref[which, 1] = result[0]


def hidden_rows(gathered, route, w_gate, w_up, w_down):
    token_count = gathered.shape[0]
    owners, share, width = w_gate.shape
    rows = 256
    whole = pl.BlockSpec(memory_space=pl.ANY)
    kept = pltpu.VMEM((owners * share, width), BF16)
    pair = pl.BlockSpec((3, 2, share, rows), lambda t, r: (0, 0, 0, t))
    return pl.pallas_call(
        hidden_kernel,
        grid_spec=pltpu.PrefetchScalarGridSpec(
            num_scalar_prefetch=1,
            grid=(token_count // rows,),
            in_specs=[whole, whole, whole, whole],
            out_specs=[pl.BlockSpec((3, owners, share, rows), lambda t, r: (0, 0, 0, t)), pair, pair],
            scratch_shapes=[
                pltpu.VMEM((2, rows, gathered.shape[1]), BF16),
                kept,
                kept,
                kept,
                pltpu.SemaphoreType.DMA((2,)),
                pltpu.SemaphoreType.DMA((3, owners)),
            ],
        ),
        out_shape=[
            jax.ShapeDtypeStruct((3, owners, share, token_count), BF16),
            jax.ShapeDtypeStruct((3, 2, share, token_count), BF16),
            jax.ShapeDtypeStruct((3, 2, share, token_count), BF16),
        ],
        compiler_params=pltpu.CompilerParams(vmem_limit_bytes=VMEM_LIMIT),
        cost_estimate=pl.CostEstimate(
            flops=6 * token_count * w_gate.size,
            bytes_accessed=2 * gathered.size + 6 * w_gate.size,
            transcendentals=token_count * owners * share,
        ),
        name="hidden_rows",
    )(route, gathered, w_gate, w_up, w_down)


def input_kernel(hidden_ref, gate_ref, up_ref, out_ref, turned):
    @pl.when(pl.program_id(0) == 0)
    def _():
        turned[0] = hidden_ref[0].T
        turned[1] = hidden_ref[1].T

    total = jnp.dot(turned[0], gate_ref[...], preferred_element_type=F32)
    total += jnp.dot(turned[1], up_ref[...], preferred_element_type=F32)
    total = total.astype(BF16).reshape(out_ref.shape[1], 2, out_ref.shape[2], out_ref.shape[3])
    out_ref[0] = total[:, 0]
    out_ref[1] = total[:, 1]


def input_rows(hidden, w_gate, w_up, share):
    _, units, token_count = hidden.shape
    width = w_gate.shape[1]
    step = 512
    groups = token_count // (2 * share)
    weight = pl.BlockSpec((units, step), lambda i: (0, i))
    return pl.pallas_call(
        input_kernel,
        grid=(width // step,),
        in_specs=[
            pl.BlockSpec((2, units, token_count), lambda i: (0, 0, 0)),
            weight,
            weight,
        ],
        out_specs=pl.BlockSpec((2, groups, share, step), lambda i: (0, 0, 0, i)),
        out_shape=jax.ShapeDtypeStruct((2, groups, share, width), BF16),
        scratch_shapes=[pltpu.VMEM((2, token_count, units), BF16)],
        compiler_params=pltpu.CompilerParams(vmem_limit_bytes=VMEM_LIMIT),
        cost_estimate=pl.CostEstimate(
            flops=4 * token_count * units * width,
            bytes_accessed=4 * w_gate.size + 2 * token_count * width,
            transcendentals=0,
        ),
        name="input_rows",
    )(hidden, w_gate, w_up)


def weight_kernel(
    pick_ref, first_ref, second_ref, other_ref, own_ref, near_ref, out_first, out_second, left
):
    share = first_ref.shape[2]

    @pl.when(pl.program_id(0) == 0)
    def _():
        left[0, :share] = first_ref[0, 0]
        left[0, share:] = second_ref[0, 0]
        left[1, :share] = other_ref[0, 0]
        left[1, share:] = other_ref[0, 1]

    total = jnp.dot(left[0], own_ref[...], preferred_element_type=F32)
    total += jnp.dot(left[1], near_ref[...], preferred_element_type=F32)
    out_first[...] = total[:share].astype(BF16)
    out_second[...] = total[share:].astype(BF16)


def weight_grads(which, half, picks, hidden, other, gathered, gathered_near):
    _, _, share, token_count = hidden.shape
    width = gathered_near.shape[1] // 2
    columns = width // 2
    step = 512
    count = columns // step
    own_base = ((which // 2) * 2 + half) * count
    near_base = (half * 2 + which // 2) * count
    out = pl.BlockSpec((share, step), lambda i, p: (0, i))
    shape = jax.ShapeDtypeStruct((share, columns), BF16)
    return pl.pallas_call(
        weight_kernel,
        grid_spec=pltpu.PrefetchScalarGridSpec(
            num_scalar_prefetch=1,
            grid=(count,),
            in_specs=[
                pl.BlockSpec((1, 1, share, token_count), lambda i, p: (which, p[0], 0, 0)),
                pl.BlockSpec((1, 1, share, token_count), lambda i, p: (which, p[1], 0, 0)),
                pl.BlockSpec((1, 2, share, token_count), lambda i, p: (which, 0, 0, 0)),
                pl.BlockSpec((token_count, step), lambda i, p: (0, own_base + i)),
                pl.BlockSpec((token_count, step), lambda i, p: (0, near_base + i)),
            ],
            out_specs=[out, out],
            scratch_shapes=[pltpu.VMEM((2, 2 * share, token_count), BF16)],
        ),
        out_shape=[shape, shape],
        compiler_params=pltpu.CompilerParams(vmem_limit_bytes=VMEM_LIMIT),
        cost_estimate=pl.CostEstimate(
            flops=8 * share * token_count * columns,
            bytes_accessed=4 * token_count * columns + 12 * share * token_count,
            transcendentals=0,
        ),
        name="weight_grads",
    )(picks, hidden, hidden, other, gathered, gathered_near)


def per_device(tokens, out_grad, expert_ids, gate_probs, w_gate, w_up, w_down):
    token_count, width = tokens.shape
    half = width // 2
    owners = lax.axis_size("dp")
    ranks = lax.axis_size(("xl", "core"))
    experts = lax.axis_size(PLANE)
    units = w_gate.shape[1]
    share = token_count // ranks
    rank = lax.axis_index(("xl", "core"))
    core = lax.axis_index("core")
    expert = lax.axis_index(PLANE)
    place = lax.axis_index("dp")
    side = place ^ 1
    mirror = owners - 1 - place
    to_side = [(i, i ^ 1) for i in range(owners)]
    to_mirror = [(i, owners - 1 - i) for i in range(owners)]

    def own_share(array):
        return lax.dynamic_slice_in_dim(array, rank * share, share, 0)

    my_tokens, my_grads = own_share(tokens), own_share(out_grad)
    hits = own_share(expert_ids)[:, :, None] == jnp.arange(experts, dtype=jnp.int32)
    table = jnp.sum(jnp.where(hits, own_share(gate_probs)[:, :, None], 0.0), axis=1)
    coarse = table.astype(BF16)
    fine = (table - coarse.astype(F32)).astype(BF16)
    pad = jnp.zeros((share, LANES // 2 - experts), BF16)
    payload = jnp.concatenate([my_tokens, my_grads, coarse, pad, fine, pad], axis=1)
    gathered = lax.all_gather(payload, PLANE, axis=0, tiled=True)
    from_side = lax.ppermute(
        jnp.concatenate([my_tokens[:, :half], my_grads[:, :half]], axis=1), "dp", to_side
    )
    from_mirror = lax.ppermute(
        jnp.concatenate([my_tokens[:, half:], my_grads[:, half:]], axis=1), "dp", to_mirror
    )
    near_payload = jnp.concatenate([from_side, from_mirror], axis=1)
    gathered, near_payload = lax.optimization_barrier((gathered, near_payload))
    gathered_near = lax.all_gather(near_payload, PLANE, axis=0, tiled=True)

    route = jnp.stack([side, place ^ 2, mirror, place, expert]).astype(jnp.int32)
    gate, up, down = (w.reshape(owners, units // owners, width) for w in (w_gate, w_up, w_down))
    hidden, for_side, for_mirror = hidden_rows(gathered, route, gate, up, down)
    other_side = lax.ppermute(for_side, "dp", to_side)
    other_mirror = lax.ppermute(for_mirror, "dp", to_mirror)

    rows = input_rows(hidden.reshape(3, units, -1), w_gate[0], w_up[0], share)
    kept = lax.dynamic_index_in_dim(rows, core, 0, keepdims=False)
    given = lax.dynamic_index_in_dim(rows, 1 - core, 0, keepdims=False)
    taken = lax.ppermute(given, "core", [(0, 1), (1, 0)])
    paired = (kept.astype(F32) + taken.astype(F32)).astype(BF16)
    returned = lax.all_to_all(paired, PLANE[:3], split_axis=0, concat_axis=0, tiled=True)
    in_grad = jnp.sum(returned.astype(F32), axis=0).astype(BF16)

    low_picks = jnp.stack([place, mirror]).astype(jnp.int32)
    high_picks = jnp.stack([side, place]).astype(jnp.int32)
    results = []
    for which in range(3):
        mine_low, theirs_low = weight_grads(
            which, 0, low_picks, hidden, other_side, gathered, gathered_near
        )
        low = lax.ppermute(theirs_low, "dp", to_mirror)
        theirs_high, mine_high = weight_grads(
            which, 1, high_picks, hidden, other_mirror, gathered, gathered_near
        )
        high = lax.ppermute(theirs_high, "dp", to_side)
        low = mine_low.astype(F32) + low.astype(F32)
        high = mine_high.astype(F32) + high.astype(F32)
        results.append(jnp.concatenate([low, high], axis=1).astype(BF16)[None])
    return (in_grad, *results)


def solution(mesh):
    dp, ctx, tensor = (mesh.shape[name] for name in ("dp", "ctx", "tensor"))
    fine = Mesh(
        mesh.devices.reshape(dp, ctx // 2, 2, tensor // 2, 2), ("dp", "z", "xh", "xl", "core")
    )
    token_spec = P(("dp", "z", "xh"), None)
    weight_spec = P(PLANE, None, None)
    grad_spec = P(PLANE, "dp", None)
    return jax.shard_map(
        per_device,
        mesh=fine,
        in_specs=(token_spec,) * 4 + (weight_spec,) * 3,
        out_specs=(P(("dp",) + PLANE, None), grad_spec, grad_spec, grad_spec),
        check_vma=False,
    )
```

time: 506 us -> 355 us (0.70)
  waiting for transfers between devices: 362 us -> 161 us
  Pallas kernels: 96.9 us -> 124 us
  starting transfers between devices: 5.96 us -> 20.9 us
  other arithmetic: 11.6 us -> 18.7 us
    unnamed x3 -> x2, waiting for transfers between devices: 220 us -> 0.03 us
    ppermute x0 -> x10, waiting for transfers between devices: none -> 35.7 us  [the longest x3 28.1 us: per_device(): high = lax.ppermute(theirs_high, 'dp', to_side)]
    pallas_call x1, Pallas kernels: 31.6 us -> 54.6 us  [hidden_rows(): pl.pallas_call(hidden_kernel, grid_spec=pltpu.PrefetchScalarGridSpec(num_...]
    ppermute x0 -> x10, starting transfers between devices: none -> 15.2 us  [the longest x3 6.04 us: per_device(): low = lax.ppermute(theirs_low, 'dp', to_mirror)]
    all_gather x1, waiting for transfers between devices: 75.7 us -> 62.7 us  [per_device(): gathered = lax.all_gather(payload, PLANE, axis=0, tiled=True)]
    concatenate x0 -> x12, other arithmetic: none -> 6.28 us  [the longest x9 5.41 us: per_device(): results.append(jnp.concatenate([low, high], axis=1).astype(BF16)[None])]
    pallas_call x1 -> x6, Pallas kernels: 46.2 us -> 50.1 us  [weight_grads(): pl.pallas_call(weight_kernel, grid_spec=pltpu.PrefetchScalarGridSpec(num_...]
  transfers between devices with their start and end apart: 4 -> 14, of which waited for: 4 -> 8; matrix products, arithmetic and copies ran while one was open for 3% -> 7% of each run, Pallas kernels for 4% -> 35%
where the time goes in v1:
time: 355 us; the launch traced here: 351 us
  waiting for transfers between devices  161 us (45%)
  Pallas kernels  124 us (35%)
  starting transfers between devices  20.9 us (6%)
  other arithmetic  18.7 us (5%)
  between operations  14.2 us (4%)
  local copies, waits for them, and re-layouts  12.1 us (3%)
    all_gather x1, waiting for transfers between devices, per_device(): gathered = lax.all_gather(payload, PLANE, axis=0, tiled=True)  62.7 us
    all_to_all x1, waiting for transfers between devices, per_device(): lax.all_to_all(paired, PLANE[:3], split_axis=0, concat_axis=0, tiled=True)  55 us
    pallas_call x1, Pallas kernels, hidden_rows(): pl.pallas_call(hidden_kernel, grid_spec=pltpu.PrefetchScalarGridSpec(num_...  54.6 us
    pallas_call x6, Pallas kernels, weight_grads(): pl.pallas_call(weight_kernel, grid_spec=pltpu.PrefetchScalarGridSpec(num_...  50.1 us
    ppermute x3, waiting for transfers between devices, per_device(): high = lax.ppermute(theirs_high, 'dp', to_side)  28.1 us
    pallas_call x1, Pallas kernels, input_rows(): pl.pallas_call(input_kernel, grid=(width // step,), in_specs=[pl.BlockSpe...  19.2 us
    convert_element_type x1, other arithmetic, per_device(): paired = (kept.astype(F32) + taken.astype(F32)).astype(BF16)  7.28 us
    ppermute x1, waiting for transfers between devices, per_device(): taken = lax.ppermute(given, 'core', [(0, 1), (1, 0)])  7.23 us
  transfers between devices with their start and end apart: 14, of which 8 were waited for; matrix products, arithmetic and copies ran while one was open for 7% of the time, Pallas kernels for 35%

profile of v1, /device:TPU:2, one launch (start us, length us, event | category | flops | bytes accessed | tf_op | source)
XLA Modules:
  0.0 350.6 jit_solution(8549534197182800095)
XLA Ops:
  9.0 1.1 constant_dynamic-slice_fusion.4
  10.1 0.9 concatenate.57
  11.1 1.1 constant_dynamic-slice_fusion
  12.3 3.1 collective-permute-start.1
  15.6 6.1 %collective-permute-done.1 = bf16[32,4096]{1,0:T(8,128)(2,1)S(1)} collective-permute-done((bf16[32,4096]{1,0:T(8,128)(2,1)S(1)}, bf16[32,4096]{1,0:T(8,128)(2,1)S(1)}, u32[]{:S(2)}, u32[]{:S(2)}) %collective-permute-start.1) | collective-permute-done | bytes 262176 | tf_op jit(solution)/shard_map/ppermute | solution.py:253
  21.7 1.6 collective-permute-done
  24.1 62.7 %all-gather.3.cloned.1.call-done.gathered_ref.own_ref = bf16[1024,8320]{1,0:T(8,128)(2,1)} async-done(((bf16[32,8320]{1,0:T(8,128)(2,1)}), bf16[1024,8320]{1,0:T(8,128)(2,1)}) %all-gather.3.cloned.1.call-update) | async-done | bytes 17039376 | tf_op jit(solution)/shard_map/all_gather | solution.py:249
  87.5 54.6 %hidden_rows.1 = (bf16[3,4,192,1024]{3,2,1,0:T(8,128)(2,1)}, bf16[3,2,192,1024]{3,2,1,0:T(8,128)(2,1)}, bf16[3,2,192,1024]{3,2,1,0:T(8,128)(2,1)}) custom-call(s32[5]{0:T(128)} %stack.33.route_ref, bf16[1024,8320]{1,0:T(8,128)(2,1)} %all-gather.3.cloned.1.call-done.gathered_ref.own_ref, bf16[4,192,4096]{2,1,0:T(8,128)(2,1)} %bitcast.30, ...), custom_call_target="tpu_custom_call" | custom-call | flops 19327352832 | bytes 35913728 | tf_op jit(solution)/shard_map/hidden_rows/pallas_call | solution.py:97
  142.1 19.2 %input_rows.1 = bf16[2,16,32,4096]{3,2,1,0:T(8,128)(2,1)} custom-call(bf16[3,768,1024]{2,1,0:T(8,128)(2,1)} %bitcast.28, bf16[768,4096]{1,0:T(8,128)(2,1)} %bitcast.31, bf16[768,4096]{1,0:T(8,128)(2,1)} %bitcast.33), custom_call_target="tpu_custom_call" | custom-call | flops 12884901888 | bytes 20971520 | tf_op jit(solution)/shard_map/input_rows/pallas_call | solution.py:147
  161.3 4.6 %dynamic-slice_bitcast_fusion = bf16[16,32,4096]{2,1,0:T(8,128)(2,1)} fusion(bf16[2,16,32,4096]{3,2,1,0:T(8,128)(2,1)} %input_rows.1, s32[]{:T(128)S(6)} %select_n.20), kind=kLoop, calls=%fused_computation.2 | loop fusion | bytes 8388612 | tf_op jit(solution)/shard_map/jit(dynamic_index_in_dim)/squeeze | solution.py:268
  166.2 7.2 %collective-permute-done.2 = bf16[16,32,4096]{2,1,0:T(8,128)(2,1)} collective-permute-done((bf16[16,32,4096]{2,1,0:T(8,128)(2,1)}, bf16[16,32,4096]{2,1,0:T(8,128)(2,1)}, u32[]{:S(2)}, u32[]{:S(2)}) %collective-permute-start.2) | collective-permute-done | bytes 4194336 | tf_op jit(solution)/shard_map/ppermute | solution.py:269
  173.5 7.3 %fusion = bf16[16,32,4096]{2,1,0:T(8,128)(2,1)} fusion(bf16[16,32,4096]{2,1,0:T(8,128)(2,1)} %collective-permute-done.2, bf16[2,16,32,4096]{3,2,1,0:T(8,128)(2,1)} %input_rows.1, s32[]{:T(128)S(6)} %select_n.19), kind=kLoop, calls=%fused_computation.1 | loop fusion | flops 8388608 | bytes 12582916 | tf_op jit(solution)/shard_map/convert_element_type | solution.py:270
  180.7 5.4 %all-to-all-start = ((bf16[16,32,4096]{2,1,0:T(8,128)(2,1)}), bf16[16,32,4096]{2,1,0:T(8,128)(2,1)}, u32[]{:S(2)}, u32[]{:S(2)}) async-start(bf16[16,32,4096]{2,1,0:T(8,128)(2,1)} %fusion), calls=%async_computation | async-start | bytes 8388608 | tf_op jit(solution)/shard_map/all_to_all | solution.py:271
  186.1 1.5 collective-permute-start.3
  187.6 2.1 collective-permute-start.5
  190.9 55.0 %all-to-all-done = bf16[16,32,4096]{2,1,0:T(8,128)(2,1)} async-done(((bf16[16,32,4096]{2,1,0:T(8,128)(2,1)}), bf16[16,32,4096]{2,1,0:T(8,128)(2,1)}, u32[]{:S(2)}, u32[]{:S(2)}) %all-to-all-start) | async-done | bytes 4194336 | tf_op jit(solution)/shard_map/all_to_all | solution.py:271
  245.9 3.7 %reduce_sum.22 = bf16[32,4096]{1,0:T(8,128)(2,1)} reduce(bf16[16,32,4096]{2,1,0:T(8,128)(2,1)} %all-to-all-done, bf16[]{:T(256)} %constant.45.clone.1), dimensions={0}, to_apply=%region_1.2 | reduce | flops 1966080 | bytes 4456450 | tf_op jit(solution)/shard_map/reduce_sum | solution.py:272
  249.6 8.3 %weight_grads.10 = (bf16[192,2048]{1,0:T(8,128)(2,1)}, bf16[192,2048]{1,0:T(8,128)(2,1)}) custom-call(s32[2]{0:T(128)} %pad_add_fusion.pick_ref, bf16[3,4,192,1024]{3,2,1,0:T(8,128)(2,1)} %get-tuple-element.22.first_ref.second_ref, bf16[3,4,192,1024]{3,2,1,0:T(8,128)(2,1)} %get-tuple-element.22.first_ref.second_ref, ...), custom_call_target="tpu_custom_call" | custom-call | flops 3221225472 | bytes 10747904 | tf_op jit(solution)/shard_map/weight_grads/pallas_call | solution.py:196
  258.0 2.8 collective-permute-start.9
  260.8 8.4 %weight_grads.8 = (bf16[192,2048]{1,0:T(8,128)(2,1)}, bf16[192,2048]{1,0:T(8,128)(2,1)}) custom-call(s32[2]{0:T(128)} %pad_add_fusion.pick_ref, bf16[3,4,192,1024]{3,2,1,0:T(8,128)(2,1)} %get-tuple-element.22.first_ref.second_ref, bf16[3,4,192,1024]{3,2,1,0:T(8,128)(2,1)} %get-tuple-element.22.first_ref.second_ref, ...), custom_call_target="tpu_custom_call" | custom-call | flops 3221225472 | bytes 10747904 | tf_op jit(solution)/shard_map/weight_grads/pallas_call | solution.py:196
  269.6 8.4 %weight_grads.6 = (bf16[192,2048]{1,0:T(8,128)(2,1)}, bf16[192,2048]{1,0:T(8,128)(2,1)}) custom-call(s32[2]{0:T(128)} %pad_add_fusion.pick_ref, bf16[3,4,192,1024]{3,2,1,0:T(8,128)(2,1)} %get-tuple-element.22.first_ref.second_ref, bf16[3,4,192,1024]{3,2,1,0:T(8,128)(2,1)} %get-tuple-element.22.first_ref.second_ref, ...), custom_call_target="tpu_custom_call" | custom-call | flops 3221225472 | bytes 10747904 | tf_op jit(solution)/shard_map/weight_grads/pallas_call | solution.py:196
  278.0 2.8 collective-permute-start.4
  280.8 1.4 copy-done.2
  282.2 8.3 %weight_grads.11 = (bf16[192,2048]{1,0:T(8,128)(2,1)}, bf16[192,2048]{1,0:T(8,128)(2,1)}) custom-call(s32[2]{0:T(128)} %pad_add_fusion.1.pick_ref, bf16[3,4,192,1024]{3,2,1,0:T(8,128)(2,1)} %get-tuple-element.22.first_ref.second_ref, bf16[3,4,192,1024]{3,2,1,0:T(8,128)(2,1)} %get-tuple-element.22.first_ref.second_ref, bf16[3,2,192,1024]{3,2,1,0:T(8,128)(2,1)} %copy-done.2, ...), custom_call_target="tpu_custom_call" | custom-call | flops 3221225472 | bytes 10747904 | tf_op jit(solution)/shard_map/weight_grads/pallas_call | solution.py:196
  290.6 8.3 %weight_grads.9 = (bf16[192,2048]{1,0:T(8,128)(2,1)}, bf16[192,2048]{1,0:T(8,128)(2,1)}) custom-call(s32[2]{0:T(128)} %pad_add_fusion.1.pick_ref, bf16[3,4,192,1024]{3,2,1,0:T(8,128)(2,1)} %get-tuple-element.22.first_ref.second_ref, bf16[3,4,192,1024]{3,2,1,0:T(8,128)(2,1)} %get-tuple-element.22.first_ref.second_ref, bf16[3,2,192,1024]{3,2,1,0:T(8,128)(2,1)} %copy-done.2, ...), custom_call_target="tpu_custom_call" | custom-call | flops 3221225472 | bytes 10747904 | tf_op jit(solution)/shard_map/weight_grads/pallas_call | solution.py:196
  298.9 2.1 collective-permute-start.8
  300.9 8.3 %weight_grads.7 = (bf16[192,2048]{1,0:T(8,128)(2,1)}, bf16[192,2048]{1,0:T(8,128)(2,1)}) custom-call(s32[2]{0:T(128)} %pad_add_fusion.1.pick_ref, bf16[3,4,192,1024]{3,2,1,0:T(8,128)(2,1)} %get-tuple-element.22.first_ref.second_ref, bf16[3,4,192,1024]{3,2,1,0:T(8,128)(2,1)} %get-tuple-element.22.first_ref.second_ref, bf16[3,2,192,1024]{3,2,1,0:T(8,128)(2,1)} %copy-done.2, ...), custom_call_target="tpu_custom_call" | custom-call | flops 3221225472 | bytes 10747904 | tf_op jit(solution)/shard_map/weight_grads/pallas_call | solution.py:196
  311.5 16.6 %collective-permute-done.8 = bf16[192,2048]{1,0:T(8,128)(2,1)S(1)} collective-permute-done((bf16[192,2048]{1,0:T(8,128)(2,1)}, bf16[192,2048]{1,0:T(8,128)(2,1)S(1)}, u32[]{:S(2)}, u32[]{:S(2)}) %collective-permute-start.8) | collective-permute-done | bytes 786464 | tf_op jit(solution)/shard_map/ppermute | solution.py:285
  328.4 1.3 pad_maximum_fusion.2
  329.7 1.3 pad_maximum_fusion.1
  331.3 10.9 %collective-permute-done.6 = bf16[192,2048]{1,0:T(8,128)(2,1)S(1)} collective-permute-done((bf16[192,2048]{1,0:T(8,128)(2,1)}, bf16[192,2048]{1,0:T(8,128)(2,1)S(1)}, u32[]{:S(2)}, u32[]{:S(2)}) %collective-permute-start.6) | collective-permute-done | bytes 786464 | tf_op jit(solution)/shard_map/ppermute | solution.py:285
  342.5 1.3 pad_maximum_fusion
  (52 shorter events, 8.6 us)
Async XLA Ops:
  7.2 0.7 copy-start
  7.2 79.6 %all-gather.3.cloned.1.call-start = ((), (), s32[]{:S(2)}) async-start(), calls=%async_computation.1 | async-start | bytes 17571840 | tf_op jit(solution)/shard_map/all_gather | solution.py:249
  11.1 238.6 %all-gather.5.cloned.1.call-start = ((), (), s32[]{:S(2)}) async-start(), calls=%async_computation.2 | async-start | bytes 17301504 | tf_op jit(solution)/shard_map/all_gather | solution.py:258
  12.3 9.4 %collective-permute-start.1 = (bf16[32,4096]{1,0:T(8,128)(2,1)S(1)}, bf16[32,4096]{1,0:T(8,128)(2,1)S(1)}, u32[]{:S(2)}, u32[]{:S(2)}) collective-permute-start(bf16[32,4096]{1,0:T(8,128)(2,1)S(1)} %pad_maximum_fusion.5), channel_id=1, source_target_pairs={{0,96},{32,64},{64,32},{96,0},{1,97},{33,65},{65,33},{97,1},{2,98}... | collective-permute-start | bytes 786440 | tf_op jit(solution)/shard_map/ppermute | solution.py:253
  15.4 7.8 %collective-permute-start = (bf16[32,4096]{1,0:T(8,128)(2,1)S(1)}, bf16[32,4096]{1,0:T(8,128)(2,1)S(1)}, u32[]{:S(2)}, u32[]{:S(2)}) collective-permute-start(bf16[32,4096]{1,0:T(8,128)(2,1)S(1)} %pad_maximum_fusion.4), channel_id=1, source_target_pairs={{0,32},{32,0},{64,96},{96,64},{1,33},{33,1},{65,97},{97,65},{2,34}... | collective-permute-start | bytes 786440 | tf_op jit(solution)/shard_map/ppermute | solution.py:250
  166.0 7.5 %collective-permute-start.2 = (bf16[16,32,4096]{2,1,0:T(8,128)(2,1)}, bf16[16,32,4096]{2,1,0:T(8,128)(2,1)}, u32[]{:S(2)}, u32[]{:S(2)}) collective-permute-start(bf16[16,32,4096]{2,1,0:T(8,128)(2,1)} %dynamic-slice_bitcast_fusion), channel_id=1, source_target_pairs={{0,1},{1,0},{2,3},{3,2},{4,5},{5,4},{6,7},{7,6},{8,9},{9,8},{10,11... | collective-permute-start | bytes 12582920 | tf_op jit(solution)/shard_map/ppermute | solution.py:269
  180.7 65.2 %all-to-all-start = ((bf16[16,32,4096]{2,1,0:T(8,128)(2,1)}), bf16[16,32,4096]{2,1,0:T(8,128)(2,1)}, u32[]{:S(2)}, u32[]{:S(2)}) async-start(bf16[16,32,4096]{2,1,0:T(8,128)(2,1)} %fusion), calls=%async_computation | async-start | bytes 8388608 | tf_op jit(solution)/shard_map/all_to_all | solution.py:271
  186.1 63.5 %collective-permute-start.3 = (bf16[3,2,192,1024]{3,2,1,0:T(8,128)(2,1)}, bf16[3,2,192,1024]{3,2,1,0:T(8,128)(2,1)}, u32[]{:S(2)}, u32[]{:S(2)}) collective-permute-start(bf16[3,2,192,1024]{3,2,1,0:T(8,128)(2,1)} %get-tuple-element.23), channel_id=1, source_target_pairs={{0,32},{32,0},{64,96},{96,64},{1,33},{33,1},{65,97},{97,65},{2,34}... | collective-permute-start | bytes 7077896 | tf_op jit(solution)/shard_map/ppermute | solution.py:263
  187.6 93.3 %collective-permute-start.5 = (bf16[3,2,192,1024]{3,2,1,0:T(8,128)(2,1)}, bf16[3,2,192,1024]{3,2,1,0:T(8,128)(2,1)S(1)}, u32[]{:S(2)}, u32[]{:S(2)}) collective-permute-start(bf16[3,2,192,1024]{3,2,1,0:T(8,128)(2,1)} %get-tuple-element.27), channel_id=1, source_target_pairs={{0,96},{32,64},{64,32},{96,0},{1,97},{33,65},{65,33},{97,1},{2,98}... | collective-permute-start | bytes 7077896 | tf_op jit(solution)/shard_map/ppermute | solution.py:264
  258.0 51.3 %collective-permute-start.9 = (bf16[192,2048]{1,0:T(8,128)(2,1)}, bf16[192,2048]{1,0:T(8,128)(2,1)S(1)}, u32[]{:S(2)}, u32[]{:S(2)}) collective-permute-start(bf16[192,2048]{1,0:T(8,128)(2,1)} %get-tuple-element.35), channel_id=1, source_target_pairs={{0,96},{32,64},{64,32},{96,0},{1,97},{33,65},{65,33},{97,1},{2,98}... | collective-permute-start | bytes 2359304 | tf_op jit(solution)/shard_map/ppermute | solution.py:281
  269.2 40.6 %collective-permute-start.7 = (bf16[192,2048]{1,0:T(8,128)(2,1)}, bf16[192,2048]{1,0:T(8,128)(2,1)S(1)}, u32[]{:S(2)}, u32[]{:S(2)}) collective-permute-start(bf16[192,2048]{1,0:T(8,128)(2,1)} %get-tuple-element.31), channel_id=1, source_target_pairs={{0,96},{32,64},{64,32},{96,0},{1,97},{33,65},{65,33},{97,1},{2,98}... | collective-permute-start | bytes 2359304 | tf_op jit(solution)/shard_map/ppermute | solution.py:281
  278.0 52.9 %collective-permute-start.4 = (bf16[192,2048]{1,0:T(8,128)(2,1)}, bf16[192,2048]{1,0:T(8,128)(2,1)S(1)}, u32[]{:S(2)}, u32[]{:S(2)}) collective-permute-start(bf16[192,2048]{1,0:T(8,128)(2,1)} %get-tuple-element.26), channel_id=1, source_target_pairs={{0,96},{32,64},{64,32},{96,0},{1,97},{33,65},{65,33},{97,1},{2,98}... | collective-permute-start | bytes 2359304 | tf_op jit(solution)/shard_map/ppermute | solution.py:281
  280.8 1.4 copy-start.2
  290.5 20.7 %collective-permute-start.10 = (bf16[192,2048]{1,0:T(8,128)(2,1)}, bf16[192,2048]{1,0:T(8,128)(2,1)S(1)}, u32[]{:S(2)}, u32[]{:S(2)}) collective-permute-start(bf16[192,2048]{1,0:T(8,128)(2,1)} %get-tuple-element.37), channel_id=1, source_target_pairs={{0,32},{32,0},{64,96},{96,64},{1,33},{33,1},{65,97},{97,65},{2,34}... | collective-permute-start | bytes 2359304 | tf_op jit(solution)/shard_map/ppermute | solution.py:285
  298.9 10.6 %copy-start.6 = (bf16[192,2048]{1,0:T(8,128)(2,1)S(1)}, bf16[192,2048]{1,0:T(8,128)(2,1)}, u32[]{:S(2)}) copy-start(bf16[192,2048]{1,0:T(8,128)(2,1)} %get-tuple-element.34) | copy-start | bytes 2359300
  298.9 29.2 %collective-permute-start.8 = (bf16[192,2048]{1,0:T(8,128)(2,1)}, bf16[192,2048]{1,0:T(8,128)(2,1)S(1)}, u32[]{:S(2)}, u32[]{:S(2)}) collective-permute-start(bf16[192,2048]{1,0:T(8,128)(2,1)} %get-tuple-element.33), channel_id=1, source_target_pairs={{0,32},{32,0},{64,96},{96,64},{1,33},{33,1},{65,97},{97,65},{2,34}... | collective-permute-start | bytes 2359304 | tf_op jit(solution)/shard_map/ppermute | solution.py:285
  309.3 1.1 copy-start.5
  309.3 32.9 %collective-permute-start.6 = (bf16[192,2048]{1,0:T(8,128)(2,1)}, bf16[192,2048]{1,0:T(8,128)(2,1)S(1)}, u32[]{:S(2)}, u32[]{:S(2)}) collective-permute-start(bf16[192,2048]{1,0:T(8,128)(2,1)} %get-tuple-element.29), channel_id=1, source_target_pairs={{0,32},{32,0},{64,96},{96,64},{1,33},{33,1},{65,97},{97,65},{2,34}... | collective-permute-start | bytes 2359304 | tf_op jit(solution)/shard_map/ppermute | solution.py:285
  309.5 1.7 copy-start.8
  310.4 17.7 %copy-start.7 = (bf16[192,2048]{1,0:T(8,128)(2,1)S(1)}, bf16[192,2048]{1,0:T(8,128)(2,1)}, u32[]{:S(2)}) copy-start(bf16[192,2048]{1,0:T(8,128)(2,1)} %get-tuple-element.32) | copy-start | bytes 2359300
  329.6 1.3 copy-start.3
  329.7 12.6 %copy-start.4 = (bf16[192,2048]{1,0:T(8,128)(2,1)S(1)}, bf16[192,2048]{1,0:T(8,128)(2,1)}, u32[]{:S(2)}) copy-start(bf16[192,2048]{1,0:T(8,128)(2,1)} %get-tuple-element.28) | copy-start | bytes 2359300
  342.2 1.5 copy-start.1
Sparse Core Ops, SparseCore 0:
  11.2 75.5 all-gather.2
  89.6 72.0 all-gather.4

commit v2 on v1

v2 whole, which is shorter than its diff:
```python
import functools

import jax
import jax.numpy as jnp
from jax import lax
from jax.experimental import pallas as pl
from jax.experimental.pallas import tpu as pltpu
from jax.sharding import Mesh
from jax.sharding import PartitionSpec as P

BF16 = jnp.bfloat16
F32 = jnp.float32
VMEM_LIMIT = 56 * 1024 * 1024
PLANE = ("z", "xh", "xl", "core")
LANES = 128
SMALL = pl.CostEstimate(flops=0, bytes_accessed=0, transcendentals=0)


def hidden_kernel(
    start, route_ref, gathered_ref, gate_ref, up_ref, down_ref, out_ref, near_ref, far_ref,
    held, gate, up, down, token_sems, weight_sems,
):
    rows = out_ref.shape[3]
    owners, share, width = gate_ref.shape
    block = 256
    weights = ((gate_ref, gate), (up_ref, up), (down_ref, down))

    def token_copy(part):
        columns = pl.ds(0, width) if part == 0 else pl.ds(width, held.shape[1] - width)
        return pltpu.make_async_copy(
            gathered_ref.at[pl.ds(start, rows), columns], held.at[:, columns], token_sems.at[part]
        )

    def weight_copy(which, place):
        source, target = weights[which]
        return pltpu.make_async_copy(
            source.at[route_ref[place]],
            target.at[pl.ds(place * share, share)],
            weight_sems.at[which, place],
        )

    token_copy(0).start()
    for which in range(3):
        if which == 2:
            token_copy(1).start()
        weight_copy(which, 0).start()
        weight_copy(which, 1).start()
    for place in range(2, owners):
        for which in range(3):
            weight_copy(which, place).start()

    by_features = (((1,), (1,)), ((), ()))
    pieces = ([], [], [])
    for third in range(3):
        span = pl.ds(third * block, block)

        def wait(which):
            if third == 0:
                weight_copy(which, 0).wait()
                weight_copy(which, 1).wait()
            else:
                weight_copy(which, third + 1).wait()

        def product(array, right):
            return lax.dot_general(array[span], right, by_features, preferred_element_type=F32)

        if third == 0:
            token_copy(0).wait()
        wait(0)
        gate_pre = product(gate, held[:, :width])
        wait(1)
        up_pre = product(up, held[:, :width])
        if third == 0:
            token_copy(1).wait()
            lane = lax.broadcasted_iota(jnp.int32, (8, LANES), 1)
            expert = route_ref[4]
            chosen = ((lane == expert) | (lane == expert + LANES // 2)).astype(F32).astype(BF16)
            prob = lax.dot_general(
                chosen, held[:, 2 * width :], by_features, preferred_element_type=F32
            )[0:1]
        wait(2)
        hidden_grad = prob * product(down, held[:, width : 2 * width])
        sigmoid = jax.nn.sigmoid(gate_pre)
        active = gate_pre * sigmoid
        slope = sigmoid * (1.0 + gate_pre * (1.0 - sigmoid))
        pieces[0].append((hidden_grad * up_pre * slope).astype(BF16))
        pieces[1].append((hidden_grad * active).astype(BF16))
        pieces[2].append((prob * active * up_pre).astype(BF16))
    for which in range(3):
        result = jnp.concatenate(pieces[which], axis=0).reshape(owners, share, rows)
        for place in range(owners):
            out_ref[which, route_ref[place]] = result[place]
        near_ref[which] = result[0:2]
        far_ref[which] = result[1:3]


def hidden_rows(gathered, start, rows, route, w_gate, w_up, w_down):
    owners, share, width = w_gate.shape
    whole = pl.BlockSpec(memory_space=pl.ANY)
    kept = pltpu.VMEM((owners * share, width), BF16)
    pair = pl.BlockSpec((3, 2, share, rows), lambda t, r: (0, 0, 0, 0))
    return pl.pallas_call(
        functools.partial(hidden_kernel, start),
        grid_spec=pltpu.PrefetchScalarGridSpec(
            num_scalar_prefetch=1,
            grid=(1,),
            in_specs=[whole, whole, whole, whole],
            out_specs=[pl.BlockSpec((3, owners, share, rows), lambda t, r: (0, 0, 0, 0)), pair, pair],
            scratch_shapes=[
                pltpu.VMEM((rows, gathered.shape[1]), BF16),
                kept,
                kept,
                kept,
                pltpu.SemaphoreType.DMA((2,)),
                pltpu.SemaphoreType.DMA((3, owners)),
            ],
        ),
        out_shape=[
            jax.ShapeDtypeStruct((3, owners, share, rows), BF16),
            jax.ShapeDtypeStruct((3, 2, share, rows), BF16),
            jax.ShapeDtypeStruct((3, 2, share, rows), BF16),
        ],
        compiler_params=pltpu.CompilerParams(vmem_limit_bytes=VMEM_LIMIT),
        cost_estimate=SMALL,
        name="hidden_rows",
    )(route, gathered, w_gate, w_up, w_down)


def input_kernel(core_ref, hidden_ref, gate_ref, up_ref, kept_ref, given_ref, turned):
    @pl.when(pl.program_id(0) == 0)
    def _():
        turned[0] = hidden_ref[0].T
        turned[1] = hidden_ref[1].T

    total = jnp.dot(turned[0], gate_ref[...], preferred_element_type=F32)
    total += jnp.dot(turned[1], up_ref[...], preferred_element_type=F32)
    groups, share, step = kept_ref.shape
    total = total.astype(BF16).reshape(groups, 2, share, step)

    @pl.when(core_ref[0] == 0)
    def _():
        kept_ref[...] = total[:, 0]
        given_ref[...] = total[:, 1]

    @pl.when(core_ref[0] != 0)
    def _():
        kept_ref[...] = total[:, 1]
        given_ref[...] = total[:, 0]


def input_rows(hidden, core, w_gate, w_up, share):
    _, units, token_count = hidden.shape
    width = w_gate.shape[1]
    step = 512
    groups = token_count // (2 * share)
    weight = pl.BlockSpec((units, step), lambda i, c: (0, i))
    part = pl.BlockSpec((groups, share, step), lambda i, c: (0, 0, i))
    shape = jax.ShapeDtypeStruct((groups, share, width), BF16)
    return pl.pallas_call(
        input_kernel,
        grid_spec=pltpu.PrefetchScalarGridSpec(
            num_scalar_prefetch=1,
            grid=(width // step,),
            in_specs=[pl.BlockSpec((2, units, token_count), lambda i, c: (0, 0, 0)), weight, weight],
            out_specs=[part, part],
            scratch_shapes=[pltpu.VMEM((2, token_count, units), BF16)],
        ),
        out_shape=[shape, shape],
        compiler_params=pltpu.CompilerParams(vmem_limit_bytes=VMEM_LIMIT),
        cost_estimate=SMALL,
        name="input_rows",
    )(core, hidden, w_gate, w_up)


def own_kernel(
    pick_ref, first_ref, second_ref, tokens_ref, grads_ref, gate_ref, up_ref, down_ref, left
):
    share = first_ref.shape[2]

    @pl.when(pl.program_id(1) == 0)
    def _():
        for which in range(3):
            left[2 * share * which : 2 * share * which + share] = first_ref[which, 0]
            left[2 * share * which + share : 2 * share * (which + 1)] = second_ref[which, 0]

    both = jnp.dot(left[: 4 * share], tokens_ref[...], preferred_element_type=F32)
    gate_ref[0] = both[: 2 * share]
    up_ref[0] = both[2 * share :]
    down_ref[0] = jnp.dot(left[4 * share :], grads_ref[...], preferred_element_type=F32)


def own_grads(picks, hidden, gathered, width):
    _, _, share, token_count = hidden.shape
    step = 512
    count = width // 2 // step
    out = pl.BlockSpec((1, 2 * share, step), lambda h, i, p: (h, 0, i))
    shape = jax.ShapeDtypeStruct((2, 2 * share, width // 2), F32)
    return pl.pallas_call(
        own_kernel,
        grid_spec=pltpu.PrefetchScalarGridSpec(
            num_scalar_prefetch=1,
            grid=(2, count),
            in_specs=[
                pl.BlockSpec((3, 1, share, token_count), lambda h, i, p: (0, p[2 * h], 0, 0)),
                pl.BlockSpec((3, 1, share, token_count), lambda h, i, p: (0, p[2 * h + 1], 0, 0)),
                pl.BlockSpec((token_count, step), lambda h, i, p: (0, h * count + i)),
                pl.BlockSpec((token_count, step), lambda h, i, p: (0, (2 + h) * count + i)),
            ],
            out_specs=[out, out, out],
            scratch_shapes=[pltpu.VMEM((6 * share, token_count), BF16)],
        ),
        out_shape=[shape, shape, shape],
        compiler_params=pltpu.CompilerParams(vmem_limit_bytes=VMEM_LIMIT),
        cost_estimate=SMALL,
        name="own_grads",
    )(picks, hidden, hidden, gathered, gathered)


def weight_kernel(other_ref, near_ref, own_ref, out_first, out_second):
    share = out_first.shape[0]
    left = other_ref[0].reshape(2 * share, other_ref.shape[3])
    total = own_ref[0] + jnp.dot(left, near_ref[...], preferred_element_type=F32)
    out_first[...] = total[:share].astype(BF16)
    out_second[...] = total[share:].astype(BF16)


def weight_grads(which, half, other, gathered_near, own):
    _, _, share, token_count = other.shape
    columns = gathered_near.shape[1] // 4
    step = 512
    count = columns // step
    near_base = (half * 2 + which // 2) * count
    out = pl.BlockSpec((share, step), lambda i: (0, i))
    shape = jax.ShapeDtypeStruct((share, columns), BF16)
    return pl.pallas_call(
        weight_kernel,
        grid=(count,),
        in_specs=[
            pl.BlockSpec((1, 2, share, token_count), lambda i: (which, 0, 0, 0)),
            pl.BlockSpec((token_count, step), lambda i: (0, near_base + i)),
            pl.BlockSpec((1, 2 * share, step), lambda i: (half, 0, i)),
        ],
        out_specs=[out, out],
        out_shape=[shape, shape],
        compiler_params=pltpu.CompilerParams(vmem_limit_bytes=VMEM_LIMIT),
        cost_estimate=SMALL,
        name="weight_grads",
    )(other, gathered_near, own)


def per_device(tokens, out_grad, expert_ids, gate_probs, w_gate, w_up, w_down):
    token_count, width = tokens.shape
    half = width // 2
    owners = lax.axis_size("dp")
    ranks = lax.axis_size(("xl", "core"))
    experts = lax.axis_size(PLANE)
    units = w_gate.shape[1]
    share = token_count // ranks
    rank = lax.axis_index(("xl", "core"))
    core = lax.axis_index("core")
    expert = lax.axis_index(PLANE)
    place = lax.axis_index("dp")
    side = place ^ 1
    mirror = owners - 1 - place
    to_side = [(i, i ^ 1) for i in range(owners)]
    to_mirror = [(i, owners - 1 - i) for i in range(owners)]

    def own_share(array):
        return lax.dynamic_slice_in_dim(array, rank * share, share, 0)

    my_tokens, my_grads = own_share(tokens), own_share(out_grad)
    hits = own_share(expert_ids)[:, :, None] == jnp.arange(experts, dtype=jnp.int32)
    table = jnp.sum(jnp.where(hits, own_share(gate_probs)[:, :, None], 0.0), axis=1)
    coarse = table.astype(BF16)
    fine = (table - coarse.astype(F32)).astype(BF16)
    pad = jnp.zeros((share, LANES // 2 - experts), BF16)
    payload = jnp.concatenate([my_tokens, my_grads, coarse, pad, fine, pad], axis=1)
    gathered = lax.all_gather(payload, PLANE, axis=0, tiled=True)
    from_side = lax.ppermute(
        jnp.concatenate([my_tokens[:, :half], my_grads[:, :half]], axis=1), "dp", to_side
    )
    from_mirror = lax.ppermute(
        jnp.concatenate([my_tokens[:, half:], my_grads[:, half:]], axis=1), "dp", to_mirror
    )
    near_payload = jnp.concatenate([from_side, from_mirror], axis=1)
    gathered, near_payload = lax.optimization_barrier((gathered, near_payload))
    gathered_near = lax.all_gather(near_payload, PLANE, axis=0, tiled=True)

    route = jnp.stack([side, place ^ 2, mirror, place, expert]).astype(jnp.int32)
    gate, up, down = (w.reshape(owners, units // owners, width) for w in (w_gate, w_up, w_down))
    hidden, for_side, for_mirror = hidden_rows(
        gathered, 0, gathered.shape[0], route, gate, up, down
    )
    other_side = lax.ppermute(for_side, "dp", to_side)
    other_mirror = lax.ppermute(for_mirror, "dp", to_mirror)

    kept, given = input_rows(
        hidden.reshape(3, units, -1), core[None], w_gate[0], w_up[0], share
    )
    picks = jnp.stack([place, mirror, side, place]).astype(jnp.int32)
    own = own_grads(picks, hidden, gathered, width)
    kept, given, own, other_side, other_mirror = lax.optimization_barrier(
        (kept, given, own, other_side, other_mirror)
    )
    taken = lax.ppermute(given, "core", [(0, 1), (1, 0)])
    paired = (kept.astype(F32) + taken.astype(F32)).astype(BF16)
    returned = lax.all_to_all(paired, PLANE[:3], split_axis=0, concat_axis=0, tiled=True)

    mine, theirs = [], []
    for which in (2, 0, 1):
        mine_low, theirs_low = weight_grads(which, 0, other_side, gathered_near, own[which])
        theirs_high, mine_high = weight_grads(which, 1, other_mirror, gathered_near, own[which])
        mine.append((mine_low, mine_high))
        theirs.append((theirs_low, theirs_high))
    results = []
    for (mine_low, mine_high), (theirs_low, theirs_high) in zip(mine, theirs):
        low = mine_low.astype(F32) + lax.ppermute(theirs_low, "dp", to_mirror).astype(F32)
        high = mine_high.astype(F32) + lax.ppermute(theirs_high, "dp", to_side).astype(F32)
        results.append(jnp.concatenate([low, high], axis=1).astype(BF16)[None])
    returned, results = lax.optimization_barrier((returned, results))
    in_grad = jnp.sum(returned.astype(F32), axis=0).astype(BF16)
    return (in_grad, results[1], results[2], results[0])


def solution(mesh):
    dp, ctx, tensor = (mesh.shape[name] for name in ("dp", "ctx", "tensor"))
    fine = Mesh(
        mesh.devices.reshape(dp, ctx // 2, 2, tensor // 2, 2), ("dp", "z", "xh", "xl", "core")
    )
    token_spec = P(("dp", "z", "xh"), None)
    weight_spec = P(PLANE, None, None)
    grad_spec = P(PLANE, "dp", None)
    return jax.shard_map(
        per_device,
        mesh=fine,
        in_specs=(token_spec,) * 4 + (weight_spec,) * 3,
        out_specs=(P(("dp",) + PLANE, None), grad_spec, grad_spec, grad_spec),
        check_vma=False,
    )
```

time: 355 us -> 278 us (0.78)
  waiting for transfers between devices: 161 us -> 104 us
  Pallas kernels: 124 us -> 113 us
  local copies, waits for them, and re-layouts: 12.1 us -> 6.13 us
    all_to_all x1, waiting for transfers between devices: 55 us -> 8.09 us  [per_device(): lax.all_to_all(paired, PLANE[:3], split_axis=0, concat_axis=0, tiled=True)]
    ppermute x6, waiting for transfers between devices: 28.1 us -> 14.7 us  [the longest x3 8.38 us: per_device(): lax.ppermute(theirs_high, 'dp', to_side).astype(F32)]
    pallas_call x8 -> x9, Pallas kernels: 124 us -> 113 us  [the longest x6 37.2 us: weight_grads(): pl.pallas_call(weight_kernel, grid=(count,), in_specs=[pl.BlockSpec((1, 2...]
    ppermute x1, waiting for transfers between devices: 0.01 us -> 8.71 us  [per_device(): other_side = lax.ppermute(for_side, 'dp', to_side)]
    ppermute x1, waiting for transfers between devices: 7.23 us -> 0.01 us  [per_device(): taken = lax.ppermute(given, 'core', [(0, 1), (1, 0)])]
    squeeze x1 -> x0, local copies, waits for them, and re-layouts: 4.63 us -> none  [per_device(): given = lax.dynamic_index_in_dim(rows, 1 - core, 0, keepdims=False)]
  transfers between devices with their start and end apart: 14 -> 14, of which waited for: 8 -> 9; matrix products, arithmetic and copies ran while one was open for 7% -> 5% of each run, Pallas kernels for 35% -> 41%
where the time goes in v2:
time: 278 us; the launch traced here: 274 us
  Pallas kernels  113 us (41%)
  waiting for transfers between devices  104 us (37%)
  starting transfers between devices  20.1 us (7%)
  other arithmetic  16.8 us (6%)
  between operations  14.3 us (5%)
  local copies, waits for them, and re-layouts  6.13 us (2%)
    all_gather x1, waiting for transfers between devices, per_device(): gathered = lax.all_gather(payload, PLANE, axis=0, tiled=True)  63 us
    pallas_call x6, Pallas kernels, weight_grads(): pl.pallas_call(weight_kernel, grid=(count,), in_specs=[pl.BlockSpec((1, 2...  37.2 us
    pallas_call x1, Pallas kernels, hidden_rows(): pl.pallas_call(functools.partial(hidden_kernel, start), grid_spec=pltpu.P...  35.2 us
    pallas_call x1, Pallas kernels, own_grads(): pl.pallas_call(own_kernel, grid_spec=pltpu.PrefetchScalarGridSpec(num_sca...  20.5 us
    pallas_call x1, Pallas kernels, input_rows(): pl.pallas_call(input_kernel, grid_spec=pltpu.PrefetchScalarGridSpec(num_s...  20.1 us
    ppermute x1, waiting for transfers between devices, per_device(): other_side = lax.ppermute(for_side, 'dp', to_side)  8.71 us
    ppermute x3, waiting for transfers between devices, per_device(): lax.ppermute(theirs_high, 'dp', to_side).astype(F32)  8.38 us
    all_to_all x1, waiting for transfers between devices, per_device(): lax.all_to_all(paired, PLANE[:3], split_axis=0, concat_axis=0, tiled=True)  8.09 us
  transfers between devices with their start and end apart: 14, of which 9 were waited for; matrix products, arithmetic and copies ran while one was open for 5% of the time, Pallas kernels for 41%

profile of v2, /device:TPU:2, one launch (start us, length us, event | category | flops | bytes accessed | tf_op | source)
XLA Modules:
  0.0 274.1 jit_solution(13199190725122304508)
XLA Ops:
  11.1 1.1 constant_dynamic-slice_fusion
  12.3 1.7 collective-permute-start
  14.0 2.3 collective-permute-start.1
  16.2 4.2 %collective-permute-done = bf16[32,4096]{1,0:T(8,128)(2,1)S(1)} collective-permute-done((bf16[32,4096]{1,0:T(8,128)(2,1)S(1)}, bf16[32,4096]{1,0:T(8,128)(2,1)S(1)}, u32[]{:S(2)}, u32[]{:S(2)}) %collective-permute-start) | collective-permute-done | bytes 262176 | tf_op jit(solution)/shard_map/ppermute | solution.py:279
  20.4 2.6 collective-permute-done.1
  23.8 63.0 %all-gather.3.cloned.1.call-done.gathered_ref.tokens_ref.grads_ref = bf16[1024,8320]{1,0:T(8,128)(2,1)} async-done(((bf16[32,8320]{1,0:T(8,128)(2,1)}), bf16[1024,8320]{1,0:T(8,128)(2,1)}) %all-gather.3.cloned.1.call-update) | async-done | bytes 17039376 | tf_op jit(solution)/shard_map/all_gather | solution.py:278
  87.4 35.2 %hidden_rows.1 = (bf16[3,4,192,1024]{3,2,1,0:T(8,128)(2,1)}, bf16[3,2,192,1024]{3,2,1,0:T(8,128)(2,1)}, bf16[3,2,192,1024]{3,2,1,0:T(8,128)(2,1)}) custom-call(s32[5]{0:T(128)} %stack.30.route_ref, bf16[1024,8320]{1,0:T(8,128)(2,1)} %all-gather.3.cloned.1.call-done.gathered_ref.tokens_ref.grads_ref, bf16[4,192,4096]{2,1,0:T(8,128)(2,1)} %bitcast.25, ...), custom_call_target="tpu_custom_call" | custom-call | tf_op jit(solution)/shard_map/hidden_rows/pallas_call | solution.py:102
  122.6 1.6 collective-permute-start.2
  124.2 2.1 collective-permute-start.3
  126.9 20.5 %own_grads.1 = (f32[2,384,2048]{2,1,0:T(8,128)}, f32[2,384,2048]{2,1,0:T(8,128)}, f32[2,384,2048]{2,1,0:T(8,128)}) custom-call(s32[4]{0:T(128)} %pad_add_fusion.pick_ref, bf16[3,4,192,1024]{3,2,1,0:T(8,128)(2,1)} %get-tuple-element.38.first_ref.second_ref, bf16[3,4,192,1024]{3,2,1,0:T(8,128)(2,1)} %get-tuple-element.38.first_ref.second_ref, ...), custom_call_target="tpu_custom_call" | custom-call | tf_op jit(solution)/shard_map/own_grads/pallas_call | solution.py:198
  147.5 20.1 %input_rows.1 = (bf16[16,32,4096]{2,1,0:T(8,128)(2,1)}, bf16[16,32,4096]{2,1,0:T(8,128)(2,1)}) custom-call(s32[1]{0:T(128)} %bitcast.core_ref, bf16[3,768,1024]{2,1,0:T(8,128)(2,1)} %bitcast.24, bf16[768,4096]{1,0:T(8,128)(2,1)} %bitcast.26, bf16[768,4096]{1,0:T(8,128)(2,1)} %bitcast.28), custom_call_target="tpu_custom_call" | custom-call | tf_op jit(solution)/shard_map/input_rows/pallas_call | solution.py:159
  167.6 8.7 %collective-permute-done.2.other_ref = bf16[3,2,192,1024]{3,2,1,0:T(8,128)(2,1)S(1)} collective-permute-done((bf16[3,2,192,1024]{3,2,1,0:T(8,128)(2,1)}, bf16[3,2,192,1024]{3,2,1,0:T(8,128)(2,1)S(1)}, u32[]{:S(2)}, u32[]{:S(2)}) %collective-permute-start.2) | collective-permute-done | bytes 2359328 | tf_op jit(solution)/shard_map/ppermute | solution.py:294
  176.3 2.4 collective-permute-done.3.other_ref
  178.8 6.8 %weight_grads.10 = (bf16[192,2048]{1,0:T(8,128)(2,1)}, bf16[192,2048]{1,0:T(8,128)(2,1)}) custom-call(bf16[3,2,192,1024]{3,2,1,0:T(8,128)(2,1)} %copy-done.3, bf16[1024,8192]{1,0:T(8,128)(2,1)} %all-gather.5.cloned.1.call-done.near_ref, f32[2,384,2048]{2,1,0:T(8,128)} %get-tuple-element.61.own_ref), custom_call_target="tpu_custom_call" | custom-call | tf_op jit(solution)/shard_map/weight_grads/pallas_call | solution.py:235
  185.6 2.1 collective-permute-start.9
  187.7 6.3 %weight_grads.11 = (bf16[192,2048]{1,0:T(8,128)(2,1)}, bf16[192,2048]{1,0:T(8,128)(2,1)}) custom-call(bf16[3,2,192,1024]{3,2,1,0:T(8,128)(2,1)} %copy-done.2, bf16[1024,8192]{1,0:T(8,128)(2,1)} %all-gather.5.cloned.1.call-done.near_ref, f32[2,384,2048]{2,1,0:T(8,128)} %get-tuple-element.61.own_ref), custom_call_target="tpu_custom_call" | custom-call | tf_op jit(solution)/shard_map/weight_grads/pallas_call | solution.py:235
  194.0 6.0 %add_convert_fusion = bf16[16,32,4096]{2,1,0:T(8,128)(2,1)} fusion(bf16[16,32,4096]{2,1,0:T(8,128)(2,1)} %collective-permute-done.4, bf16[16,32,4096]{2,1,0:T(8,128)(2,1)S(1)} %copy-done.4), kind=kLoop, calls=%fused_computation | loop fusion | flops 8388608 | bytes 12582912 | tf_op jit(solution)/shard_map/convert_element_type | solution.py:306
  200.0 5.5 %all-to-all-start = ((bf16[16,32,4096]{2,1,0:T(8,128)(2,1)}), bf16[16,32,4096]{2,1,0:T(8,128)(2,1)}, u32[]{:S(2)}, u32[]{:S(2)}) async-start(bf16[16,32,4096]{2,1,0:T(8,128)(2,1)} %add_convert_fusion), calls=%async_computation | async-start | bytes 8388608 | tf_op jit(solution)/shard_map/all_to_all | solution.py:307
  205.5 6.3 %weight_grads.8 = (bf16[192,2048]{1,0:T(8,128)(2,1)}, bf16[192,2048]{1,0:T(8,128)(2,1)}) custom-call(bf16[3,2,192,1024]{3,2,1,0:T(8,128)(2,1)} %copy-done.3, bf16[1024,8192]{1,0:T(8,128)(2,1)} %all-gather.5.cloned.1.call-done.near_ref, f32[2,384,2048]{2,1,0:T(8,128)} %get-tuple-element.56.own_ref), custom_call_target="tpu_custom_call" | custom-call | tf_op jit(solution)/shard_map/weight_grads/pallas_call | solution.py:235
  212.9 5.9 %weight_grads.9 = (bf16[192,2048]{1,0:T(8,128)(2,1)}, bf16[192,2048]{1,0:T(8,128)(2,1)}) custom-call(bf16[3,2,192,1024]{3,2,1,0:T(8,128)(2,1)} %copy-done.2, bf16[1024,8192]{1,0:T(8,128)(2,1)} %all-gather.5.cloned.1.call-done.near_ref, f32[2,384,2048]{2,1,0:T(8,128)} %get-tuple-element.56.own_ref), custom_call_target="tpu_custom_call" | custom-call | tf_op jit(solution)/shard_map/weight_grads/pallas_call | solution.py:235
  218.8 1.4 collective-permute-start.8
  220.3 6.0 %weight_grads.6 = (bf16[192,2048]{1,0:T(8,128)(2,1)}, bf16[192,2048]{1,0:T(8,128)(2,1)}) custom-call(bf16[3,2,192,1024]{3,2,1,0:T(8,128)(2,1)} %copy-done.3, bf16[1024,8192]{1,0:T(8,128)(2,1)} %all-gather.5.cloned.1.call-done.near_ref, f32[2,384,2048]{2,1,0:T(8,128)} %get-tuple-element.50.own_ref), custom_call_target="tpu_custom_call" | custom-call | tf_op jit(solution)/shard_map/weight_grads/pallas_call | solution.py:235
  226.2 2.1 collective-permute-start.5
  228.3 6.0 %weight_grads.7 = (bf16[192,2048]{1,0:T(8,128)(2,1)}, bf16[192,2048]{1,0:T(8,128)(2,1)}) custom-call(bf16[3,2,192,1024]{3,2,1,0:T(8,128)(2,1)} %copy-done.2, bf16[1024,8192]{1,0:T(8,128)(2,1)} %all-gather.5.cloned.1.call-done.near_ref, f32[2,384,2048]{2,1,0:T(8,128)} %get-tuple-element.50.own_ref), custom_call_target="tpu_custom_call" | custom-call | tf_op jit(solution)/shard_map/weight_grads/pallas_call | solution.py:235
  236.0 3.1 %collective-permute-done.8 = bf16[192,2048]{1,0:T(8,128)(2,1)S(1)} collective-permute-done((bf16[192,2048]{1,0:T(8,128)(2,1)}, bf16[192,2048]{1,0:T(8,128)(2,1)S(1)}, u32[]{:S(2)}, u32[]{:S(2)}) %collective-permute-start.8) | collective-permute-done | bytes 786464 | tf_op jit(solution)/shard_map/ppermute | solution.py:318
  239.4 1.3 pad_maximum_fusion.2
  240.7 1.3 pad_maximum_fusion.1
  242.0 6.4 %collective-permute-done.5 = bf16[192,2048]{1,0:T(8,128)(2,1)S(1)} collective-permute-done((bf16[192,2048]{1,0:T(8,128)(2,1)}, bf16[192,2048]{1,0:T(8,128)(2,1)S(1)}, u32[]{:S(2)}, u32[]{:S(2)}) %collective-permute-start.5) | collective-permute-done | bytes 786464 | tf_op jit(solution)/shard_map/ppermute | solution.py:317
  248.6 5.3 %collective-permute-done.6 = bf16[192,2048]{1,0:T(8,128)(2,1)S(1)} collective-permute-done((bf16[192,2048]{1,0:T(8,128)(2,1)}, bf16[192,2048]{1,0:T(8,128)(2,1)S(1)}, u32[]{:S(2)}, u32[]{:S(2)}) %collective-permute-start.6) | collective-permute-done | bytes 786464 | tf_op jit(solution)/shard_map/ppermute | solution.py:318
  254.2 1.3 pad_maximum_fusion
  255.4 8.1 %all-to-all-done = bf16[16,32,4096]{2,1,0:T(8,128)(2,1)} async-done(((bf16[16,32,4096]{2,1,0:T(8,128)(2,1)}), bf16[16,32,4096]{2,1,0:T(8,128)(2,1)}, u32[]{:S(2)}, u32[]{:S(2)}) %all-to-all-start) | async-done | bytes 4194336 | tf_op jit(solution)/shard_map/all_to_all | solution.py:307
  263.5 3.7 %reduce_sum.22 = bf16[32,4096]{1,0:T(8,128)(2,1)} reduce(bf16[16,32,4096]{2,1,0:T(8,128)(2,1)} %all-to-all-done, bf16[]{:T(256)} %constant.38.clone.1), dimensions={0}, to_apply=%region_1.2 | reduce | flops 1966080 | bytes 4456450 | tf_op jit(solution)/shard_map/reduce_sum | solution.py:321
  (55 shorter events, 9.6 us)
Async XLA Ops:
  7.2 0.7 copy-start
  7.2 79.6 %all-gather.3.cloned.1.call-start = ((), (), s32[]{:S(2)}) async-start(), calls=%async_computation.1 | async-start | bytes 17571840 | tf_op jit(solution)/shard_map/all_gather | solution.py:278
  11.1 167.7 %all-gather.5.cloned.1.call-start = ((), (), s32[]{:S(2)}) async-start(), calls=%async_computation.2 | async-start | bytes 17301504 | tf_op jit(solution)/shard_map/all_gather | solution.py:287
  12.3 8.1 %collective-permute-start = (bf16[32,4096]{1,0:T(8,128)(2,1)S(1)}, bf16[32,4096]{1,0:T(8,128)(2,1)S(1)}, u32[]{:S(2)}, u32[]{:S(2)}) collective-permute-start(bf16[32,4096]{1,0:T(8,128)(2,1)S(1)} %pad_maximum_fusion.4), channel_id=1, source_target_pairs={{0,32},{32,0},{64,96},{96,64},{1,33},{33,1},{65,97},{97,65},{2,34}... | collective-permute-start | bytes 786440 | tf_op jit(solution)/shard_map/ppermute | solution.py:279
  14.0 9.1 %collective-permute-start.1 = (bf16[32,4096]{1,0:T(8,128)(2,1)S(1)}, bf16[32,4096]{1,0:T(8,128)(2,1)S(1)}, u32[]{:S(2)}, u32[]{:S(2)}) collective-permute-start(bf16[32,4096]{1,0:T(8,128)(2,1)S(1)} %pad_maximum_fusion.5), channel_id=1, source_target_pairs={{0,96},{32,64},{64,32},{96,0},{1,97},{33,65},{65,33},{97,1},{2,98}... | collective-permute-start | bytes 786440 | tf_op jit(solution)/shard_map/ppermute | solution.py:282
  122.6 53.7 %collective-permute-start.2 = (bf16[3,2,192,1024]{3,2,1,0:T(8,128)(2,1)}, bf16[3,2,192,1024]{3,2,1,0:T(8,128)(2,1)S(1)}, u32[]{:S(2)}, u32[]{:S(2)}) collective-permute-start(bf16[3,2,192,1024]{3,2,1,0:T(8,128)(2,1)} %get-tuple-element.44), channel_id=1, source_target_pairs={{0,32},{32,0},{64,96},{96,64},{1,33},{33,1},{65,97},{97,65},{2,34}... | collective-permute-start | bytes 7077896 | tf_op jit(solution)/shard_map/ppermute | solution.py:294
  124.2 54.6 %collective-permute-start.3 = (bf16[3,2,192,1024]{3,2,1,0:T(8,128)(2,1)}, bf16[3,2,192,1024]{3,2,1,0:T(8,128)(2,1)S(1)}, u32[]{:S(2)}, u32[]{:S(2)}) collective-permute-start(bf16[3,2,192,1024]{3,2,1,0:T(8,128)(2,1)} %get-tuple-element.45), channel_id=1, source_target_pairs={{0,96},{32,64},{64,32},{96,0},{1,97},{33,65},{65,33},{97,1},{2,98}... | collective-permute-start | bytes 7077896 | tf_op jit(solution)/shard_map/ppermute | solution.py:295
  176.3 2.4 copy-start.3
  178.8 6.8 %copy-start.2 = (bf16[3,2,192,1024]{3,2,1,0:T(8,128)(2,1)}, bf16[3,2,192,1024]{3,2,1,0:T(8,128)(2,1)S(1)}, u32[]{:S(2)}) copy-start(bf16[3,2,192,1024]{3,2,1,0:T(8,128)(2,1)S(1)} %collective-permute-done.3.other_ref) | copy-start | bytes 7077892
  178.8 15.3 %collective-permute-start.4 = (bf16[16,32,4096]{2,1,0:T(8,128)(2,1)}, bf16[16,32,4096]{2,1,0:T(8,128)(2,1)}, u32[]{:S(2)}, u32[]{:S(2)}) collective-permute-start(bf16[16,32,4096]{2,1,0:T(8,128)(2,1)} %get-tuple-element.47), channel_id=1, source_target_pairs={{0,1},{1,0},{2,3},{3,2},{4,5},{5,4},{6,7},{7,6},{8,9},{9,8},{10,11... | collective-permute-start | bytes 12582920 | tf_op jit(solution)/shard_map/ppermute | solution.py:305
  185.6 48.7 %collective-permute-start.9 = (bf16[192,2048]{1,0:T(8,128)(2,1)}, bf16[192,2048]{1,0:T(8,128)(2,1)S(1)}, u32[]{:S(2)}, u32[]{:S(2)}) collective-permute-start(bf16[192,2048]{1,0:T(8,128)(2,1)} %get-tuple-element.63), channel_id=1, source_target_pairs={{0,96},{32,64},{64,32},{96,0},{1,97},{33,65},{65,33},{97,1},{2,98}... | collective-permute-start | bytes 2359304 | tf_op jit(solution)/shard_map/ppermute | solution.py:317
  187.7 6.3 %copy-start.4 = (bf16[16,32,4096]{2,1,0:T(8,128)(2,1)S(1)}, bf16[16,32,4096]{2,1,0:T(8,128)(2,1)}, u32[]{:S(2)}) copy-start(bf16[16,32,4096]{2,1,0:T(8,128)(2,1)} %get-tuple-element.46) | copy-start | bytes 12582916
  194.0 40.7 %collective-permute-start.10 = (bf16[192,2048]{1,0:T(8,128)(2,1)}, bf16[192,2048]{1,0:T(8,128)(2,1)S(1)}, u32[]{:S(2)}, u32[]{:S(2)}) collective-permute-start(bf16[192,2048]{1,0:T(8,128)(2,1)} %get-tuple-element.65), channel_id=1, source_target_pairs={{0,32},{32,0},{64,96},{96,64},{1,33},{33,1},{65,97},{97,65},{2,34}... | collective-permute-start | bytes 2359304 | tf_op jit(solution)/shard_map/ppermute | solution.py:318
  200.0 63.5 %all-to-all-start = ((bf16[16,32,4096]{2,1,0:T(8,128)(2,1)}), bf16[16,32,4096]{2,1,0:T(8,128)(2,1)}, u32[]{:S(2)}, u32[]{:S(2)}) async-start(bf16[16,32,4096]{2,1,0:T(8,128)(2,1)} %add_convert_fusion), calls=%async_computation | async-start | bytes 8388608 | tf_op jit(solution)/shard_map/all_to_all | solution.py:307
  211.8 23.9 %collective-permute-start.7 = (bf16[192,2048]{1,0:T(8,128)(2,1)}, bf16[192,2048]{1,0:T(8,128)(2,1)S(1)}, u32[]{:S(2)}, u32[]{:S(2)}) collective-permute-start(bf16[192,2048]{1,0:T(8,128)(2,1)} %get-tuple-element.58), channel_id=1, source_target_pairs={{0,96},{32,64},{64,32},{96,0},{1,97},{33,65},{65,33},{97,1},{2,98}... | collective-permute-start | bytes 2359304 | tf_op jit(solution)/shard_map/ppermute | solution.py:317
  218.8 20.3 %collective-permute-start.8 = (bf16[192,2048]{1,0:T(8,128)(2,1)}, bf16[192,2048]{1,0:T(8,128)(2,1)S(1)}, u32[]{:S(2)}, u32[]{:S(2)}) collective-permute-start(bf16[192,2048]{1,0:T(8,128)(2,1)} %get-tuple-element.60), channel_id=1, source_target_pairs={{0,32},{32,0},{64,96},{96,64},{1,33},{33,1},{65,97},{97,65},{2,34}... | collective-permute-start | bytes 2359304 | tf_op jit(solution)/shard_map/ppermute | solution.py:318
  226.2 8.2 %copy-start.6 = (bf16[192,2048]{1,0:T(8,128)(2,1)S(1)}, bf16[192,2048]{1,0:T(8,128)(2,1)}, u32[]{:S(2)}) copy-start(bf16[192,2048]{1,0:T(8,128)(2,1)} %get-tuple-element.62) | copy-start | bytes 2359300
  226.2 22.1 %collective-permute-start.5 = (bf16[192,2048]{1,0:T(8,128)(2,1)}, bf16[192,2048]{1,0:T(8,128)(2,1)S(1)}, u32[]{:S(2)}, u32[]{:S(2)}) collective-permute-start(bf16[192,2048]{1,0:T(8,128)(2,1)} %get-tuple-element.52), channel_id=1, source_target_pairs={{0,96},{32,64},{64,32},{96,0},{1,97},{33,65},{65,33},{97,1},{2,98}... | collective-permute-start | bytes 2359304 | tf_op jit(solution)/shard_map/ppermute | solution.py:317
  234.3 1.1 copy-start.5
  234.3 19.6 %collective-permute-start.6 = (bf16[192,2048]{1,0:T(8,128)(2,1)}, bf16[192,2048]{1,0:T(8,128)(2,1)S(1)}, u32[]{:S(2)}, u32[]{:S(2)}) collective-permute-start(bf16[192,2048]{1,0:T(8,128)(2,1)} %get-tuple-element.55), channel_id=1, source_target_pairs={{0,32},{32,0},{64,96},{96,64},{1,33},{33,1},{65,97},{97,65},{2,34}... | collective-permute-start | bytes 2359304 | tf_op jit(solution)/shard_map/ppermute | solution.py:318
  234.4 1.3 copy-start.10
  235.4 3.7 %copy-start.9 = (bf16[192,2048]{1,0:T(8,128)(2,1)S(1)}, bf16[192,2048]{1,0:T(8,128)(2,1)}, u32[]{:S(2)}) copy-start(bf16[192,2048]{1,0:T(8,128)(2,1)} %get-tuple-element.59) | copy-start | bytes 2359300
  240.7 7.6 %copy-start.7 = (bf16[192,2048]{1,0:T(8,128)(2,1)S(1)}, bf16[192,2048]{1,0:T(8,128)(2,1)}, u32[]{:S(2)}) copy-start(bf16[192,2048]{1,0:T(8,128)(2,1)} %get-tuple-element.51) | copy-start | bytes 2359300
  240.7 13.2 %copy-start.8 = (bf16[192,2048]{1,0:T(8,128)(2,1)S(1)}, bf16[192,2048]{1,0:T(8,128)(2,1)}, u32[]{:S(2)}) copy-start(bf16[192,2048]{1,0:T(8,128)(2,1)} %get-tuple-element.54) | copy-start | bytes 2359300
  254.2 13.1 %copy-start.1 = (s32[128,8]{0,1:T(8,128)S(1)}, s32[128,8]{0,1:T(8,128)}, u32[]{:S(2)}) copy-start(s32[128,8]{0,1:T(8,128)} %param.9) | copy-start | bytes 12292
Sparse Core Ops, SparseCore 0:
  11.2 75.5 all-gather.2
  89.6 71.9 all-gather.4

commit v3 on v2

--- a/solution.py
+++ b/solution.py
@@ -13,14 +13,15 @@
 VMEM_LIMIT = 56 * 1024 * 1024
 PLANE = ("z", "xh", "xl", "core")
 LANES = 128
+GIVEN = 4
 SMALL = pl.CostEstimate(flops=0, bytes_accessed=0, transcendentals=0)
 
 
 def hidden_kernel(
     start, route_ref, gathered_ref, gate_ref, up_ref, down_ref, out_ref, near_ref, far_ref,
-    held, gate, up, down, token_sems, weight_sems,
+    held, gate, up, down, stage, token_sems, weight_sems, out_sems,
 ):
-    rows = out_ref.shape[3]
+    rows = stage.shape[2]
     owners, share, width = gate_ref.shape
     block = 256
     weights = ((gate_ref, gate), (up_ref, up), (down_ref, down))
@@ -49,8 +50,19 @@
         for which in range(3):
             weight_copy(which, place).start()
 
+    def flush(place):
+        source = stage.at[:, pl.ds(place * share, share)]
+        targets = [out_ref.at[:, route_ref[place]]]
+        if place < 2:
+            targets.append(near_ref.at[:, place])
+        if 0 < place < 3:
+            targets.append(far_ref.at[:, place - 1])
+        return [
+            pltpu.make_async_copy(source, target, out_sems.at[place, index])
+            for index, target in enumerate(targets)
+        ]
+
     by_features = (((1,), (1,)), ((), ()))
-    pieces = ([], [], [])
     for third in range(3):
         span = pl.ds(third * block, block)
 
@@ -83,36 +95,38 @@
         sigmoid = jax.nn.sigmoid(gate_pre)
         active = gate_pre * sigmoid
         slope = sigmoid * (1.0 + gate_pre * (1.0 - sigmoid))
-        pieces[0].append((hidden_grad * up_pre * slope).astype(BF16))
-        pieces[1].append((hidden_grad * active).astype(BF16))
-        pieces[2].append((prob * active * up_pre).astype(BF16))
-    for which in range(3):
-        result = jnp.concatenate(pieces[which], axis=0).reshape(owners, share, rows)
+        stage[0, span] = (hidden_grad * up_pre * slope).astype(BF16)
+        stage[1, span] = (hidden_grad * active).astype(BF16)
+        stage[2, span] = (prob * active * up_pre).astype(BF16)
         for place in range(owners):
-            out_ref[which, route_ref[place]] = result[place]
-        near_ref[which] = result[0:2]
-        far_ref[which] = result[1:3]
+            if third * block < (place + 1) * share <= (third + 1) * block:
+                for copy in flush(place):
+                    copy.start()
+    for place in range(owners):
+        for copy in flush(place):
+            copy.wait()
 
 
 def hidden_rows(gathered, start, rows, route, w_gate, w_up, w_down):
     owners, share, width = w_gate.shape
     whole = pl.BlockSpec(memory_space=pl.ANY)
     kept = pltpu.VMEM((owners * share, width), BF16)
-    pair = pl.BlockSpec((3, 2, share, rows), lambda t, r: (0, 0, 0, 0))
     return pl.pallas_call(
         functools.partial(hidden_kernel, start),
         grid_spec=pltpu.PrefetchScalarGridSpec(
             num_scalar_prefetch=1,
             grid=(1,),
             in_specs=[whole, whole, whole, whole],
-            out_specs=[pl.BlockSpec((3, owners, share, rows), lambda t, r: (0, 0, 0, 0)), pair, pair],
+            out_specs=[whole, whole, whole],
             scratch_shapes=[
                 pltpu.VMEM((rows, gathered.shape[1]), BF16),
                 kept,
                 kept,
                 kept,
+                pltpu.VMEM((3, owners * share, rows), BF16),
                 pltpu.SemaphoreType.DMA((2,)),
                 pltpu.SemaphoreType.DMA((3, owners)),
+                pltpu.SemaphoreType.DMA((owners, 3)),
             ],
         ),
         out_shape=[
@@ -126,7 +140,10 @@
     )(route, gathered, w_gate, w_up, w_down)
 
 
-def input_kernel(core_ref, hidden_ref, gate_ref, up_ref, kept_ref, given_ref, turned):
+def input_kernel(core_ref, hidden_ref, gate_ref, up_ref, kept_ref, *rest):
+    given_refs, turned = rest[:-1], rest[-1]
+    count = pl.num_programs(0) // len(given_refs)
+
     @pl.when(pl.program_id(0) == 0)
     def _():
         turned[0] = hidden_ref[0].T
@@ -137,15 +154,13 @@
     groups, share, step = kept_ref.shape
     total = total.astype(BF16).reshape(groups, 2, share, step)
 
-    @pl.when(core_ref[0] == 0)
-    def _():
-        kept_ref[...] = total[:, 0]
-        given_ref[...] = total[:, 1]
-
-    @pl.when(core_ref[0] != 0)
-    def _():
-        kept_ref[...] = total[:, 1]
-        given_ref[...] = total[:, 0]
+    mine = core_ref[0] == 0
+    kept_ref[...] = jnp.where(mine, total[:, 0], total[:, 1])
+    for index, given_ref in enumerate(given_refs):
+
+        @pl.when(pl.program_id(0) // count == index)
+        def _():
+            given_ref[...] = jnp.where(mine, total[:, 1], total[:, 0])
 
 
 def input_rows(hidden, core, w_gate, w_up, share):
@@ -156,20 +171,54 @@
     weight = pl.BlockSpec((units, step), lambda i, c: (0, i))
     part = pl.BlockSpec((groups, share, step), lambda i, c: (0, 0, i))
     shape = jax.ShapeDtypeStruct((groups, share, width), BF16)
+    given_shape = jax.ShapeDtypeStruct((groups, share, width // GIVEN), BF16)
+    count = width // step // GIVEN
+
+    def given_part(index):
+        return pl.BlockSpec(
+            (groups, share, step),
+            lambda i, c: (0, 0, jnp.clip(i - index * count, 0, count - 1)),
+        )
+
     return pl.pallas_call(
         input_kernel,
         grid_spec=pltpu.PrefetchScalarGridSpec(
             num_scalar_prefetch=1,
             grid=(width // step,),
             in_specs=[pl.BlockSpec((2, units, token_count), lambda i, c: (0, 0, 0)), weight, weight],
-            out_specs=[part, part],
+            out_specs=[part] + [given_part(index) for index in range(GIVEN)],
             scratch_shapes=[pltpu.VMEM((2, token_count, units), BF16)],
         ),
-        out_shape=[shape, shape],
+        out_shape=[shape] + [given_shape] * GIVEN,
         compiler_params=pltpu.CompilerParams(vmem_limit_bytes=VMEM_LIMIT),
         cost_estimate=SMALL,
         name="input_rows",
     )(core, hidden, w_gate, w_up)
+
+
+def pair_kernel(kept_ref, *refs):
+    parts, out_ref = refs[:-1], refs[-1]
+    step = parts[0].shape[2]
+    for index, part in enumerate(parts):
+        span = slice(index * step, (index + 1) * step)
+        out_ref[:, :, span] = (kept_ref[:, :, span].astype(F32) + part[...].astype(F32)).astype(BF16)
+
+
+def pair_sum(kept, parts):
+    groups, share, width = kept.shape
+    count = 4
+    whole = pl.BlockSpec((groups // count, share, width), lambda i: (i, 0, 0))
+    part = pl.BlockSpec((groups // count, share, width // len(parts)), lambda i: (i, 0, 0))
+    return pl.pallas_call(
+        pair_kernel,
+        grid=(count,),
+        in_specs=[whole] + [part] * len(parts),
+        out_specs=whole,
+        out_shape=jax.ShapeDtypeStruct(kept.shape, BF16),
+        compiler_params=pltpu.CompilerParams(vmem_limit_bytes=VMEM_LIMIT),
+        cost_estimate=SMALL,
+        name="pair_sum",
+    )(kept, *parts)
 
 
 def own_kernel(
@@ -294,16 +343,16 @@
     other_side = lax.ppermute(for_side, "dp", to_side)
     other_mirror = lax.ppermute(for_mirror, "dp", to_mirror)
 
-    kept, given = input_rows(
+    kept, *given = input_rows(
         hidden.reshape(3, units, -1), core[None], w_gate[0], w_up[0], share
     )
     picks = jnp.stack([place, mirror, side, place]).astype(jnp.int32)
     own = own_grads(picks, hidden, gathered, width)
-    kept, given, own, other_side, other_mirror = lax.optimization_barrier(
-        (kept, given, own, other_side, other_mirror)
-    )
-    taken = lax.ppermute(given, "core", [(0, 1), (1, 0)])
-    paired = (kept.astype(F32) + taken.astype(F32)).astype(BF16)
+    taken = [lax.ppermute(part, "core", [(0, 1), (1, 0)]) for part in given]
+    paired = pair_sum(kept, taken)
+    paired, own, other_side, other_mirror = lax.optimization_barrier(
+        (paired, own, other_side, other_mirror)
+    )
     returned = lax.all_to_all(paired, PLANE[:3], split_axis=0, concat_axis=0, tiled=True)
 
     mine, theirs = [], []
@@ -312,12 +361,16 @@
         theirs_high, mine_high = weight_grads(which, 1, other_mirror, gathered_near, own[which])
         mine.append((mine_low, mine_high))
         theirs.append((theirs_low, theirs_high))
+    received = [
+        (lax.ppermute(low, "dp", to_mirror), lax.ppermute(high, "dp", to_side)) for low, high in theirs
+    ]
     results = []
-    for (mine_low, mine_high), (theirs_low, theirs_high) in zip(mine, theirs):
-        low = mine_low.astype(F32) + lax.ppermute(theirs_low, "dp", to_mirror).astype(F32)
-        high = mine_high.astype(F32) + lax.ppermute(theirs_high, "dp", to_side).astype(F32)
+    for (mine_low, mine_high), (low, high) in zip(mine, received):
+        if len(results) == 2:
+            returned, low, high, results = lax.optimization_barrier((returned, low, high, results))
+        low = mine_low.astype(F32) + low.astype(F32)
+        high = mine_high.astype(F32) + high.astype(F32)
         results.append(jnp.concatenate([low, high], axis=1).astype(BF16)[None])
-    returned, results = lax.optimization_barrier((returned, results))
     in_grad = jnp.sum(returned.astype(F32), axis=0).astype(BF16)
     return (in_grad, results[1], results[2], results[0])
 

time: 278 us -> 263 us (0.946); the launches traced: 274 us -> 262 us
  waiting for transfers between devices: 104 us -> 92 us
  other arithmetic: 16.8 us -> 10.8 us
    ppermute x1, waiting for transfers between devices: 8.71 us -> 0.01 us  [per_device(): other_side = lax.ppermute(for_side, 'dp', to_side)]
    convert_element_type x1 -> x0, other arithmetic: 5.96 us -> none  [per_device(): paired = (kept.astype(F32) + taken.astype(F32)).astype(BF16)]
    pallas_call x0 -> x1, Pallas kernels: none -> 5.93 us  [pair_sum(): pl.pallas_call(pair_kernel, grid=(count,), in_specs=[whole] + [part] * le...]
    ppermute x7 -> x10, starting transfers between devices: 6.87 us -> 7.58 us  [the longest x3 4.26 us: per_device(): lax.ppermute(low, 'dp', to_mirror)]
    ppermute x7 -> x10, waiting for transfers between devices: 14.7 us -> 14.3 us  [the longest x3 12 us: per_device(): lax.ppermute(high, 'dp', to_side)]
  transfers between devices with their start and end apart: 14 -> 17, of which waited for: 9 -> 8; matrix products, arithmetic and copies ran while one was open for 5% -> 3% of each run, Pallas kernels for 41% -> 44%
where the time goes in v3:
time: 263 us; the launch traced here: 262 us
  Pallas kernels  115 us (44%)
  waiting for transfers between devices  92 us (35%)
  starting transfers between devices  21.9 us (8%)
  between operations  14.3 us (5%)
  other arithmetic  10.8 us (4%)
  local copies, waits for them, and re-layouts  8.76 us (3%)
    all_gather x1, waiting for transfers between devices, per_device(): gathered = lax.all_gather(payload, PLANE, axis=0, tiled=True)  63 us
    pallas_call x6, Pallas kernels, weight_grads(): pl.pallas_call(weight_kernel, grid=(count,), in_specs=[pl.BlockSpec((1, 2...  36.1 us
    pallas_call x1, Pallas kernels, hidden_rows(): pl.pallas_call(functools.partial(hidden_kernel, start), grid_spec=pltpu.P...  32.9 us
    pallas_call x1, Pallas kernels, input_rows(): pl.pallas_call(input_kernel, grid_spec=pltpu.PrefetchScalarGridSpec(num_s...  20.3 us
    pallas_call x1, Pallas kernels, own_grads(): pl.pallas_call(own_kernel, grid_spec=pltpu.PrefetchScalarGridSpec(num_sca...  19.3 us
    ppermute x3, waiting for transfers between devices, per_device(): lax.ppermute(high, 'dp', to_side)  12 us
    all_to_all x1, starting transfers between devices, per_device(): lax.all_to_all(paired, PLANE[:3], split_axis=0, concat_axis=0, tiled=True)  6.7 us
    all_to_all x1, waiting for transfers between devices, per_device(): lax.all_to_all(paired, PLANE[:3], split_axis=0, concat_axis=0, tiled=True)  6.28 us
  transfers between devices with their start and end apart: 17, of which 8 were waited for; matrix products, arithmetic and copies ran while one was open for 3% of the time, Pallas kernels for 44%

profile of v3, /device:TPU:2, one launch (start us, length us, event | category | flops | bytes accessed | tf_op | source)
XLA Modules:
  0.0 262.3 jit_solution(3071565667237414937)
XLA Ops:
  9.0 1.1 constant_dynamic-slice_fusion.4
  11.1 1.1 constant_dynamic-slice_fusion
  12.3 1.7 collective-permute-start
  14.0 2.3 collective-permute-start.1
  16.2 4.2 %collective-permute-done = bf16[32,4096]{1,0:T(8,128)(2,1)S(1)} collective-permute-done((bf16[32,4096]{1,0:T(8,128)(2,1)S(1)}, bf16[32,4096]{1,0:T(8,128)(2,1)S(1)}, u32[]{:S(2)}, u32[]{:S(2)}) %collective-permute-start) | collective-permute-done | bytes 262176 | tf_op jit(solution)/shard_map/ppermute | solution.py:328
  20.4 2.6 collective-permute-done.1
  23.8 63.0 %all-gather.3.cloned.1.call-done.gathered_ref.tokens_ref.grads_ref = bf16[1024,8320]{1,0:T(8,128)(2,1)} async-done(((bf16[32,8320]{1,0:T(8,128)(2,1)}), bf16[1024,8320]{1,0:T(8,128)(2,1)}) %all-gather.3.cloned.1.call-update) | async-done | bytes 17039376 | tf_op jit(solution)/shard_map/all_gather | solution.py:327
  87.4 32.9 %hidden_rows.1 = (bf16[3,4,192,1024]{3,2,1,0:T(8,128)(2,1)}, bf16[3,2,192,1024]{3,2,1,0:T(8,128)(2,1)}, bf16[3,2,192,1024]{3,2,1,0:T(8,128)(2,1)}) custom-call(s32[5]{0:T(128)} %stack.30.route_ref, bf16[1024,8320]{1,0:T(8,128)(2,1)} %all-gather.3.cloned.1.call-done.gathered_ref.tokens_ref.grads_ref, bf16[4,192,4096]{2,1,0:T(8,128)(2,1)} %bitcast.25, ...), custom_call_target="tpu_custom_call" | custom-call | tf_op jit(solution)/shard_map/hidden_rows/pallas_call | solution.py:114
  120.4 1.6 collective-permute-start.6
  121.9 2.1 collective-permute-start.7
  124.0 20.3 %input_rows.1 = (bf16[16,32,4096]{2,1,0:T(8,128)(2,1)}, bf16[16,32,1024]{2,1,0:T(8,128)(2,1)}, bf16[16,32,1024]{2,1,0:T(8,128)(2,1)}, bf16[16,32,1024]{2,1,0:T(8,128)(2,1)}, bf16[16,32,1024]{2,1,0:T(8,128)(2,1)}) custom-call(s32[1]{0:T(128)} %bitcast.core_ref, bf16[3,768,1024]{2,1,0:T(8,128)(2,1)} %bitcast.24, bf16[768,4096]{1,0:T(8,128)(2,1)} %bitcast.26, ...), custom_call_target="tpu_custom_call" | custom-call | tf_op jit(solution)/shard_map/input_rows/pallas_call | solution.py:183
  144.9 2.3 collective-permute-done.2.refs_0_
  148.0 19.3 %own_grads.1 = (f32[2,384,2048]{2,1,0:T(8,128)}, f32[2,384,2048]{2,1,0:T(8,128)}, f32[2,384,2048]{2,1,0:T(8,128)}) custom-call(s32[4]{0:T(128)} %pad_add_fusion.pick_ref, bf16[3,4,192,1024]{3,2,1,0:T(8,128)(2,1)} %get-tuple-element.41.first_ref.second_ref, bf16[3,4,192,1024]{3,2,1,0:T(8,128)(2,1)} %get-tuple-element.41.first_ref.second_ref, ...), custom_call_target="tpu_custom_call" | custom-call | tf_op jit(solution)/shard_map/own_grads/pallas_call | solution.py:247
  169.0 5.9 %pair_sum.1 = bf16[16,32,4096]{2,1,0:T(8,128)(2,1)} custom-call(bf16[16,32,4096]{2,1,0:T(8,128)(2,1)} %get-tuple-element.42.kept_ref, bf16[16,32,1024]{2,1,0:T(8,128)(2,1)} %copy-done.3, bf16[16,32,1024]{2,1,0:T(8,128)(2,1)} %copy-done.4, bf16[16,32,1024]{2,1,0:T(8,128)(2,1)} %copy-done.5, bf16[16,32,1024]{2,1,0:T(8,128)(2,1)} %copy-done.6), custom_call_target="tpu_custom_call" | custom-call | tf_op jit(solution)/shard_map/pair_sum/pallas_call | solution.py:212
  175.0 1.6 collective-permute-done.7.other_ref
  176.6 6.7 %all-to-all-start = ((bf16[16,32,4096]{2,1,0:T(8,128)(2,1)}), bf16[16,32,4096]{2,1,0:T(8,128)(2,1)}, u32[]{:S(2)}, u32[]{:S(2)}) async-start(bf16[16,32,4096]{2,1,0:T(8,128)(2,1)} %pair_sum.1), calls=%async_computation | async-start | bytes 8388608 | tf_op jit(solution)/shard_map/all_to_all | solution.py:356
  183.3 6.3 %weight_grads.10 = (bf16[192,2048]{1,0:T(8,128)(2,1)}, bf16[192,2048]{1,0:T(8,128)(2,1)}) custom-call(bf16[3,2,192,1024]{3,2,1,0:T(8,128)(2,1)} %copy-done.2, bf16[1024,8192]{1,0:T(8,128)(2,1)} %all-gather.5.cloned.1.call-done.near_ref, f32[2,384,2048]{2,1,0:T(8,128)} %get-tuple-element.64.own_ref), custom_call_target="tpu_custom_call" | custom-call | tf_op jit(solution)/shard_map/weight_grads/pallas_call | solution.py:284
  189.6 0.9 collective-permute-start.12
  190.6 5.9 %weight_grads.11 = (bf16[192,2048]{1,0:T(8,128)(2,1)}, bf16[192,2048]{1,0:T(8,128)(2,1)}) custom-call(bf16[3,2,192,1024]{3,2,1,0:T(8,128)(2,1)} %collective-permute-done.7.other_ref, bf16[1024,8192]{1,0:T(8,128)(2,1)} %all-gather.5.cloned.1.call-done.near_ref, f32[2,384,2048]{2,1,0:T(8,128)} %get-tuple-element.64.own_ref), custom_call_target="tpu_custom_call" | custom-call | tf_op jit(solution)/shard_map/weight_grads/pallas_call | solution.py:284
  197.1 6.0 %weight_grads.8 = (bf16[192,2048]{1,0:T(8,128)(2,1)}, bf16[192,2048]{1,0:T(8,128)(2,1)}) custom-call(bf16[3,2,192,1024]{3,2,1,0:T(8,128)(2,1)} %copy-done.2, bf16[1024,8192]{1,0:T(8,128)(2,1)} %all-gather.5.cloned.1.call-done.near_ref, f32[2,384,2048]{2,1,0:T(8,128)} %get-tuple-element.59.own_ref), custom_call_target="tpu_custom_call" | custom-call | tf_op jit(solution)/shard_map/weight_grads/pallas_call | solution.py:284
  203.0 2.6 collective-permute-start.10
  205.6 6.0 %weight_grads.9 = (bf16[192,2048]{1,0:T(8,128)(2,1)}, bf16[192,2048]{1,0:T(8,128)(2,1)}) custom-call(bf16[3,2,192,1024]{3,2,1,0:T(8,128)(2,1)} %collective-permute-done.7.other_ref, bf16[1024,8192]{1,0:T(8,128)(2,1)} %all-gather.5.cloned.1.call-done.near_ref, f32[2,384,2048]{2,1,0:T(8,128)} %get-tuple-element.59.own_ref), custom_call_target="tpu_custom_call" | custom-call | tf_op jit(solution)/shard_map/weight_grads/pallas_call | solution.py:284
  212.2 5.9 %weight_grads.7 = (bf16[192,2048]{1,0:T(8,128)(2,1)}, bf16[192,2048]{1,0:T(8,128)(2,1)}) custom-call(bf16[3,2,192,1024]{3,2,1,0:T(8,128)(2,1)} %collective-permute-done.7.other_ref, bf16[1024,8192]{1,0:T(8,128)(2,1)} %all-gather.5.cloned.1.call-done.near_ref, f32[2,384,2048]{2,1,0:T(8,128)} %get-tuple-element.55.own_ref), custom_call_target="tpu_custom_call" | custom-call | tf_op jit(solution)/shard_map/weight_grads/pallas_call | solution.py:284
  218.1 1.5 collective-permute-start.9
  219.6 6.0 %weight_grads.6 = (bf16[192,2048]{1,0:T(8,128)(2,1)}, bf16[192,2048]{1,0:T(8,128)(2,1)}) custom-call(bf16[3,2,192,1024]{3,2,1,0:T(8,128)(2,1)} %copy-done.2, bf16[1024,8192]{1,0:T(8,128)(2,1)} %all-gather.5.cloned.1.call-done.near_ref, f32[2,384,2048]{2,1,0:T(8,128)} %get-tuple-element.55.own_ref), custom_call_target="tpu_custom_call" | custom-call | tf_op jit(solution)/shard_map/weight_grads/pallas_call | solution.py:284
  228.0 6.0 %collective-permute-done.11 = bf16[192,2048]{1,0:T(8,128)(2,1)S(1)} collective-permute-done((bf16[192,2048]{1,0:T(8,128)(2,1)}, bf16[192,2048]{1,0:T(8,128)(2,1)S(1)}, u32[]{:S(2)}, u32[]{:S(2)}) %collective-permute-start.11) | collective-permute-done | bytes 786464 | tf_op jit(solution)/shard_map/ppermute | solution.py:365
  234.3 1.3 pad_maximum_fusion.1
  235.6 1.3 pad_maximum_fusion
  236.8 6.3 %all-to-all-done = bf16[16,32,4096]{2,1,0:T(8,128)(2,1)} async-done(((bf16[16,32,4096]{2,1,0:T(8,128)(2,1)}), bf16[16,32,4096]{2,1,0:T(8,128)(2,1)}, u32[]{:S(2)}, u32[]{:S(2)}) %all-to-all-start) | async-done | bytes 4194336 | tf_op jit(solution)/shard_map/all_to_all | solution.py:356
  243.1 6.0 %collective-permute-done.9 = bf16[192,2048]{1,0:T(8,128)(2,1)S(1)} collective-permute-done((bf16[192,2048]{1,0:T(8,128)(2,1)}, bf16[192,2048]{1,0:T(8,128)(2,1)S(1)}, u32[]{:S(2)}, u32[]{:S(2)}) %collective-permute-start.9) | collective-permute-done | bytes 786464 | tf_op jit(solution)/shard_map/ppermute | solution.py:365
  249.1 3.7 %reduce_sum.22 = bf16[32,4096]{1,0:T(8,128)(2,1)} reduce(bf16[16,32,4096]{2,1,0:T(8,128)(2,1)} %all-to-all-done, bf16[]{:T(256)} %constant.38.clone.1), dimensions={0}, to_apply=%region_1.2 | reduce | flops 1966080 | bytes 4456450 | tf_op jit(solution)/shard_map/reduce_sum | solution.py:374
  254.2 1.3 pad_maximum_fusion.2
  (65 shorter events, 12.6 us)
Async XLA Ops:
  7.2 0.7 copy-start
  7.2 79.6 %all-gather.3.cloned.1.call-start = ((), (), s32[]{:S(2)}) async-start(), calls=%async_computation.1 | async-start | bytes 17571840 | tf_op jit(solution)/shard_map/all_gather | solution.py:327
  11.1 172.2 %all-gather.5.cloned.1.call-start = ((), (), s32[]{:S(2)}) async-start(), calls=%async_computation.2 | async-start | bytes 17301504 | tf_op jit(solution)/shard_map/all_gather | solution.py:336
  12.3 8.1 %collective-permute-start = (bf16[32,4096]{1,0:T(8,128)(2,1)S(1)}, bf16[32,4096]{1,0:T(8,128)(2,1)S(1)}, u32[]{:S(2)}, u32[]{:S(2)}) collective-permute-start(bf16[32,4096]{1,0:T(8,128)(2,1)S(1)} %pad_maximum_fusion.4), channel_id=1, source_target_pairs={{0,32},{32,0},{64,96},{96,64},{1,33},{33,1},{65,97},{97,65},{2,34}... | collective-permute-start | bytes 786440 | tf_op jit(solution)/shard_map/ppermute | solution.py:328
  14.0 9.1 %collective-permute-start.1 = (bf16[32,4096]{1,0:T(8,128)(2,1)S(1)}, bf16[32,4096]{1,0:T(8,128)(2,1)S(1)}, u32[]{:S(2)}, u32[]{:S(2)}) collective-permute-start(bf16[32,4096]{1,0:T(8,128)(2,1)S(1)} %pad_maximum_fusion.5), channel_id=1, source_target_pairs={{0,96},{32,64},{64,32},{96,0},{1,97},{33,65},{65,33},{97,1},{2,98}... | collective-permute-start | bytes 786440 | tf_op jit(solution)/shard_map/ppermute | solution.py:331
  120.4 54.6 %collective-permute-start.6 = (bf16[3,2,192,1024]{3,2,1,0:T(8,128)(2,1)}, bf16[3,2,192,1024]{3,2,1,0:T(8,128)(2,1)S(1)}, u32[]{:S(2)}, u32[]{:S(2)}) collective-permute-start(bf16[3,2,192,1024]{3,2,1,0:T(8,128)(2,1)} %get-tuple-element.50), channel_id=1, source_target_pairs={{0,32},{32,0},{64,96},{96,64},{1,33},{33,1},{65,97},{97,65},{2,34}... | collective-permute-start | bytes 7077896 | tf_op jit(solution)/shard_map/ppermute | solution.py:343
  121.9 54.7 %collective-permute-start.7 = (bf16[3,2,192,1024]{3,2,1,0:T(8,128)(2,1)}, bf16[3,2,192,1024]{3,2,1,0:T(8,128)(2,1)}, u32[]{:S(2)}, u32[]{:S(2)}) collective-permute-start(bf16[3,2,192,1024]{3,2,1,0:T(8,128)(2,1)} %get-tuple-element.51), channel_id=1, source_target_pairs={{0,96},{32,64},{64,32},{96,0},{1,97},{33,65},{65,33},{97,1},{2,98}... | collective-permute-start | bytes 7077896 | tf_op jit(solution)/shard_map/ppermute | solution.py:344
  144.3 2.9 %collective-permute-start.2 = (bf16[16,32,1024]{2,1,0:T(8,128)(2,1)}, bf16[16,32,1024]{2,1,0:T(8,128)(2,1)S(1)}, u32[]{:S(2)}, u32[]{:S(2)}) collective-permute-start(bf16[16,32,1024]{2,1,0:T(8,128)(2,1)} %get-tuple-element.43), channel_id=1, source_target_pairs={{0,1},{1,0},{2,3},{3,2},{4,5},{5,4},{6,7},{7,6},{8,9},{9,8},{10,11... | collective-permute-start | bytes 3145736 | tf_op jit(solution)/shard_map/ppermute | solution.py:351
  144.3 23.0 %collective-permute-start.3 = (bf16[16,32,1024]{2,1,0:T(8,128)(2,1)}, bf16[16,32,1024]{2,1,0:T(8,128)(2,1)S(1)}, u32[]{:S(2)}, u32[]{:S(2)}) collective-permute-start(bf16[16,32,1024]{2,1,0:T(8,128)(2,1)} %get-tuple-element.44), channel_id=1, source_target_pairs={{0,1},{1,0},{2,3},{3,2},{4,5},{5,4},{6,7},{7,6},{8,9},{9,8},{10,11... | collective-permute-start | bytes 3145736 | tf_op jit(solution)/shard_map/ppermute | solution.py:351
  144.8 22.6 %collective-permute-start.4 = (bf16[16,32,1024]{2,1,0:T(8,128)(2,1)}, bf16[16,32,1024]{2,1,0:T(8,128)(2,1)S(1)}, u32[]{:S(2)}, u32[]{:S(2)}) collective-permute-start(bf16[16,32,1024]{2,1,0:T(8,128)(2,1)} %get-tuple-element.45), channel_id=1, source_target_pairs={{0,1},{1,0},{2,3},{3,2},{4,5},{5,4},{6,7},{7,6},{8,9},{9,8},{10,11... | collective-permute-start | bytes 3145736 | tf_op jit(solution)/shard_map/ppermute | solution.py:351
  147.2 20.2 %copy-start.3 = (bf16[16,32,1024]{2,1,0:T(8,128)(2,1)}, bf16[16,32,1024]{2,1,0:T(8,128)(2,1)S(1)}, u32[]{:S(2)}) copy-start(bf16[16,32,1024]{2,1,0:T(8,128)(2,1)S(1)} %collective-permute-done.2.refs_0_) | copy-start | bytes 3145732
  147.2 20.2 %collective-permute-start.5 = (bf16[16,32,1024]{2,1,0:T(8,128)(2,1)}, bf16[16,32,1024]{2,1,0:T(8,128)(2,1)S(1)}, u32[]{:S(2)}, u32[]{:S(2)}) collective-permute-start(bf16[16,32,1024]{2,1,0:T(8,128)(2,1)} %get-tuple-element.46), channel_id=1, source_target_pairs={{0,1},{1,0},{2,3},{3,2},{4,5},{5,4},{6,7},{7,6},{8,9},{9,8},{10,11... | collective-permute-start | bytes 3145736 | tf_op jit(solution)/shard_map/ppermute | solution.py:351
  167.3 1.0 copy-start.4
  167.4 1.3 copy-start.5
  167.4 1.7 copy-start.6
  175.0 1.6 copy-start.2
  176.6 66.5 %all-to-all-start = ((bf16[16,32,4096]{2,1,0:T(8,128)(2,1)}), bf16[16,32,4096]{2,1,0:T(8,128)(2,1)}, u32[]{:S(2)}, u32[]{:S(2)}) async-start(bf16[16,32,4096]{2,1,0:T(8,128)(2,1)} %pair_sum.1), calls=%async_computation | async-start | bytes 8388608 | tf_op jit(solution)/shard_map/all_to_all | solution.py:356
  189.6 36.0 %collective-permute-start.12 = (bf16[192,2048]{1,0:T(8,128)(2,1)}, bf16[192,2048]{1,0:T(8,128)(2,1)S(1)}, u32[]{:S(2)}, u32[]{:S(2)}) collective-permute-start(bf16[192,2048]{1,0:T(8,128)(2,1)} %get-tuple-element.66), channel_id=1, source_target_pairs={{0,96},{32,64},{64,32},{96,0},{1,97},{33,65},{65,33},{97,1},{2,98}... | collective-permute-start | bytes 2359304 | tf_op jit(solution)/shard_map/ppermute | solution.py:365
  196.5 30.1 %collective-permute-start.13 = (bf16[192,2048]{1,0:T(8,128)(2,1)}, bf16[192,2048]{1,0:T(8,128)(2,1)S(1)}, u32[]{:S(2)}, u32[]{:S(2)}) collective-permute-start(bf16[192,2048]{1,0:T(8,128)(2,1)} %get-tuple-element.68), channel_id=1, source_target_pairs={{0,32},{32,0},{64,96},{96,64},{1,33},{33,1},{65,97},{97,65},{2,34}... | collective-permute-start | bytes 2359304 | tf_op jit(solution)/shard_map/ppermute | solution.py:365
  203.0 24.0 %collective-permute-start.10 = (bf16[192,2048]{1,0:T(8,128)(2,1)}, bf16[192,2048]{1,0:T(8,128)(2,1)S(1)}, u32[]{:S(2)}, u32[]{:S(2)}) collective-permute-start(bf16[192,2048]{1,0:T(8,128)(2,1)} %get-tuple-element.61), channel_id=1, source_target_pairs={{0,96},{32,64},{64,32},{96,0},{1,97},{33,65},{65,33},{97,1},{2,98}... | collective-permute-start | bytes 2359304 | tf_op jit(solution)/shard_map/ppermute | solution.py:365
  211.6 22.4 %collective-permute-start.11 = (bf16[192,2048]{1,0:T(8,128)(2,1)}, bf16[192,2048]{1,0:T(8,128)(2,1)S(1)}, u32[]{:S(2)}, u32[]{:S(2)}) collective-permute-start(bf16[192,2048]{1,0:T(8,128)(2,1)} %get-tuple-element.63), channel_id=1, source_target_pairs={{0,32},{32,0},{64,96},{96,64},{1,33},{33,1},{65,97},{97,65},{2,34}... | collective-permute-start | bytes 2359304 | tf_op jit(solution)/shard_map/ppermute | solution.py:365
  218.1 8.2 %copy-start.12 = (bf16[192,2048]{1,0:T(8,128)(2,1)S(1)}, bf16[192,2048]{1,0:T(8,128)(2,1)}, u32[]{:S(2)}) copy-start(bf16[192,2048]{1,0:T(8,128)(2,1)} %get-tuple-element.65) | copy-start | bytes 2359300
  218.1 30.9 %collective-permute-start.9 = (bf16[192,2048]{1,0:T(8,128)(2,1)}, bf16[192,2048]{1,0:T(8,128)(2,1)S(1)}, u32[]{:S(2)}, u32[]{:S(2)}) collective-permute-start(bf16[192,2048]{1,0:T(8,128)(2,1)} %get-tuple-element.58), channel_id=1, source_target_pairs={{0,32},{32,0},{64,96},{96,64},{1,33},{33,1},{65,97},{97,65},{2,34}... | collective-permute-start | bytes 2359304 | tf_op jit(solution)/shard_map/ppermute | solution.py:365
  225.6 1.1 copy-start.10
  225.6 23.5 %collective-permute-start.8 = (bf16[192,2048]{1,0:T(8,128)(2,1)}, bf16[192,2048]{1,0:T(8,128)(2,1)S(1)}, u32[]{:S(2)}, u32[]{:S(2)}) collective-permute-start(bf16[192,2048]{1,0:T(8,128)(2,1)} %get-tuple-element.56), channel_id=1, source_target_pairs={{0,96},{32,64},{64,32},{96,0},{1,97},{33,65},{65,33},{97,1},{2,98}... | collective-permute-start | bytes 2359304 | tf_op jit(solution)/shard_map/ppermute | solution.py:365
  226.6 1.2 copy-start.11
  227.0 7.0 %copy-start.9 = (bf16[192,2048]{1,0:T(8,128)(2,1)S(1)}, bf16[192,2048]{1,0:T(8,128)(2,1)}, u32[]{:S(2)}) copy-start(bf16[192,2048]{1,0:T(8,128)(2,1)} %get-tuple-element.62) | copy-start | bytes 2359300
  236.8 16.0 %copy-start.8 = (bf16[192,2048]{1,0:T(8,128)(2,1)S(1)}, bf16[192,2048]{1,0:T(8,128)(2,1)}, u32[]{:S(2)}) copy-start(bf16[192,2048]{1,0:T(8,128)(2,1)} %get-tuple-element.71) | copy-start | bytes 2359300
  252.8 1.1 copy-start.7
  253.9 1.5 copy-start.1
Sparse Core Ops, SparseCore 0:
  11.2 75.5 all-gather.2
  89.1 72.0 all-gather.4

commit v4 on v3

--- a/solution.py
+++ b/solution.py
@@ -233,9 +233,11 @@
             left[2 * share * which + share : 2 * share * (which + 1)] = second_ref[which, 0]
 
     both = jnp.dot(left[: 4 * share], tokens_ref[...], preferred_element_type=F32)
-    gate_ref[0] = both[: 2 * share]
-    up_ref[0] = both[2 * share :]
-    down_ref[0] = jnp.dot(left[4 * share :], grads_ref[...], preferred_element_type=F32)
+    gate_ref[0] = both[: 2 * share].astype(BF16)
+    up_ref[0] = both[2 * share :].astype(BF16)
+    down_ref[0] = jnp.dot(
+        left[4 * share :], grads_ref[...], preferred_element_type=F32
+    ).astype(BF16)
 
 
 def own_grads(picks, hidden, gathered, width):
@@ -243,7 +245,7 @@
     step = 512
     count = width // 2 // step
     out = pl.BlockSpec((1, 2 * share, step), lambda h, i, p: (h, 0, i))
-    shape = jax.ShapeDtypeStruct((2, 2 * share, width // 2), F32)
+    shape = jax.ShapeDtypeStruct((2, 2 * share, width // 2), BF16)
     return pl.pallas_call(
         own_kernel,
         grid_spec=pltpu.PrefetchScalarGridSpec(
@@ -268,7 +270,7 @@
 def weight_kernel(other_ref, near_ref, own_ref, out_first, out_second):
     share = out_first.shape[0]
     left = other_ref[0].reshape(2 * share, other_ref.shape[3])
-    total = own_ref[0] + jnp.dot(left, near_ref[...], preferred_element_type=F32)
+    total = own_ref[0].astype(F32) + jnp.dot(left, near_ref[...], preferred_element_type=F32)
     out_first[...] = total[:share].astype(BF16)
     out_second[...] = total[share:].astype(BF16)
 

time: 263 us -> 261 us (level)
  Pallas kernels: 115 us -> 111 us
  waiting for transfers between devices: 92 us -> 95.5 us
    ppermute x3, waiting for transfers between devices: 12 us -> 14.7 us  [per_device(): lax.ppermute(high, 'dp', to_side)]
  transfers between devices with their start and end apart: 17 -> 17, of which waited for: 8 -> 10; matrix products, arithmetic and copies ran while one was open for 3% -> 3% of each run, Pallas kernels for 44% -> 42%
where the time goes in v4:
time: 261 us; the launch traced here: 260 us
  Pallas kernels  111 us (43%)
  waiting for transfers between devices  95.5 us (37%)
  starting transfers between devices  21.4 us (8%)
  between operations  14.3 us (5%)
  other arithmetic  10.8 us (4%)
  local copies, waits for them, and re-layouts  7.89 us (3%)
    all_gather x1, waiting for transfers between devices, per_device(): gathered = lax.all_gather(payload, PLANE, axis=0, tiled=True)  63 us
    pallas_call x6, Pallas kernels, weight_grads(): pl.pallas_call(weight_kernel, grid=(count,), in_specs=[pl.BlockSpec((1, 2...  33.7 us
    pallas_call x1, Pallas kernels, hidden_rows(): pl.pallas_call(functools.partial(hidden_kernel, start), grid_spec=pltpu.P...  32.9 us
    pallas_call x1, Pallas kernels, input_rows(): pl.pallas_call(input_kernel, grid_spec=pltpu.PrefetchScalarGridSpec(num_s...  20.3 us
    pallas_call x1, Pallas kernels, own_grads(): pl.pallas_call(own_kernel, grid_spec=pltpu.PrefetchScalarGridSpec(num_sca...  17.7 us
    ppermute x3, waiting for transfers between devices, per_device(): lax.ppermute(high, 'dp', to_side)  14.7 us
    pallas_call x1, Pallas kernels, pair_sum(): pl.pallas_call(pair_kernel, grid=(count,), in_specs=[whole] + [part] * le...  5.93 us
    all_to_all x1, starting transfers between devices, per_device(): lax.all_to_all(paired, PLANE[:3], split_axis=0, concat_axis=0, tiled=True)  5.54 us
  transfers between devices with their start and end apart: 17, of which 10 were waited for; matrix products, arithmetic and copies ran while one was open for 3% of the time, Pallas kernels for 42%

profile of v4, /device:TPU:2, one launch (start us, length us, event | category | flops | bytes accessed | tf_op | source)
XLA Modules:
  0.0 260.4 jit_solution(14691570740143483085)
XLA Ops:
  12.3 1.7 collective-permute-start
  14.0 2.3 collective-permute-start.1
  16.2 4.2 %collective-permute-done = bf16[32,4096]{1,0:T(8,128)(2,1)S(1)} collective-permute-done((bf16[32,4096]{1,0:T(8,128)(2,1)S(1)}, bf16[32,4096]{1,0:T(8,128)(2,1)S(1)}, u32[]{:S(2)}, u32[]{:S(2)}) %collective-permute-start) | collective-permute-done | bytes 262176 | tf_op jit(solution)/shard_map/ppermute | solution.py:330
  20.4 2.6 %collective-permute-done.1 = bf16[32,4096]{1,0:T(8,128)(2,1)S(1)} collective-permute-done((bf16[32,4096]{1,0:T(8,128)(2,1)S(1)}, bf16[32,4096]{1,0:T(8,128)(2,1)S(1)}, u32[]{:S(2)}, u32[]{:S(2)}) %collective-permute-start.1) | collective-permute-done | bytes 262176 | tf_op jit(solution)/shard_map/ppermute | solution.py:333
  23.8 63.0 %all-gather.3.cloned.1.call-done.gathered_ref.tokens_ref.grads_ref = bf16[1024,8320]{1,0:T(8,128)(2,1)} async-done(((bf16[32,8320]{1,0:T(8,128)(2,1)}), bf16[1024,8320]{1,0:T(8,128)(2,1)}) %all-gather.3.cloned.1.call-update) | async-done | bytes 17039376 | tf_op jit(solution)/shard_map/all_gather | solution.py:329
  87.4 32.9 %hidden_rows.1 = (bf16[3,4,192,1024]{3,2,1,0:T(8,128)(2,1)}, bf16[3,2,192,1024]{3,2,1,0:T(8,128)(2,1)}, bf16[3,2,192,1024]{3,2,1,0:T(8,128)(2,1)}) custom-call(s32[5]{0:T(128)} %stack.30.route_ref, bf16[1024,8320]{1,0:T(8,128)(2,1)} %all-gather.3.cloned.1.call-done.gathered_ref.tokens_ref.grads_ref, bf16[4,192,4096]{2,1,0:T(8,128)(2,1)} %bitcast.25, ...), custom_call_target="tpu_custom_call" | custom-call | tf_op jit(solution)/shard_map/hidden_rows/pallas_call | solution.py:114
  120.4 1.7 collective-permute-start.6
  122.0 2.1 collective-permute-start.7
  124.1 20.3 %input_rows.1 = (bf16[16,32,4096]{2,1,0:T(8,128)(2,1)}, bf16[16,32,1024]{2,1,0:T(8,128)(2,1)}, bf16[16,32,1024]{2,1,0:T(8,128)(2,1)}, bf16[16,32,1024]{2,1,0:T(8,128)(2,1)}, bf16[16,32,1024]{2,1,0:T(8,128)(2,1)}) custom-call(s32[1]{0:T(128)} %bitcast.core_ref, bf16[3,768,1024]{2,1,0:T(8,128)(2,1)} %bitcast.24, bf16[768,4096]{1,0:T(8,128)(2,1)} %bitcast.26, ...), custom_call_target="tpu_custom_call" | custom-call | tf_op jit(solution)/shard_map/input_rows/pallas_call | solution.py:183
  144.9 2.3 collective-permute-done.2.refs_0_
  148.1 17.7 %own_grads.1 = (bf16[2,384,2048]{2,1,0:T(8,128)(2,1)}, bf16[2,384,2048]{2,1,0:T(8,128)(2,1)}, bf16[2,384,2048]{2,1,0:T(8,128)(2,1)}) custom-call(s32[4]{0:T(128)} %pad_add_fusion.pick_ref, bf16[3,4,192,1024]{3,2,1,0:T(8,128)(2,1)} %get-tuple-element.41.first_ref.second_ref, bf16[3,4,192,1024]{3,2,1,0:T(8,128)(2,1)} %get-tuple-element.41.first_ref.second_ref, ...), custom_call_target="tpu_custom_call" | custom-call | tf_op jit(solution)/shard_map/own_grads/pallas_call | solution.py:249
  167.5 5.9 %pair_sum.1 = bf16[16,32,4096]{2,1,0:T(8,128)(2,1)} custom-call(bf16[16,32,4096]{2,1,0:T(8,128)(2,1)} %get-tuple-element.42.kept_ref, bf16[16,32,1024]{2,1,0:T(8,128)(2,1)} %copy-done.3, bf16[16,32,1024]{2,1,0:T(8,128)(2,1)} %copy-done.4, bf16[16,32,1024]{2,1,0:T(8,128)(2,1)} %copy-done.5, bf16[16,32,1024]{2,1,0:T(8,128)(2,1)} %copy-done.6), custom_call_target="tpu_custom_call" | custom-call | tf_op jit(solution)/shard_map/pair_sum/pallas_call | solution.py:212
  174.1 2.6 collective-permute-done.7.other_ref
  176.7 5.5 %all-to-all-start = ((bf16[16,32,4096]{2,1,0:T(8,128)(2,1)}), bf16[16,32,4096]{2,1,0:T(8,128)(2,1)}, u32[]{:S(2)}, u32[]{:S(2)}) async-start(bf16[16,32,4096]{2,1,0:T(8,128)(2,1)} %pair_sum.1), calls=%async_computation | async-start | bytes 8388608 | tf_op jit(solution)/shard_map/all_to_all | solution.py:358
  182.2 5.7 %weight_grads.10 = (bf16[192,2048]{1,0:T(8,128)(2,1)}, bf16[192,2048]{1,0:T(8,128)(2,1)}) custom-call(bf16[3,2,192,1024]{3,2,1,0:T(8,128)(2,1)} %copy-done.2, bf16[1024,8192]{1,0:T(8,128)(2,1)} %all-gather.5.cloned.1.call-done.near_ref, bf16[2,384,2048]{2,1,0:T(8,128)(2,1)} %get-tuple-element.64.own_ref), custom_call_target="tpu_custom_call" | custom-call | tf_op jit(solution)/shard_map/weight_grads/pallas_call | solution.py:286
  187.9 2.1 collective-permute-start.12
  190.0 5.6 %weight_grads.11 = (bf16[192,2048]{1,0:T(8,128)(2,1)}, bf16[192,2048]{1,0:T(8,128)(2,1)}) custom-call(bf16[3,2,192,1024]{3,2,1,0:T(8,128)(2,1)} %collective-permute-done.7.other_ref, bf16[1024,8192]{1,0:T(8,128)(2,1)} %all-gather.5.cloned.1.call-done.near_ref, bf16[2,384,2048]{2,1,0:T(8,128)(2,1)} %get-tuple-element.64.own_ref), custom_call_target="tpu_custom_call" | custom-call | tf_op jit(solution)/shard_map/weight_grads/pallas_call | solution.py:286
  195.5 5.7 %weight_grads.8 = (bf16[192,2048]{1,0:T(8,128)(2,1)}, bf16[192,2048]{1,0:T(8,128)(2,1)}) custom-call(bf16[3,2,192,1024]{3,2,1,0:T(8,128)(2,1)} %copy-done.2, bf16[1024,8192]{1,0:T(8,128)(2,1)} %all-gather.5.cloned.1.call-done.near_ref, bf16[2,384,2048]{2,1,0:T(8,128)(2,1)} %get-tuple-element.59.own_ref), custom_call_target="tpu_custom_call" | custom-call | tf_op jit(solution)/shard_map/weight_grads/pallas_call | solution.py:286
  201.2 1.2 collective-permute-start.10
  202.4 5.6 %weight_grads.9 = (bf16[192,2048]{1,0:T(8,128)(2,1)}, bf16[192,2048]{1,0:T(8,128)(2,1)}) custom-call(bf16[3,2,192,1024]{3,2,1,0:T(8,128)(2,1)} %collective-permute-done.7.other_ref, bf16[1024,8192]{1,0:T(8,128)(2,1)} %all-gather.5.cloned.1.call-done.near_ref, bf16[2,384,2048]{2,1,0:T(8,128)(2,1)} %get-tuple-element.59.own_ref), custom_call_target="tpu_custom_call" | custom-call | tf_op jit(solution)/shard_map/weight_grads/pallas_call | solution.py:286
  208.0 1.4 collective-permute-start.11
  209.4 5.6 %weight_grads.7 = (bf16[192,2048]{1,0:T(8,128)(2,1)}, bf16[192,2048]{1,0:T(8,128)(2,1)}) custom-call(bf16[3,2,192,1024]{3,2,1,0:T(8,128)(2,1)} %collective-permute-done.7.other_ref, bf16[1024,8192]{1,0:T(8,128)(2,1)} %all-gather.5.cloned.1.call-done.near_ref, bf16[2,384,2048]{2,1,0:T(8,128)(2,1)} %get-tuple-element.55.own_ref), custom_call_target="tpu_custom_call" | custom-call | tf_op jit(solution)/shard_map/weight_grads/pallas_call | solution.py:286
  215.6 5.6 %weight_grads.6 = (bf16[192,2048]{1,0:T(8,128)(2,1)}, bf16[192,2048]{1,0:T(8,128)(2,1)}) custom-call(bf16[3,2,192,1024]{3,2,1,0:T(8,128)(2,1)} %copy-done.2, bf16[1024,8192]{1,0:T(8,128)(2,1)} %all-gather.5.cloned.1.call-done.near_ref, bf16[2,384,2048]{2,1,0:T(8,128)(2,1)} %get-tuple-element.55.own_ref), custom_call_target="tpu_custom_call" | custom-call | tf_op jit(solution)/shard_map/weight_grads/pallas_call | solution.py:286
  221.2 2.1 collective-permute-start.8
  224.0 1.2 collective-permute-done.10
  225.4 7.6 %collective-permute-done.11 = bf16[192,2048]{1,0:T(8,128)(2,1)S(1)} collective-permute-done((bf16[192,2048]{1,0:T(8,128)(2,1)}, bf16[192,2048]{1,0:T(8,128)(2,1)S(1)}, u32[]{:S(2)}, u32[]{:S(2)}) %collective-permute-start.11) | collective-permute-done | bytes 786464 | tf_op jit(solution)/shard_map/ppermute | solution.py:367
  233.3 1.3 pad_maximum_fusion.1
  234.6 1.3 pad_maximum_fusion
  235.8 4.3 %all-to-all-done = bf16[16,32,4096]{2,1,0:T(8,128)(2,1)} async-done(((bf16[16,32,4096]{2,1,0:T(8,128)(2,1)}), bf16[16,32,4096]{2,1,0:T(8,128)(2,1)}, u32[]{:S(2)}, u32[]{:S(2)}) %all-to-all-start) | async-done | bytes 4194336 | tf_op jit(solution)/shard_map/all_to_all | solution.py:358
  240.1 7.1 %collective-permute-done.9 = bf16[192,2048]{1,0:T(8,128)(2,1)S(1)} collective-permute-done((bf16[192,2048]{1,0:T(8,128)(2,1)}, bf16[192,2048]{1,0:T(8,128)(2,1)S(1)}, u32[]{:S(2)}, u32[]{:S(2)}) %collective-permute-start.9) | collective-permute-done | bytes 786464 | tf_op jit(solution)/shard_map/ppermute | solution.py:367
  247.2 3.7 %reduce_sum.22 = bf16[32,4096]{1,0:T(8,128)(2,1)} reduce(bf16[16,32,4096]{2,1,0:T(8,128)(2,1)} %all-to-all-done, bf16[]{:T(256)} %constant.38.clone.1), dimensions={0}, to_apply=%region_1.2 | reduce | flops 1966080 | bytes 4456450 | tf_op jit(solution)/shard_map/reduce_sum | solution.py:376
  252.3 1.3 pad_maximum_fusion.2
  (65 shorter events, 13.4 us)
Async XLA Ops:
  7.2 0.7 copy-start
  7.2 79.6 %all-gather.3.cloned.1.call-start = ((), (), s32[]{:S(2)}) async-start(), calls=%async_computation.1 | async-start | bytes 17571840 | tf_op jit(solution)/shard_map/all_gather | solution.py:329
  11.1 171.2 %all-gather.5.cloned.1.call-start = ((), (), s32[]{:S(2)}) async-start(), calls=%async_computation.2 | async-start | bytes 17301504 | tf_op jit(solution)/shard_map/all_gather | solution.py:338
  12.3 8.1 %collective-permute-start = (bf16[32,4096]{1,0:T(8,128)(2,1)S(1)}, bf16[32,4096]{1,0:T(8,128)(2,1)S(1)}, u32[]{:S(2)}, u32[]{:S(2)}) collective-permute-start(bf16[32,4096]{1,0:T(8,128)(2,1)S(1)} %pad_maximum_fusion.4), channel_id=1, source_target_pairs={{0,32},{32,0},{64,96},{96,64},{1,33},{33,1},{65,97},{97,65},{2,34}... | collective-permute-start | bytes 786440 | tf_op jit(solution)/shard_map/ppermute | solution.py:330
  14.0 9.1 %collective-permute-start.1 = (bf16[32,4096]{1,0:T(8,128)(2,1)S(1)}, bf16[32,4096]{1,0:T(8,128)(2,1)S(1)}, u32[]{:S(2)}, u32[]{:S(2)}) collective-permute-start(bf16[32,4096]{1,0:T(8,128)(2,1)S(1)} %pad_maximum_fusion.5), channel_id=1, source_target_pairs={{0,96},{32,64},{64,32},{96,0},{1,97},{33,65},{65,33},{97,1},{2,98}... | collective-permute-start | bytes 786440 | tf_op jit(solution)/shard_map/ppermute | solution.py:333
  120.4 53.7 %collective-permute-start.6 = (bf16[3,2,192,1024]{3,2,1,0:T(8,128)(2,1)}, bf16[3,2,192,1024]{3,2,1,0:T(8,128)(2,1)S(1)}, u32[]{:S(2)}, u32[]{:S(2)}) collective-permute-start(bf16[3,2,192,1024]{3,2,1,0:T(8,128)(2,1)} %get-tuple-element.50), channel_id=1, source_target_pairs={{0,32},{32,0},{64,96},{96,64},{1,33},{33,1},{65,97},{97,65},{2,34}... | collective-permute-start | bytes 7077896 | tf_op jit(solution)/shard_map/ppermute | solution.py:345
  122.0 54.7 %collective-permute-start.7 = (bf16[3,2,192,1024]{3,2,1,0:T(8,128)(2,1)}, bf16[3,2,192,1024]{3,2,1,0:T(8,128)(2,1)}, u32[]{:S(2)}, u32[]{:S(2)}) collective-permute-start(bf16[3,2,192,1024]{3,2,1,0:T(8,128)(2,1)} %get-tuple-element.51), channel_id=1, source_target_pairs={{0,96},{32,64},{64,32},{96,0},{1,97},{33,65},{65,33},{97,1},{2,98}... | collective-permute-start | bytes 7077896 | tf_op jit(solution)/shard_map/ppermute | solution.py:346
  144.3 2.9 %collective-permute-start.2 = (bf16[16,32,1024]{2,1,0:T(8,128)(2,1)}, bf16[16,32,1024]{2,1,0:T(8,128)(2,1)S(1)}, u32[]{:S(2)}, u32[]{:S(2)}) collective-permute-start(bf16[16,32,1024]{2,1,0:T(8,128)(2,1)} %get-tuple-element.43), channel_id=1, source_target_pairs={{0,1},{1,0},{2,3},{3,2},{4,5},{5,4},{6,7},{7,6},{8,9},{9,8},{10,11... | collective-permute-start | bytes 3145736 | tf_op jit(solution)/shard_map/ppermute | solution.py:353
  144.4 21.4 %collective-permute-start.3 = (bf16[16,32,1024]{2,1,0:T(8,128)(2,1)}, bf16[16,32,1024]{2,1,0:T(8,128)(2,1)S(1)}, u32[]{:S(2)}, u32[]{:S(2)}) collective-permute-start(bf16[16,32,1024]{2,1,0:T(8,128)(2,1)} %get-tuple-element.44), channel_id=1, source_target_pairs={{0,1},{1,0},{2,3},{3,2},{4,5},{5,4},{6,7},{7,6},{8,9},{9,8},{10,11... | collective-permute-start | bytes 3145736 | tf_op jit(solution)/shard_map/ppermute | solution.py:353
  144.9 21.0 %collective-permute-start.4 = (bf16[16,32,1024]{2,1,0:T(8,128)(2,1)}, bf16[16,32,1024]{2,1,0:T(8,128)(2,1)S(1)}, u32[]{:S(2)}, u32[]{:S(2)}) collective-permute-start(bf16[16,32,1024]{2,1,0:T(8,128)(2,1)} %get-tuple-element.45), channel_id=1, source_target_pairs={{0,1},{1,0},{2,3},{3,2},{4,5},{5,4},{6,7},{7,6},{8,9},{9,8},{10,11... | collective-permute-start | bytes 3145736 | tf_op jit(solution)/shard_map/ppermute | solution.py:353
  147.2 18.6 %copy-start.3 = (bf16[16,32,1024]{2,1,0:T(8,128)(2,1)}, bf16[16,32,1024]{2,1,0:T(8,128)(2,1)S(1)}, u32[]{:S(2)}) copy-start(bf16[16,32,1024]{2,1,0:T(8,128)(2,1)S(1)} %collective-permute-done.2.refs_0_) | copy-start | bytes 3145732
  147.2 18.6 %collective-permute-start.5 = (bf16[16,32,1024]{2,1,0:T(8,128)(2,1)}, bf16[16,32,1024]{2,1,0:T(8,128)(2,1)S(1)}, u32[]{:S(2)}, u32[]{:S(2)}) collective-permute-start(bf16[16,32,1024]{2,1,0:T(8,128)(2,1)} %get-tuple-element.46), channel_id=1, source_target_pairs={{0,1},{1,0},{2,3},{3,2},{4,5},{5,4},{6,7},{7,6},{8,9},{9,8},{10,11... | collective-permute-start | bytes 3145736 | tf_op jit(solution)/shard_map/ppermute | solution.py:353
  165.8 1.0 copy-start.4
  165.8 1.3 copy-start.5
  165.9 1.6 copy-start.6
  174.1 2.6 copy-start.2
  176.7 63.4 %all-to-all-start = ((bf16[16,32,4096]{2,1,0:T(8,128)(2,1)}), bf16[16,32,4096]{2,1,0:T(8,128)(2,1)}, u32[]{:S(2)}, u32[]{:S(2)}) async-start(bf16[16,32,4096]{2,1,0:T(8,128)(2,1)} %pair_sum.1), calls=%async_computation | async-start | bytes 8388608 | tf_op jit(solution)/shard_map/all_to_all | solution.py:358
  187.9 33.3 %collective-permute-start.12 = (bf16[192,2048]{1,0:T(8,128)(2,1)}, bf16[192,2048]{1,0:T(8,128)(2,1)S(1)}, u32[]{:S(2)}, u32[]{:S(2)}) collective-permute-start(bf16[192,2048]{1,0:T(8,128)(2,1)} %get-tuple-element.66), channel_id=1, source_target_pairs={{0,96},{32,64},{64,32},{96,0},{1,97},{33,65},{65,33},{97,1},{2,98}... | collective-permute-start | bytes 2359304 | tf_op jit(solution)/shard_map/ppermute | solution.py:367
  195.5 28.1 %collective-permute-start.13 = (bf16[192,2048]{1,0:T(8,128)(2,1)}, bf16[192,2048]{1,0:T(8,128)(2,1)S(1)}, u32[]{:S(2)}, u32[]{:S(2)}) collective-permute-start(bf16[192,2048]{1,0:T(8,128)(2,1)} %get-tuple-element.68), channel_id=1, source_target_pairs={{0,32},{32,0},{64,96},{96,64},{1,33},{33,1},{65,97},{97,65},{2,34}... | collective-permute-start | bytes 2359304 | tf_op jit(solution)/shard_map/ppermute | solution.py:367
  201.2 24.0 %collective-permute-start.10 = (bf16[192,2048]{1,0:T(8,128)(2,1)}, bf16[192,2048]{1,0:T(8,128)(2,1)S(1)}, u32[]{:S(2)}, u32[]{:S(2)}) collective-permute-start(bf16[192,2048]{1,0:T(8,128)(2,1)} %get-tuple-element.61), channel_id=1, source_target_pairs={{0,96},{32,64},{64,32},{96,0},{1,97},{33,65},{65,33},{97,1},{2,98}... | collective-permute-start | bytes 2359304 | tf_op jit(solution)/shard_map/ppermute | solution.py:367
  208.0 25.1 %collective-permute-start.11 = (bf16[192,2048]{1,0:T(8,128)(2,1)}, bf16[192,2048]{1,0:T(8,128)(2,1)S(1)}, u32[]{:S(2)}, u32[]{:S(2)}) collective-permute-start(bf16[192,2048]{1,0:T(8,128)(2,1)} %get-tuple-element.63), channel_id=1, source_target_pairs={{0,32},{32,0},{64,96},{96,64},{1,33},{33,1},{65,97},{97,65},{2,34}... | collective-permute-start | bytes 2359304 | tf_op jit(solution)/shard_map/ppermute | solution.py:367
  215.0 8.4 %copy-start.12 = (bf16[192,2048]{1,0:T(8,128)(2,1)S(1)}, bf16[192,2048]{1,0:T(8,128)(2,1)}, u32[]{:S(2)}) copy-start(bf16[192,2048]{1,0:T(8,128)(2,1)} %get-tuple-element.65) | copy-start | bytes 2359300
  215.0 32.2 %collective-permute-start.9 = (bf16[192,2048]{1,0:T(8,128)(2,1)}, bf16[192,2048]{1,0:T(8,128)(2,1)S(1)}, u32[]{:S(2)}, u32[]{:S(2)}) collective-permute-start(bf16[192,2048]{1,0:T(8,128)(2,1)} %get-tuple-element.58), channel_id=1, source_target_pairs={{0,32},{32,0},{64,96},{96,64},{1,33},{33,1},{65,97},{97,65},{2,34}... | collective-permute-start | bytes 2359304 | tf_op jit(solution)/shard_map/ppermute | solution.py:367
  221.2 2.5 copy-start.10
  221.2 25.9 %collective-permute-start.8 = (bf16[192,2048]{1,0:T(8,128)(2,1)}, bf16[192,2048]{1,0:T(8,128)(2,1)S(1)}, u32[]{:S(2)}, u32[]{:S(2)}) collective-permute-start(bf16[192,2048]{1,0:T(8,128)(2,1)} %get-tuple-element.56), channel_id=1, source_target_pairs={{0,96},{32,64},{64,32},{96,0},{1,97},{33,65},{65,33},{97,1},{2,98}... | collective-permute-start | bytes 2359304 | tf_op jit(solution)/shard_map/ppermute | solution.py:367
  223.6 1.5 copy-start.11
  224.0 9.1 %copy-start.9 = (bf16[192,2048]{1,0:T(8,128)(2,1)S(1)}, bf16[192,2048]{1,0:T(8,128)(2,1)}, u32[]{:S(2)}) copy-start(bf16[192,2048]{1,0:T(8,128)(2,1)} %get-tuple-element.62) | copy-start | bytes 2359300
  235.8 15.0 %copy-start.8 = (bf16[192,2048]{1,0:T(8,128)(2,1)S(1)}, bf16[192,2048]{1,0:T(8,128)(2,1)}, u32[]{:S(2)}) copy-start(bf16[192,2048]{1,0:T(8,128)(2,1)} %get-tuple-element.71) | copy-start | bytes 2359300
  250.9 1.1 copy-start.7
  252.0 1.5 copy-start.1
Sparse Core Ops, SparseCore 0:
  11.2 75.5 all-gather.2
  89.1 72.0 all-gather.4

commit v5 on v4

--- a/solution.py
+++ b/solution.py
@@ -369,7 +369,7 @@
     results = []
     for (mine_low, mine_high), (low, high) in zip(mine, received):
         if len(results) == 2:
-            returned, low, high, results = lax.optimization_barrier((returned, low, high, results))
+            returned, results = lax.optimization_barrier((returned, results))
         low = mine_low.astype(F32) + low.astype(F32)
         high = mine_high.astype(F32) + high.astype(F32)
         results.append(jnp.concatenate([low, high], axis=1).astype(BF16)[None])

time: 261 us -> 266 us (1.019)
  waiting for transfers between devices: 95.5 us -> 98.4 us
    ppermute x3, waiting for transfers between devices: 1.19 us -> 16.9 us  [per_device(): lax.ppermute(low, 'dp', to_mirror)]
    ppermute x3, waiting for transfers between devices: 14.7 us -> 5.86 us  [per_device(): lax.ppermute(high, 'dp', to_side)]
    all_to_all x1, waiting for transfers between devices: 4.26 us -> 0.01 us  [per_device(): lax.all_to_all(paired, PLANE[:3], split_axis=0, concat_axis=0, tiled=True)]
  transfers between devices with their start and end apart: 17 -> 17, of which waited for: 10 -> 8; matrix products, arithmetic and copies ran while one was open for 3% -> 4% of each run, Pallas kernels for 42% -> 42%
where the time goes in v5:
time: 266 us; the launch traced here: 265 us
  Pallas kernels  111 us (42%)
  waiting for transfers between devices  98.4 us (37%)
  starting transfers between devices  20.8 us (8%)
  between operations  14.3 us (5%)
  other arithmetic  10.9 us (4%)
  local copies, waits for them, and re-layouts  9.69 us (4%)
    all_gather x1, waiting for transfers between devices, per_device(): gathered = lax.all_gather(payload, PLANE, axis=0, tiled=True)  63 us
    pallas_call x6, Pallas kernels, weight_grads(): pl.pallas_call(weight_kernel, grid=(count,), in_specs=[pl.BlockSpec((1, 2...  33.8 us
    pallas_call x1, Pallas kernels, hidden_rows(): pl.pallas_call(functools.partial(hidden_kernel, start), grid_spec=pltpu.P...  33 us
    pallas_call x1, Pallas kernels, input_rows(): pl.pallas_call(input_kernel, grid_spec=pltpu.PrefetchScalarGridSpec(num_s...  20.3 us
    pallas_call x1, Pallas kernels, own_grads(): pl.pallas_call(own_kernel, grid_spec=pltpu.PrefetchScalarGridSpec(num_sca...  17.7 us
    ppermute x3, waiting for transfers between devices, per_device(): lax.ppermute(low, 'dp', to_mirror)  16.9 us
    pallas_call x1, Pallas kernels, pair_sum(): pl.pallas_call(pair_kernel, grid=(count,), in_specs=[whole] + [part] * le...  5.93 us
    ppermute x3, waiting for transfers between devices, per_device(): lax.ppermute(high, 'dp', to_side)  5.86 us
  transfers between devices with their start and end apart: 17, of which 8 were waited for; matrix products, arithmetic and copies ran while one was open for 4% of the time, Pallas kernels for 42%

profile of v5, /device:TPU:2, one launch (start us, length us, event | category | flops | bytes accessed | tf_op | source)
XLA Modules:
  0.0 264.7 jit_solution(17598212211490573212)
XLA Ops:
  11.1 1.1 constant_dynamic-slice_fusion
  12.3 1.7 collective-permute-start
  14.0 2.3 collective-permute-start.1
  16.2 4.2 %collective-permute-done = bf16[32,4096]{1,0:T(8,128)(2,1)S(1)} collective-permute-done((bf16[32,4096]{1,0:T(8,128)(2,1)S(1)}, bf16[32,4096]{1,0:T(8,128)(2,1)S(1)}, u32[]{:S(2)}, u32[]{:S(2)}) %collective-permute-start) | collective-permute-done | bytes 262176 | tf_op jit(solution)/shard_map/ppermute | solution.py:330
  20.4 2.6 collective-permute-done.1
  23.8 63.0 %all-gather.3.cloned.1.call-done.gathered_ref.tokens_ref.grads_ref = bf16[1024,8320]{1,0:T(8,128)(2,1)} async-done(((bf16[32,8320]{1,0:T(8,128)(2,1)}), bf16[1024,8320]{1,0:T(8,128)(2,1)}) %all-gather.3.cloned.1.call-update) | async-done | bytes 17039376 | tf_op jit(solution)/shard_map/all_gather | solution.py:329
  87.4 33.0 %hidden_rows.1 = (bf16[3,4,192,1024]{3,2,1,0:T(8,128)(2,1)}, bf16[3,2,192,1024]{3,2,1,0:T(8,128)(2,1)}, bf16[3,2,192,1024]{3,2,1,0:T(8,128)(2,1)}) custom-call(s32[5]{0:T(128)} %stack.30.route_ref, bf16[1024,8320]{1,0:T(8,128)(2,1)} %all-gather.3.cloned.1.call-done.gathered_ref.tokens_ref.grads_ref, bf16[4,192,4096]{2,1,0:T(8,128)(2,1)} %bitcast.25, ...), custom_call_target="tpu_custom_call" | custom-call | tf_op jit(solution)/shard_map/hidden_rows/pallas_call | solution.py:114
  120.4 1.6 collective-permute-start.6
  122.1 2.1 collective-permute-start.7
  124.1 20.3 %input_rows.1 = (bf16[16,32,4096]{2,1,0:T(8,128)(2,1)}, bf16[16,32,1024]{2,1,0:T(8,128)(2,1)}, bf16[16,32,1024]{2,1,0:T(8,128)(2,1)}, bf16[16,32,1024]{2,1,0:T(8,128)(2,1)}, bf16[16,32,1024]{2,1,0:T(8,128)(2,1)}) custom-call(s32[1]{0:T(128)} %bitcast.core_ref, bf16[3,768,1024]{2,1,0:T(8,128)(2,1)} %bitcast.24, bf16[768,4096]{1,0:T(8,128)(2,1)} %bitcast.26, ...), custom_call_target="tpu_custom_call" | custom-call | tf_op jit(solution)/shard_map/input_rows/pallas_call | solution.py:183
  145.0 2.4 collective-permute-done.2.refs_0_
  148.2 17.7 %own_grads.1 = (bf16[2,384,2048]{2,1,0:T(8,128)(2,1)}, bf16[2,384,2048]{2,1,0:T(8,128)(2,1)}, bf16[2,384,2048]{2,1,0:T(8,128)(2,1)}) custom-call(s32[4]{0:T(128)} %pad_add_fusion.pick_ref, bf16[3,4,192,1024]{3,2,1,0:T(8,128)(2,1)} %get-tuple-element.39.first_ref.second_ref, bf16[3,4,192,1024]{3,2,1,0:T(8,128)(2,1)} %get-tuple-element.39.first_ref.second_ref, ...), custom_call_target="tpu_custom_call" | custom-call | tf_op jit(solution)/shard_map/own_grads/pallas_call | solution.py:249
  167.2 5.9 %pair_sum.1 = bf16[16,32,4096]{2,1,0:T(8,128)(2,1)} custom-call(bf16[16,32,4096]{2,1,0:T(8,128)(2,1)} %get-tuple-element.40.kept_ref, bf16[16,32,1024]{2,1,0:T(8,128)(2,1)} %copy-done.4, bf16[16,32,1024]{2,1,0:T(8,128)(2,1)} %copy-done.5, bf16[16,32,1024]{2,1,0:T(8,128)(2,1)} %copy-done.6, bf16[16,32,1024]{2,1,0:T(8,128)(2,1)} %collective-permute-done.5.refs_3_), custom_call_target="tpu_custom_call" | custom-call | tf_op jit(solution)/shard_map/pair_sum/pallas_call | solution.py:212
  174.1 2.5 collective-permute-done.7.other_ref
  176.6 1.4 copy-done.2
  178.1 5.5 %all-to-all-start = ((bf16[16,32,4096]{2,1,0:T(8,128)(2,1)}), bf16[16,32,4096]{2,1,0:T(8,128)(2,1)}, u32[]{:S(2)}, u32[]{:S(2)}) async-start(bf16[16,32,4096]{2,1,0:T(8,128)(2,1)} %pair_sum.1), calls=%async_computation | async-start | bytes 8388608 | tf_op jit(solution)/shard_map/all_to_all | solution.py:358
  183.6 5.7 %weight_grads.8 = (bf16[192,2048]{1,0:T(8,128)(2,1)}, bf16[192,2048]{1,0:T(8,128)(2,1)}) custom-call(bf16[3,2,192,1024]{3,2,1,0:T(8,128)(2,1)} %copy-done.3, bf16[1024,8192]{1,0:T(8,128)(2,1)} %all-gather.5.cloned.1.call-done.near_ref, bf16[2,384,2048]{2,1,0:T(8,128)(2,1)} %get-tuple-element.59.own_ref), custom_call_target="tpu_custom_call" | custom-call | tf_op jit(solution)/shard_map/weight_grads/pallas_call | solution.py:286
  189.3 2.1 collective-permute-start.10
  191.4 5.6 %weight_grads.9 = (bf16[192,2048]{1,0:T(8,128)(2,1)}, bf16[192,2048]{1,0:T(8,128)(2,1)}) custom-call(bf16[3,2,192,1024]{3,2,1,0:T(8,128)(2,1)} %copy-done.2, bf16[1024,8192]{1,0:T(8,128)(2,1)} %all-gather.5.cloned.1.call-done.near_ref, bf16[2,384,2048]{2,1,0:T(8,128)(2,1)} %get-tuple-element.59.own_ref), custom_call_target="tpu_custom_call" | custom-call | tf_op jit(solution)/shard_map/weight_grads/pallas_call | solution.py:286
  196.9 5.6 %weight_grads.10 = (bf16[192,2048]{1,0:T(8,128)(2,1)}, bf16[192,2048]{1,0:T(8,128)(2,1)}) custom-call(bf16[3,2,192,1024]{3,2,1,0:T(8,128)(2,1)} %copy-done.3, bf16[1024,8192]{1,0:T(8,128)(2,1)} %all-gather.5.cloned.1.call-done.near_ref, bf16[2,384,2048]{2,1,0:T(8,128)(2,1)} %get-tuple-element.66.own_ref), custom_call_target="tpu_custom_call" | custom-call | tf_op jit(solution)/shard_map/weight_grads/pallas_call | solution.py:286
  202.6 1.2 collective-permute-start.12
  203.7 5.6 %weight_grads.11 = (bf16[192,2048]{1,0:T(8,128)(2,1)}, bf16[192,2048]{1,0:T(8,128)(2,1)}) custom-call(bf16[3,2,192,1024]{3,2,1,0:T(8,128)(2,1)} %copy-done.2, bf16[1024,8192]{1,0:T(8,128)(2,1)} %all-gather.5.cloned.1.call-done.near_ref, bf16[2,384,2048]{2,1,0:T(8,128)(2,1)} %get-tuple-element.66.own_ref), custom_call_target="tpu_custom_call" | custom-call | tf_op jit(solution)/shard_map/weight_grads/pallas_call | solution.py:286
  209.4 1.4 collective-permute-start.13
  210.8 5.6 %weight_grads.6 = (bf16[192,2048]{1,0:T(8,128)(2,1)}, bf16[192,2048]{1,0:T(8,128)(2,1)}) custom-call(bf16[3,2,192,1024]{3,2,1,0:T(8,128)(2,1)} %copy-done.3, bf16[1024,8192]{1,0:T(8,128)(2,1)} %all-gather.5.cloned.1.call-done.near_ref, bf16[2,384,2048]{2,1,0:T(8,128)(2,1)} %get-tuple-element.53.own_ref), custom_call_target="tpu_custom_call" | custom-call | tf_op jit(solution)/shard_map/weight_grads/pallas_call | solution.py:286
  216.4 2.1 collective-permute-start.8
  218.5 5.6 %weight_grads.7 = (bf16[192,2048]{1,0:T(8,128)(2,1)}, bf16[192,2048]{1,0:T(8,128)(2,1)}) custom-call(bf16[3,2,192,1024]{3,2,1,0:T(8,128)(2,1)} %copy-done.2, bf16[1024,8192]{1,0:T(8,128)(2,1)} %all-gather.5.cloned.1.call-done.near_ref, bf16[2,384,2048]{2,1,0:T(8,128)(2,1)} %get-tuple-element.53.own_ref), custom_call_target="tpu_custom_call" | custom-call | tf_op jit(solution)/shard_map/weight_grads/pallas_call | solution.py:286
  225.5 16.9 %collective-permute-done.8 = bf16[192,2048]{1,0:T(8,128)(2,1)S(1)} collective-permute-done((bf16[192,2048]{1,0:T(8,128)(2,1)}, bf16[192,2048]{1,0:T(8,128)(2,1)S(1)}, u32[]{:S(2)}, u32[]{:S(2)}) %collective-permute-start.8) | collective-permute-done | bytes 786464 | tf_op jit(solution)/shard_map/ppermute | solution.py:367
  242.7 5.9 %collective-permute-done.9 = bf16[192,2048]{1,0:T(8,128)(2,1)S(1)} collective-permute-done((bf16[192,2048]{1,0:T(8,128)(2,1)}, bf16[192,2048]{1,0:T(8,128)(2,1)S(1)}, u32[]{:S(2)}, u32[]{:S(2)}) %collective-permute-start.9) | collective-permute-done | bytes 786464 | tf_op jit(solution)/shard_map/ppermute | solution.py:367
  248.8 1.3 pad_maximum_fusion.1
  250.1 1.3 pad_maximum_fusion
  251.4 3.8 %reduce_sum.22 = bf16[32,4096]{1,0:T(8,128)(2,1)} reduce(bf16[16,32,4096]{2,1,0:T(8,128)(2,1)} %all-to-all-done, bf16[]{:T(256)} %constant.38.clone.1), dimensions={0}, to_apply=%region_1.2 | reduce | flops 1966080 | bytes 4456450 | tf_op jit(solution)/shard_map/reduce_sum | solution.py:376
  256.6 1.3 pad_maximum_fusion.2
  (65 shorter events, 12.4 us)
Async XLA Ops:
  7.2 0.7 copy-start
  7.2 79.6 %all-gather.3.cloned.1.call-start = ((), (), s32[]{:S(2)}) async-start(), calls=%async_computation.1 | async-start | bytes 17571840 | tf_op jit(solution)/shard_map/all_gather | solution.py:329
  11.1 172.6 %all-gather.5.cloned.1.call-start = ((), (), s32[]{:S(2)}) async-start(), calls=%async_computation.2 | async-start | bytes 17301504 | tf_op jit(solution)/shard_map/all_gather | solution.py:338
  12.3 8.1 %collective-permute-start = (bf16[32,4096]{1,0:T(8,128)(2,1)S(1)}, bf16[32,4096]{1,0:T(8,128)(2,1)S(1)}, u32[]{:S(2)}, u32[]{:S(2)}) collective-permute-start(bf16[32,4096]{1,0:T(8,128)(2,1)S(1)} %pad_maximum_fusion.4), channel_id=1, source_target_pairs={{0,32},{32,0},{64,96},{96,64},{1,33},{33,1},{65,97},{97,65},{2,34}... | collective-permute-start | bytes 786440 | tf_op jit(solution)/shard_map/ppermute | solution.py:330
  14.0 9.1 %collective-permute-start.1 = (bf16[32,4096]{1,0:T(8,128)(2,1)S(1)}, bf16[32,4096]{1,0:T(8,128)(2,1)S(1)}, u32[]{:S(2)}, u32[]{:S(2)}) collective-permute-start(bf16[32,4096]{1,0:T(8,128)(2,1)S(1)} %pad_maximum_fusion.5), channel_id=1, source_target_pairs={{0,96},{32,64},{64,32},{96,0},{1,97},{33,65},{65,33},{97,1},{2,98}... | collective-permute-start | bytes 786440 | tf_op jit(solution)/shard_map/ppermute | solution.py:333
  120.4 53.7 %collective-permute-start.6 = (bf16[3,2,192,1024]{3,2,1,0:T(8,128)(2,1)}, bf16[3,2,192,1024]{3,2,1,0:T(8,128)(2,1)S(1)}, u32[]{:S(2)}, u32[]{:S(2)}) collective-permute-start(bf16[3,2,192,1024]{3,2,1,0:T(8,128)(2,1)} %get-tuple-element.48), channel_id=1, source_target_pairs={{0,32},{32,0},{64,96},{96,64},{1,33},{33,1},{65,97},{97,65},{2,34}... | collective-permute-start | bytes 7077896 | tf_op jit(solution)/shard_map/ppermute | solution.py:345
  122.1 54.6 %collective-permute-start.7 = (bf16[3,2,192,1024]{3,2,1,0:T(8,128)(2,1)}, bf16[3,2,192,1024]{3,2,1,0:T(8,128)(2,1)S(1)}, u32[]{:S(2)}, u32[]{:S(2)}) collective-permute-start(bf16[3,2,192,1024]{3,2,1,0:T(8,128)(2,1)} %get-tuple-element.49), channel_id=1, source_target_pairs={{0,96},{32,64},{64,32},{96,0},{1,97},{33,65},{65,33},{97,1},{2,98}... | collective-permute-start | bytes 7077896 | tf_op jit(solution)/shard_map/ppermute | solution.py:346
  144.4 3.0 %collective-permute-start.2 = (bf16[16,32,1024]{2,1,0:T(8,128)(2,1)}, bf16[16,32,1024]{2,1,0:T(8,128)(2,1)S(1)}, u32[]{:S(2)}, u32[]{:S(2)}) collective-permute-start(bf16[16,32,1024]{2,1,0:T(8,128)(2,1)} %get-tuple-element.41), channel_id=1, source_target_pairs={{0,1},{1,0},{2,3},{3,2},{4,5},{5,4},{6,7},{7,6},{8,9},{9,8},{10,11... | collective-permute-start | bytes 3145736 | tf_op jit(solution)/shard_map/ppermute | solution.py:353
  144.4 21.5 %collective-permute-start.3 = (bf16[16,32,1024]{2,1,0:T(8,128)(2,1)}, bf16[16,32,1024]{2,1,0:T(8,128)(2,1)S(1)}, u32[]{:S(2)}, u32[]{:S(2)}) collective-permute-start(bf16[16,32,1024]{2,1,0:T(8,128)(2,1)} %get-tuple-element.42), channel_id=1, source_target_pairs={{0,1},{1,0},{2,3},{3,2},{4,5},{5,4},{6,7},{7,6},{8,9},{9,8},{10,11... | collective-permute-start | bytes 3145736 | tf_op jit(solution)/shard_map/ppermute | solution.py:353
  144.9 21.0 %collective-permute-start.4 = (bf16[16,32,1024]{2,1,0:T(8,128)(2,1)}, bf16[16,32,1024]{2,1,0:T(8,128)(2,1)S(1)}, u32[]{:S(2)}, u32[]{:S(2)}) collective-permute-start(bf16[16,32,1024]{2,1,0:T(8,128)(2,1)} %get-tuple-element.43), channel_id=1, source_target_pairs={{0,1},{1,0},{2,3},{3,2},{4,5},{5,4},{6,7},{7,6},{8,9},{9,8},{10,11... | collective-permute-start | bytes 3145736 | tf_op jit(solution)/shard_map/ppermute | solution.py:353
  147.4 18.5 %copy-start.4 = (bf16[16,32,1024]{2,1,0:T(8,128)(2,1)}, bf16[16,32,1024]{2,1,0:T(8,128)(2,1)S(1)}, u32[]{:S(2)}) copy-start(bf16[16,32,1024]{2,1,0:T(8,128)(2,1)S(1)} %collective-permute-done.2.refs_0_) | copy-start | bytes 3145732
  147.4 18.6 %collective-permute-start.5 = (bf16[16,32,1024]{2,1,0:T(8,128)(2,1)}, bf16[16,32,1024]{2,1,0:T(8,128)(2,1)}, u32[]{:S(2)}, u32[]{:S(2)}) collective-permute-start(bf16[16,32,1024]{2,1,0:T(8,128)(2,1)} %get-tuple-element.44), channel_id=1, source_target_pairs={{0,1},{1,0},{2,3},{3,2},{4,5},{5,4},{6,7},{7,6},{8,9},{9,8},{10,11... | collective-permute-start | bytes 3145736 | tf_op jit(solution)/shard_map/ppermute | solution.py:353
  165.9 1.0 copy-start.5
  165.9 1.3 copy-start.6
  174.1 2.5 copy-start.3
  176.6 1.4 copy-start.2
  178.1 73.3 %all-to-all-start = ((bf16[16,32,4096]{2,1,0:T(8,128)(2,1)}), bf16[16,32,4096]{2,1,0:T(8,128)(2,1)}, u32[]{:S(2)}, u32[]{:S(2)}) async-start(bf16[16,32,4096]{2,1,0:T(8,128)(2,1)} %pair_sum.1), calls=%async_computation | async-start | bytes 8388608 | tf_op jit(solution)/shard_map/all_to_all | solution.py:358
  189.3 34.8 %collective-permute-start.10 = (bf16[192,2048]{1,0:T(8,128)(2,1)}, bf16[192,2048]{1,0:T(8,128)(2,1)S(1)}, u32[]{:S(2)}, u32[]{:S(2)}) collective-permute-start(bf16[192,2048]{1,0:T(8,128)(2,1)} %get-tuple-element.61), channel_id=1, source_target_pairs={{0,96},{32,64},{64,32},{96,0},{1,97},{33,65},{65,33},{97,1},{2,98}... | collective-permute-start | bytes 2359304 | tf_op jit(solution)/shard_map/ppermute | solution.py:367
  196.9 27.6 %collective-permute-start.11 = (bf16[192,2048]{1,0:T(8,128)(2,1)}, bf16[192,2048]{1,0:T(8,128)(2,1)S(1)}, u32[]{:S(2)}, u32[]{:S(2)}) collective-permute-start(bf16[192,2048]{1,0:T(8,128)(2,1)} %get-tuple-element.63), channel_id=1, source_target_pairs={{0,32},{32,0},{64,96},{96,64},{1,33},{33,1},{65,97},{97,65},{2,34}... | collective-permute-start | bytes 2359304 | tf_op jit(solution)/shard_map/ppermute | solution.py:367
  202.6 52.6 %collective-permute-start.12 = (bf16[192,2048]{1,0:T(8,128)(2,1)}, bf16[192,2048]{1,0:T(8,128)(2,1)S(1)}, u32[]{:S(2)}, u32[]{:S(2)}) collective-permute-start(bf16[192,2048]{1,0:T(8,128)(2,1)} %get-tuple-element.68), channel_id=1, source_target_pairs={{0,96},{32,64},{64,32},{96,0},{1,97},{33,65},{65,33},{97,1},{2,98}... | collective-permute-start | bytes 2359304 | tf_op jit(solution)/shard_map/ppermute | solution.py:367
  209.4 46.1 %collective-permute-start.13 = (bf16[192,2048]{1,0:T(8,128)(2,1)}, bf16[192,2048]{1,0:T(8,128)(2,1)S(1)}, u32[]{:S(2)}, u32[]{:S(2)}) collective-permute-start(bf16[192,2048]{1,0:T(8,128)(2,1)} %get-tuple-element.70), channel_id=1, source_target_pairs={{0,32},{32,0},{64,96},{96,64},{1,33},{33,1},{65,97},{97,65},{2,34}... | collective-permute-start | bytes 2359304 | tf_op jit(solution)/shard_map/ppermute | solution.py:367
  216.4 7.8 %copy-start.10 = (bf16[192,2048]{1,0:T(8,128)(2,1)S(1)}, bf16[192,2048]{1,0:T(8,128)(2,1)}, u32[]{:S(2)}) copy-start(bf16[192,2048]{1,0:T(8,128)(2,1)} %get-tuple-element.60) | copy-start | bytes 2359300
  216.4 26.0 %collective-permute-start.8 = (bf16[192,2048]{1,0:T(8,128)(2,1)}, bf16[192,2048]{1,0:T(8,128)(2,1)S(1)}, u32[]{:S(2)}, u32[]{:S(2)}) collective-permute-start(bf16[192,2048]{1,0:T(8,128)(2,1)} %get-tuple-element.55), channel_id=1, source_target_pairs={{0,96},{32,64},{64,32},{96,0},{1,97},{33,65},{65,33},{97,1},{2,98}... | collective-permute-start | bytes 2359304 | tf_op jit(solution)/shard_map/ppermute | solution.py:367
  224.1 1.1 copy-start.9
  224.1 24.4 %collective-permute-start.9 = (bf16[192,2048]{1,0:T(8,128)(2,1)}, bf16[192,2048]{1,0:T(8,128)(2,1)S(1)}, u32[]{:S(2)}, u32[]{:S(2)}) collective-permute-start(bf16[192,2048]{1,0:T(8,128)(2,1)} %get-tuple-element.58), channel_id=1, source_target_pairs={{0,32},{32,0},{64,96},{96,64},{1,33},{33,1},{65,97},{97,65},{2,34}... | collective-permute-start | bytes 2359304 | tf_op jit(solution)/shard_map/ppermute | solution.py:367
  224.5 17.9 %copy-start.11 = (bf16[192,2048]{1,0:T(8,128)(2,1)S(1)}, bf16[192,2048]{1,0:T(8,128)(2,1)}, u32[]{:S(2)}) copy-start(bf16[192,2048]{1,0:T(8,128)(2,1)} %get-tuple-element.54) | copy-start | bytes 2359300
  225.5 23.0 %copy-start.12 = (bf16[192,2048]{1,0:T(8,128)(2,1)S(1)}, bf16[192,2048]{1,0:T(8,128)(2,1)}, u32[]{:S(2)}) copy-start(bf16[192,2048]{1,0:T(8,128)(2,1)} %get-tuple-element.57) | copy-start | bytes 2359300
  251.4 3.8 %copy-start.8 = (bf16[192,2048]{1,0:T(8,128)(2,1)S(1)}, bf16[192,2048]{1,0:T(8,128)(2,1)}, u32[]{:S(2)}) copy-start(bf16[192,2048]{1,0:T(8,128)(2,1)} %get-tuple-element.67) | copy-start | bytes 2359300
  255.2 1.1 copy-start.7
  256.3 1.5 copy-start.1
Sparse Core Ops, SparseCore 0:
  11.2 75.5 all-gather.2
  89.1 71.9 all-gather.4

commit v6 on v4

--- a/solution.py
+++ b/solution.py
@@ -278,7 +278,7 @@
 def weight_grads(which, half, other, gathered_near, own):
     _, _, share, token_count = other.shape
     columns = gathered_near.shape[1] // 4
-    step = 512
+    step = 1024
     count = columns // step
     near_base = (half * 2 + which // 2) * count
     out = pl.BlockSpec((share, step), lambda i: (0, i))

time: 261 us -> 260 us (level)
  Pallas kernels: 111 us -> 107 us
  waiting for transfers between devices: 95.5 us -> 98.4 us
    ppermute x3, waiting for transfers between devices: 1.19 us -> 6.35 us  [per_device(): lax.ppermute(low, 'dp', to_mirror)]
    pallas_call x6, Pallas kernels: 33.7 us -> 29.9 us  [weight_grads(): pl.pallas_call(weight_kernel, grid=(count,), in_specs=[pl.BlockSpec((1, 2...]
    ppermute x3, waiting for transfers between devices: 14.7 us -> 11.6 us  [per_device(): lax.ppermute(high, 'dp', to_side)]
  transfers between devices with their start and end apart: 17 -> 17, of which waited for: 10 -> 10; matrix products, arithmetic and copies ran while one was open for 3% -> 3% of each run, Pallas kernels for 42% -> 41%
where the time goes in v6:
time: 260 us
  Pallas kernels  107 us (41%)
  waiting for transfers between devices  98.4 us (38%)
  starting transfers between devices  21.4 us (8%)
  between operations  14.3 us (6%)
  other arithmetic  10.8 us (4%)
  local copies, waits for them, and re-layouts  7.89 us (3%)
    all_gather x1, waiting for transfers between devices, per_device(): gathered = lax.all_gather(payload, PLANE, axis=0, tiled=True)  63 us
    pallas_call x1, Pallas kernels, hidden_rows(): pl.pallas_call(functools.partial(hidden_kernel, start), grid_spec=pltpu.P...  32.9 us
    pallas_call x6, Pallas kernels, weight_grads(): pl.pallas_call(weight_kernel, grid=(count,), in_specs=[pl.BlockSpec((1, 2...  29.9 us
    pallas_call x1, Pallas kernels, input_rows(): pl.pallas_call(input_kernel, grid_spec=pltpu.PrefetchScalarGridSpec(num_s...  20.3 us
    pallas_call x1, Pallas kernels, own_grads(): pl.pallas_call(own_kernel, grid_spec=pltpu.PrefetchScalarGridSpec(num_sca...  17.7 us
    ppermute x3, waiting for transfers between devices, per_device(): lax.ppermute(high, 'dp', to_side)  11.6 us
    ppermute x3, waiting for transfers between devices, per_device(): lax.ppermute(low, 'dp', to_mirror)  6.35 us
    pallas_call x1, Pallas kernels, pair_sum(): pl.pallas_call(pair_kernel, grid=(count,), in_specs=[whole] + [part] * le...  5.93 us
  transfers between devices with their start and end apart: 17, of which 10 were waited for; matrix products, arithmetic and copies ran while one was open for 3% of the time, Pallas kernels for 41%

profile of v6, /device:TPU:2, one launch (start us, length us, event | category | flops | bytes accessed | tf_op | source)
XLA Modules:
  0.0 259.5 jit_solution(17423868852592451371)
XLA Ops:
  12.3 1.7 collective-permute-start
  14.0 2.3 collective-permute-start.1
  16.2 4.2 %collective-permute-done = bf16[32,4096]{1,0:T(8,128)(2,1)S(1)} collective-permute-done((bf16[32,4096]{1,0:T(8,128)(2,1)S(1)}, bf16[32,4096]{1,0:T(8,128)(2,1)S(1)}, u32[]{:S(2)}, u32[]{:S(2)}) %collective-permute-start) | collective-permute-done | bytes 262176 | tf_op jit(solution)/shard_map/ppermute | solution.py:330
  20.4 2.6 %collective-permute-done.1 = bf16[32,4096]{1,0:T(8,128)(2,1)S(1)} collective-permute-done((bf16[32,4096]{1,0:T(8,128)(2,1)S(1)}, bf16[32,4096]{1,0:T(8,128)(2,1)S(1)}, u32[]{:S(2)}, u32[]{:S(2)}) %collective-permute-start.1) | collective-permute-done | bytes 262176 | tf_op jit(solution)/shard_map/ppermute | solution.py:333
  23.8 63.0 %all-gather.3.cloned.1.call-done.gathered_ref.tokens_ref.grads_ref = bf16[1024,8320]{1,0:T(8,128)(2,1)} async-done(((bf16[32,8320]{1,0:T(8,128)(2,1)}), bf16[1024,8320]{1,0:T(8,128)(2,1)}) %all-gather.3.cloned.1.call-update) | async-done | bytes 17039376 | tf_op jit(solution)/shard_map/all_gather | solution.py:329
  87.4 32.9 %hidden_rows.1 = (bf16[3,4,192,1024]{3,2,1,0:T(8,128)(2,1)}, bf16[3,2,192,1024]{3,2,1,0:T(8,128)(2,1)}, bf16[3,2,192,1024]{3,2,1,0:T(8,128)(2,1)}) custom-call(s32[5]{0:T(128)} %stack.30.route_ref, bf16[1024,8320]{1,0:T(8,128)(2,1)} %all-gather.3.cloned.1.call-done.gathered_ref.tokens_ref.grads_ref, bf16[4,192,4096]{2,1,0:T(8,128)(2,1)} %bitcast.25, ...), custom_call_target="tpu_custom_call" | custom-call | tf_op jit(solution)/shard_map/hidden_rows/pallas_call | solution.py:114
  120.4 1.7 collective-permute-start.6
  122.0 2.1 collective-permute-start.7
  124.1 20.3 %input_rows.1 = (bf16[16,32,4096]{2,1,0:T(8,128)(2,1)}, bf16[16,32,1024]{2,1,0:T(8,128)(2,1)}, bf16[16,32,1024]{2,1,0:T(8,128)(2,1)}, bf16[16,32,1024]{2,1,0:T(8,128)(2,1)}, bf16[16,32,1024]{2,1,0:T(8,128)(2,1)}) custom-call(s32[1]{0:T(128)} %bitcast.core_ref, bf16[3,768,1024]{2,1,0:T(8,128)(2,1)} %bitcast.24, bf16[768,4096]{1,0:T(8,128)(2,1)} %bitcast.26, ...), custom_call_target="tpu_custom_call" | custom-call | tf_op jit(solution)/shard_map/input_rows/pallas_call | solution.py:183
  144.9 2.3 collective-permute-done.2.refs_0_
  148.1 17.7 %own_grads.1 = (bf16[2,384,2048]{2,1,0:T(8,128)(2,1)}, bf16[2,384,2048]{2,1,0:T(8,128)(2,1)}, bf16[2,384,2048]{2,1,0:T(8,128)(2,1)}) custom-call(s32[4]{0:T(128)} %pad_add_fusion.pick_ref, bf16[3,4,192,1024]{3,2,1,0:T(8,128)(2,1)} %get-tuple-element.41.first_ref.second_ref, bf16[3,4,192,1024]{3,2,1,0:T(8,128)(2,1)} %get-tuple-element.41.first_ref.second_ref, ...), custom_call_target="tpu_custom_call" | custom-call | tf_op jit(solution)/shard_map/own_grads/pallas_call | solution.py:249
  167.5 5.9 %pair_sum.1 = bf16[16,32,4096]{2,1,0:T(8,128)(2,1)} custom-call(bf16[16,32,4096]{2,1,0:T(8,128)(2,1)} %get-tuple-element.42.kept_ref, bf16[16,32,1024]{2,1,0:T(8,128)(2,1)} %copy-done.3, bf16[16,32,1024]{2,1,0:T(8,128)(2,1)} %copy-done.4, bf16[16,32,1024]{2,1,0:T(8,128)(2,1)} %copy-done.5, bf16[16,32,1024]{2,1,0:T(8,128)(2,1)} %copy-done.6), custom_call_target="tpu_custom_call" | custom-call | tf_op jit(solution)/shard_map/pair_sum/pallas_call | solution.py:212
  174.1 2.6 %collective-permute-done.7.other_ref = bf16[3,2,192,1024]{3,2,1,0:T(8,128)(2,1)} collective-permute-done((bf16[3,2,192,1024]{3,2,1,0:T(8,128)(2,1)}, bf16[3,2,192,1024]{3,2,1,0:T(8,128)(2,1)}, u32[]{:S(2)}, u32[]{:S(2)}) %collective-permute-start.7) | collective-permute-done | bytes 2359328 | tf_op jit(solution)/shard_map/ppermute | solution.py:346
  176.7 5.5 %all-to-all-start = ((bf16[16,32,4096]{2,1,0:T(8,128)(2,1)}), bf16[16,32,4096]{2,1,0:T(8,128)(2,1)}, u32[]{:S(2)}, u32[]{:S(2)}) async-start(bf16[16,32,4096]{2,1,0:T(8,128)(2,1)} %pair_sum.1), calls=%async_computation | async-start | bytes 8388608 | tf_op jit(solution)/shard_map/all_to_all | solution.py:358
  182.2 5.5 %weight_grads.10 = (bf16[192,2048]{1,0:T(8,128)(2,1)}, bf16[192,2048]{1,0:T(8,128)(2,1)}) custom-call(bf16[3,2,192,1024]{3,2,1,0:T(8,128)(2,1)} %copy-done.2, bf16[1024,8192]{1,0:T(8,128)(2,1)} %all-gather.5.cloned.1.call-done.near_ref, bf16[2,384,2048]{2,1,0:T(8,128)(2,1)} %get-tuple-element.64.own_ref), custom_call_target="tpu_custom_call" | custom-call | tf_op jit(solution)/shard_map/weight_grads/pallas_call | solution.py:286
  187.8 2.1 collective-permute-start.12
  189.8 4.8 %weight_grads.11 = (bf16[192,2048]{1,0:T(8,128)(2,1)}, bf16[192,2048]{1,0:T(8,128)(2,1)}) custom-call(bf16[3,2,192,1024]{3,2,1,0:T(8,128)(2,1)} %collective-permute-done.7.other_ref, bf16[1024,8192]{1,0:T(8,128)(2,1)} %all-gather.5.cloned.1.call-done.near_ref, bf16[2,384,2048]{2,1,0:T(8,128)(2,1)} %get-tuple-element.64.own_ref), custom_call_target="tpu_custom_call" | custom-call | tf_op jit(solution)/shard_map/weight_grads/pallas_call | solution.py:286
  194.7 4.9 %weight_grads.8 = (bf16[192,2048]{1,0:T(8,128)(2,1)}, bf16[192,2048]{1,0:T(8,128)(2,1)}) custom-call(bf16[3,2,192,1024]{3,2,1,0:T(8,128)(2,1)} %copy-done.2, bf16[1024,8192]{1,0:T(8,128)(2,1)} %all-gather.5.cloned.1.call-done.near_ref, bf16[2,384,2048]{2,1,0:T(8,128)(2,1)} %get-tuple-element.59.own_ref), custom_call_target="tpu_custom_call" | custom-call | tf_op jit(solution)/shard_map/weight_grads/pallas_call | solution.py:286
  199.6 1.2 collective-permute-start.10
  200.8 4.9 %weight_grads.9 = (bf16[192,2048]{1,0:T(8,128)(2,1)}, bf16[192,2048]{1,0:T(8,128)(2,1)}) custom-call(bf16[3,2,192,1024]{3,2,1,0:T(8,128)(2,1)} %collective-permute-done.7.other_ref, bf16[1024,8192]{1,0:T(8,128)(2,1)} %all-gather.5.cloned.1.call-done.near_ref, bf16[2,384,2048]{2,1,0:T(8,128)(2,1)} %get-tuple-element.59.own_ref), custom_call_target="tpu_custom_call" | custom-call | tf_op jit(solution)/shard_map/weight_grads/pallas_call | solution.py:286
  205.6 1.4 collective-permute-start.11
  207.0 4.9 %weight_grads.7 = (bf16[192,2048]{1,0:T(8,128)(2,1)}, bf16[192,2048]{1,0:T(8,128)(2,1)}) custom-call(bf16[3,2,192,1024]{3,2,1,0:T(8,128)(2,1)} %collective-permute-done.7.other_ref, bf16[1024,8192]{1,0:T(8,128)(2,1)} %all-gather.5.cloned.1.call-done.near_ref, bf16[2,384,2048]{2,1,0:T(8,128)(2,1)} %get-tuple-element.55.own_ref), custom_call_target="tpu_custom_call" | custom-call | tf_op jit(solution)/shard_map/weight_grads/pallas_call | solution.py:286
  212.5 4.9 %weight_grads.6 = (bf16[192,2048]{1,0:T(8,128)(2,1)}, bf16[192,2048]{1,0:T(8,128)(2,1)}) custom-call(bf16[3,2,192,1024]{3,2,1,0:T(8,128)(2,1)} %copy-done.2, bf16[1024,8192]{1,0:T(8,128)(2,1)} %all-gather.5.cloned.1.call-done.near_ref, bf16[2,384,2048]{2,1,0:T(8,128)(2,1)} %get-tuple-element.55.own_ref), custom_call_target="tpu_custom_call" | custom-call | tf_op jit(solution)/shard_map/weight_grads/pallas_call | solution.py:286
  217.4 2.1 collective-permute-start.8
  220.2 6.3 %collective-permute-done.10 = bf16[192,2048]{1,0:T(8,128)(2,1)S(1)} collective-permute-done((bf16[192,2048]{1,0:T(8,128)(2,1)}, bf16[192,2048]{1,0:T(8,128)(2,1)S(1)}, u32[]{:S(2)}, u32[]{:S(2)}) %collective-permute-start.10) | collective-permute-done | bytes 786464 | tf_op jit(solution)/shard_map/ppermute | solution.py:367
  226.8 5.4 %collective-permute-done.11 = bf16[192,2048]{1,0:T(8,128)(2,1)S(1)} collective-permute-done((bf16[192,2048]{1,0:T(8,128)(2,1)}, bf16[192,2048]{1,0:T(8,128)(2,1)S(1)}, u32[]{:S(2)}, u32[]{:S(2)}) %collective-permute-start.11) | collective-permute-done | bytes 786464 | tf_op jit(solution)/shard_map/ppermute | solution.py:367
  232.5 1.3 pad_maximum_fusion.1
  233.7 1.3 pad_maximum_fusion
  235.0 5.1 %all-to-all-done = bf16[16,32,4096]{2,1,0:T(8,128)(2,1)} async-done(((bf16[16,32,4096]{2,1,0:T(8,128)(2,1)}), bf16[16,32,4096]{2,1,0:T(8,128)(2,1)}, u32[]{:S(2)}, u32[]{:S(2)}) %all-to-all-start) | async-done | bytes 4194336 | tf_op jit(solution)/shard_map/all_to_all | solution.py:358
  240.1 6.2 %collective-permute-done.9 = bf16[192,2048]{1,0:T(8,128)(2,1)S(1)} collective-permute-done((bf16[192,2048]{1,0:T(8,128)(2,1)}, bf16[192,2048]{1,0:T(8,128)(2,1)S(1)}, u32[]{:S(2)}, u32[]{:S(2)}) %collective-permute-start.9) | collective-permute-done | bytes 786464 | tf_op jit(solution)/shard_map/ppermute | solution.py:367
  246.3 3.7 %reduce_sum.22 = bf16[32,4096]{1,0:T(8,128)(2,1)} reduce(bf16[16,32,4096]{2,1,0:T(8,128)(2,1)} %all-to-all-done, bf16[]{:T(256)} %constant.38.clone.1), dimensions={0}, to_apply=%region_1.2 | reduce | flops 1966080 | bytes 4456450 | tf_op jit(solution)/shard_map/reduce_sum | solution.py:376
  251.4 1.3 pad_maximum_fusion.2
  (65 shorter events, 13.4 us)
Async XLA Ops:
  7.2 0.7 copy-start
  7.2 79.6 %all-gather.3.cloned.1.call-start = ((), (), s32[]{:S(2)}) async-start(), calls=%async_computation.1 | async-start | bytes 17571840 | tf_op jit(solution)/shard_map/all_gather | solution.py:329
  11.1 171.2 %all-gather.5.cloned.1.call-start = ((), (), s32[]{:S(2)}) async-start(), calls=%async_computation.2 | async-start | bytes 17301504 | tf_op jit(solution)/shard_map/all_gather | solution.py:338
  12.3 8.1 %collective-permute-start = (bf16[32,4096]{1,0:T(8,128)(2,1)S(1)}, bf16[32,4096]{1,0:T(8,128)(2,1)S(1)}, u32[]{:S(2)}, u32[]{:S(2)}) collective-permute-start(bf16[32,4096]{1,0:T(8,128)(2,1)S(1)} %pad_maximum_fusion.4), channel_id=1, source_target_pairs={{0,32},{32,0},{64,96},{96,64},{1,33},{33,1},{65,97},{97,65},{2,34}... | collective-permute-start | bytes 786440 | tf_op jit(solution)/shard_map/ppermute | solution.py:330
  14.0 9.1 %collective-permute-start.1 = (bf16[32,4096]{1,0:T(8,128)(2,1)S(1)}, bf16[32,4096]{1,0:T(8,128)(2,1)S(1)}, u32[]{:S(2)}, u32[]{:S(2)}) collective-permute-start(bf16[32,4096]{1,0:T(8,128)(2,1)S(1)} %pad_maximum_fusion.5), channel_id=1, source_target_pairs={{0,96},{32,64},{64,32},{96,0},{1,97},{33,65},{65,33},{97,1},{2,98}... | collective-permute-start | bytes 786440 | tf_op jit(solution)/shard_map/ppermute | solution.py:333
  120.4 53.7 %collective-permute-start.6 = (bf16[3,2,192,1024]{3,2,1,0:T(8,128)(2,1)}, bf16[3,2,192,1024]{3,2,1,0:T(8,128)(2,1)S(1)}, u32[]{:S(2)}, u32[]{:S(2)}) collective-permute-start(bf16[3,2,192,1024]{3,2,1,0:T(8,128)(2,1)} %get-tuple-element.50), channel_id=1, source_target_pairs={{0,32},{32,0},{64,96},{96,64},{1,33},{33,1},{65,97},{97,65},{2,34}... | collective-permute-start | bytes 7077896 | tf_op jit(solution)/shard_map/ppermute | solution.py:345
  122.0 54.7 %collective-permute-start.7 = (bf16[3,2,192,1024]{3,2,1,0:T(8,128)(2,1)}, bf16[3,2,192,1024]{3,2,1,0:T(8,128)(2,1)}, u32[]{:S(2)}, u32[]{:S(2)}) collective-permute-start(bf16[3,2,192,1024]{3,2,1,0:T(8,128)(2,1)} %get-tuple-element.51), channel_id=1, source_target_pairs={{0,96},{32,64},{64,32},{96,0},{1,97},{33,65},{65,33},{97,1},{2,98}... | collective-permute-start | bytes 7077896 | tf_op jit(solution)/shard_map/ppermute | solution.py:346
  144.3 2.9 %collective-permute-start.2 = (bf16[16,32,1024]{2,1,0:T(8,128)(2,1)}, bf16[16,32,1024]{2,1,0:T(8,128)(2,1)S(1)}, u32[]{:S(2)}, u32[]{:S(2)}) collective-permute-start(bf16[16,32,1024]{2,1,0:T(8,128)(2,1)} %get-tuple-element.43), channel_id=1, source_target_pairs={{0,1},{1,0},{2,3},{3,2},{4,5},{5,4},{6,7},{7,6},{8,9},{9,8},{10,11... | collective-permute-start | bytes 3145736 | tf_op jit(solution)/shard_map/ppermute | solution.py:353
  144.4 21.4 %collective-permute-start.3 = (bf16[16,32,1024]{2,1,0:T(8,128)(2,1)}, bf16[16,32,1024]{2,1,0:T(8,128)(2,1)S(1)}, u32[]{:S(2)}, u32[]{:S(2)}) collective-permute-start(bf16[16,32,1024]{2,1,0:T(8,128)(2,1)} %get-tuple-element.44), channel_id=1, source_target_pairs={{0,1},{1,0},{2,3},{3,2},{4,5},{5,4},{6,7},{7,6},{8,9},{9,8},{10,11... | collective-permute-start | bytes 3145736 | tf_op jit(solution)/shard_map/ppermute | solution.py:353
  144.9 21.0 %collective-permute-start.4 = (bf16[16,32,1024]{2,1,0:T(8,128)(2,1)}, bf16[16,32,1024]{2,1,0:T(8,128)(2,1)S(1)}, u32[]{:S(2)}, u32[]{:S(2)}) collective-permute-start(bf16[16,32,1024]{2,1,0:T(8,128)(2,1)} %get-tuple-element.45), channel_id=1, source_target_pairs={{0,1},{1,0},{2,3},{3,2},{4,5},{5,4},{6,7},{7,6},{8,9},{9,8},{10,11... | collective-permute-start | bytes 3145736 | tf_op jit(solution)/shard_map/ppermute | solution.py:353
  147.2 18.6 %copy-start.3 = (bf16[16,32,1024]{2,1,0:T(8,128)(2,1)}, bf16[16,32,1024]{2,1,0:T(8,128)(2,1)S(1)}, u32[]{:S(2)}) copy-start(bf16[16,32,1024]{2,1,0:T(8,128)(2,1)S(1)} %collective-permute-done.2.refs_0_) | copy-start | bytes 3145732
  147.2 18.6 %collective-permute-start.5 = (bf16[16,32,1024]{2,1,0:T(8,128)(2,1)}, bf16[16,32,1024]{2,1,0:T(8,128)(2,1)S(1)}, u32[]{:S(2)}, u32[]{:S(2)}) collective-permute-start(bf16[16,32,1024]{2,1,0:T(8,128)(2,1)} %get-tuple-element.46), channel_id=1, source_target_pairs={{0,1},{1,0},{2,3},{3,2},{4,5},{5,4},{6,7},{7,6},{8,9},{9,8},{10,11... | collective-permute-start | bytes 3145736 | tf_op jit(solution)/shard_map/ppermute | solution.py:353
  165.8 1.0 copy-start.4
  165.8 1.3 copy-start.5
  165.9 1.6 copy-start.6
  174.1 2.6 %copy-start.2 = (bf16[3,2,192,1024]{3,2,1,0:T(8,128)(2,1)}, bf16[3,2,192,1024]{3,2,1,0:T(8,128)(2,1)S(1)}, u32[]{:S(2)}) copy-start(bf16[3,2,192,1024]{3,2,1,0:T(8,128)(2,1)S(1)} %collective-permute-done.6.other_ref) | copy-start | bytes 7077892
  176.7 63.4 %all-to-all-start = ((bf16[16,32,4096]{2,1,0:T(8,128)(2,1)}), bf16[16,32,4096]{2,1,0:T(8,128)(2,1)}, u32[]{:S(2)}, u32[]{:S(2)}) async-start(bf16[16,32,4096]{2,1,0:T(8,128)(2,1)} %pair_sum.1), calls=%async_computation | async-start | bytes 8388608 | tf_op jit(solution)/shard_map/all_to_all | solution.py:358
  187.8 29.7 %collective-permute-start.12 = (bf16[192,2048]{1,0:T(8,128)(2,1)}, bf16[192,2048]{1,0:T(8,128)(2,1)S(1)}, u32[]{:S(2)}, u32[]{:S(2)}) collective-permute-start(bf16[192,2048]{1,0:T(8,128)(2,1)} %get-tuple-element.66), channel_id=1, source_target_pairs={{0,96},{32,64},{64,32},{96,0},{1,97},{33,65},{65,33},{97,1},{2,98}... | collective-permute-start | bytes 2359304 | tf_op jit(solution)/shard_map/ppermute | solution.py:367
  194.7 25.2 %collective-permute-start.13 = (bf16[192,2048]{1,0:T(8,128)(2,1)}, bf16[192,2048]{1,0:T(8,128)(2,1)S(1)}, u32[]{:S(2)}, u32[]{:S(2)}) collective-permute-start(bf16[192,2048]{1,0:T(8,128)(2,1)} %get-tuple-element.68), channel_id=1, source_target_pairs={{0,32},{32,0},{64,96},{96,64},{1,33},{33,1},{65,97},{97,65},{2,34}... | collective-permute-start | bytes 2359304 | tf_op jit(solution)/shard_map/ppermute | solution.py:367
  199.6 26.9 %collective-permute-start.10 = (bf16[192,2048]{1,0:T(8,128)(2,1)}, bf16[192,2048]{1,0:T(8,128)(2,1)S(1)}, u32[]{:S(2)}, u32[]{:S(2)}) collective-permute-start(bf16[192,2048]{1,0:T(8,128)(2,1)} %get-tuple-element.61), channel_id=1, source_target_pairs={{0,96},{32,64},{64,32},{96,0},{1,97},{33,65},{65,33},{97,1},{2,98}... | collective-permute-start | bytes 2359304 | tf_op jit(solution)/shard_map/ppermute | solution.py:367
  205.6 26.6 %collective-permute-start.11 = (bf16[192,2048]{1,0:T(8,128)(2,1)}, bf16[192,2048]{1,0:T(8,128)(2,1)S(1)}, u32[]{:S(2)}, u32[]{:S(2)}) collective-permute-start(bf16[192,2048]{1,0:T(8,128)(2,1)} %get-tuple-element.63), channel_id=1, source_target_pairs={{0,32},{32,0},{64,96},{96,64},{1,33},{33,1},{65,97},{97,65},{2,34}... | collective-permute-start | bytes 2359304 | tf_op jit(solution)/shard_map/ppermute | solution.py:367
  211.9 7.7 %copy-start.12 = (bf16[192,2048]{1,0:T(8,128)(2,1)S(1)}, bf16[192,2048]{1,0:T(8,128)(2,1)}, u32[]{:S(2)}) copy-start(bf16[192,2048]{1,0:T(8,128)(2,1)} %get-tuple-element.65) | copy-start | bytes 2359300
  211.9 34.4 %collective-permute-start.9 = (bf16[192,2048]{1,0:T(8,128)(2,1)}, bf16[192,2048]{1,0:T(8,128)(2,1)S(1)}, u32[]{:S(2)}, u32[]{:S(2)}) collective-permute-start(bf16[192,2048]{1,0:T(8,128)(2,1)} %get-tuple-element.58), channel_id=1, source_target_pairs={{0,32},{32,0},{64,96},{96,64},{1,33},{33,1},{65,97},{97,65},{2,34}... | collective-permute-start | bytes 2359304 | tf_op jit(solution)/shard_map/ppermute | solution.py:367
  217.4 2.5 copy-start.10
  217.4 28.9 %collective-permute-start.8 = (bf16[192,2048]{1,0:T(8,128)(2,1)}, bf16[192,2048]{1,0:T(8,128)(2,1)S(1)}, u32[]{:S(2)}, u32[]{:S(2)}) collective-permute-start(bf16[192,2048]{1,0:T(8,128)(2,1)} %get-tuple-element.56), channel_id=1, source_target_pairs={{0,96},{32,64},{64,32},{96,0},{1,97},{33,65},{65,33},{97,1},{2,98}... | collective-permute-start | bytes 2359304 | tf_op jit(solution)/shard_map/ppermute | solution.py:367
  219.8 6.7 %copy-start.11 = (bf16[192,2048]{1,0:T(8,128)(2,1)S(1)}, bf16[192,2048]{1,0:T(8,128)(2,1)}, u32[]{:S(2)}) copy-start(bf16[192,2048]{1,0:T(8,128)(2,1)} %get-tuple-element.60) | copy-start | bytes 2359300
  220.2 12.1 %copy-start.9 = (bf16[192,2048]{1,0:T(8,128)(2,1)S(1)}, bf16[192,2048]{1,0:T(8,128)(2,1)}, u32[]{:S(2)}) copy-start(bf16[192,2048]{1,0:T(8,128)(2,1)} %get-tuple-element.62) | copy-start | bytes 2359300
  235.0 15.0 %copy-start.8 = (bf16[192,2048]{1,0:T(8,128)(2,1)S(1)}, bf16[192,2048]{1,0:T(8,128)(2,1)}, u32[]{:S(2)}) copy-start(bf16[192,2048]{1,0:T(8,128)(2,1)} %get-tuple-element.71) | copy-start | bytes 2359300
  250.0 1.1 copy-start.7
  251.2 1.5 copy-start.1
Sparse Core Ops, SparseCore 0:
  11.2 75.5 all-gather.2
  89.1 72.0 all-gather.4
